TPU v7x, 32 devices: a whole 2x2x4 slice. The times are simulated.
32 devices in a mesh: depth: 8 (over y, x, core), light: 4 (over z).
Axes of the slice: x: 2, y: 2, z: 4, core: 2. Of those that a mesh axis runs over, the one named last changes fastest.
Arguments:
- density: bfloat16 [512, 32, 1024], P('depth', 'light'), may hold values from 0.049804688 to 1
- light_rate: float32 [1024], replicated, may hold values from 0.001 to 0.3
- view_rate: float32 [2, 1024], replicated, may hold values from 5e-05 to 0.005
- centers: float32 [3], replicated, may hold values from 0.1 to 0.9
- rank: int32 [2, 8], replicated, may hold values from 0 to 7, each once within a row
Outputs:
- image: float32 [2, 4, 32, 1024], P(None, None, 'light', 'depth')
Inputs may be any that keep to these rules, and one draw needn't show every extreme that they name: Each row of rank is a permutation of 0 to 7.
All inputs are finite; a program needn't handle non-finite values.
Results may differ from a plain program's by a relative error of at most 0.0003.
Values sent between devices are 32-bit elements; how exact they have to be, the bound alone decides.
No kernel may reach another device: no remote copies, remote signals or barrier semaphores. Data moves between devices by JAX's collectives and lax.ppermute only.
A program may use at most 64 MiB of HBM per device.

v0:
```python
import jax
import jax.numpy as jnp
from jax import lax
from jax.sharding import PartitionSpec as P

VIEWPOINTS = 2


def lower_sums(pieces):
    below = jnp.cumsum(pieces, axis=0) - pieces
    return lax.all_to_all(below, "light", split_axis=0, concat_axis=2, tiled=True)


def shards(density, light_rate, view_rate, centers, rank):
    rho = density.astype(jnp.float32)
    sample_count = rho.shape[0]
    extinct = rho * light_rate
    inner_depth = jnp.cumsum(extinct, axis=1) - extinct
    totals = jnp.sum(extinct, axis=1)
    incoming = lower_sums(
        lax.all_to_all(totals[None], "light", split_axis=2, concat_axis=0, tiled=True)
    )[0]
    lit_field = jnp.exp(-(incoming[:, None, :] + inner_depth))
    steps = jnp.arange(sample_count, dtype=jnp.int32)
    before = (steps[:, None] > steps[None, :]).astype(jnp.float32)
    shape = rho.shape
    layers = []
    for view in range(VIEWPOINTS):
        depth_rate = rho * view_rate[view]
        order_mat = before if view == 0 else before.T
        ahead = jnp.dot(
            order_mat, depth_rate.reshape(shape[0], -1), precision=lax.Precision.HIGHEST
        ).reshape(shape)
        weight = -jnp.expm1(-depth_rate) * jnp.exp(-ahead) * lit_field * 4.0
        channels = [
            jnp.sum(weight * jnp.exp(-8.0 * (rho - centers[k]) ** 2), axis=0) for k in range(3)
        ]
        channels.append(jnp.sum(depth_rate, axis=0))
        layers.append(jnp.stack(channels))
    packed = jnp.stack(layers)
    received = lax.all_to_all(packed[None], "depth", split_axis=4, concat_axis=0, tiled=True)
    order_mat = (rank[:, None, :] < rank[:, :, None]).astype(jnp.float32)
    optical = received[:, :, 3]
    front = jnp.einsum("vij,jvrc->ivrc", order_mat, optical, precision=lax.Precision.HIGHEST)
    colors = jnp.sum(received[:, :, :3] * jnp.exp(-front)[:, :, None], axis=0)
    opacity = -jnp.expm1(-jnp.sum(optical, axis=0))
    return jnp.concatenate([colors, opacity[:, None]], axis=1)


def solution(mesh):
    return jax.shard_map(
        shards,
        mesh=mesh,
        in_specs=(P("depth", "light", None), P(), P(), P(), P()),
        out_specs=P(None, None, "light", "depth"),
        check_vma=False,
    )
```

profile of v0, /device:TPU:0, one launch (start us, length us, event | category | flops | bytes accessed | tf_op | source)
XLA Modules:
  0.0 93.7 jit_solution(14077014898367945659)
XLA Ops:
  0.0 0.8 fusion.68
  0.8 3.3 %fusion.7 = (f32[8,8,8,1024]{3,2,1,0:T(8,128)S(1)}, f32[64,1024]{1,0:T(8,128)S(1)}, f32[8,8,8,1024]{3,2,1,0:T(8,128)}) fusion(f32[1024]{0:T(1024)S(1)} %bitcast.100, bf16[64,8,1024]{2,1,0:T(8,128)(2,1)} %param.5, f32[1024]{0:T(1024)} %param.6, f32[1024]{0:T(1024)S(1)} %bitcast.111), kind=kLoop, calls=%fused_computation.13 | loop fusion | flops 2555904 | bytes 5517312
  4.1 0.3 copy.37
  4.4 0.5 broadcast.20
  4.9 1.9 %reduce.1 = f32[1024,64]{1,0:T(8,128)S(1)} reduce(f32[1024,1,64]{2,1,0:T(1,128)S(1)} %bitcast.92, f32[]{:T(128)} %broadcast.20), dimensions={1}, to_apply=%bitcast.74.reduce_sub_computation | reduce | bytes 524292
  6.9 0.0 copy-start.3
  6.9 0.3 reshape.39
  7.2 15.1 %all_to_all.51 = f32[4,1,16384]{2,1,0:T(1,128)} all-to-all(f32[4,1,16384]{2,1,0:T(1,128)S(1)} %reshape.39), channel_id=1, replica_groups=mesh['depth'=8,'light'=4] {'light'}, dimensions={0} | all-to-all | bytes 524288 | tf_op jit(solution)/shard_map/all_to_all | solution.py:21
  22.3 0.0 copy-start
  22.3 0.0 copy-start.2
  22.3 2.3 %reduce.2 = f32[4,16384]{1,0:T(4,128)S(1)} reduce(f32[4,1,16384]{2,1,0:T(1,128)} %all_to_all.51, f32[]{:T(128)} %broadcast.20), dimensions={1}, to_apply=%all_to_all.37.reduce_sub_computation | reduce | bytes 524292 | tf_op jit(solution)/shard_map/all_to_all | solution.py:21
  24.6 1.4 %reshape.40 = f32[1024,1,64]{2,1,0:T(1,128)} reshape(f32[4,16384]{1,0:T(4,128)S(1)} %reduce.2) | data formatting | bytes 524288
  26.1 1.2 %copy.38 = f32[1,64,4,256]{3,1,2,0:T(8,128)S(1)} copy(f32[1,64,4,256]{1,3,2,0:T(8,128)} %bitcast.91) | data formatting | bytes 524288 | tf_op jit(solution)/shard_map/all_to_all | solution.py:21
  27.3 0.7 reduce-window_subtract_fusion
  28.1 3.6 %all-to-all-start.1 = ((f32[4,64,256]{2,1,0:T(8,128)}), f32[4,64,256]{2,1,0:T(8,128)S(1)}, u32[]{:S(2)}, u32[]{:S(2)}) async-start(f32[4,64,256]{2,1,0:T(8,128)} %reduce-window_subtract_fusion), calls=%async_computation.1 | async-start | bytes 524288 | tf_op jit(solution)/shard_map/all_to_all | solution.py:11
  31.7 0.0 copy-done.3
  31.7 0.6 fusion.69
  32.3 7.1 %all-to-all-done.1 = f32[4,64,256]{2,1,0:T(8,128)S(1)} async-done(((f32[4,64,256]{2,1,0:T(8,128)}), f32[4,64,256]{2,1,0:T(8,128)S(1)}, u32[]{:S(2)}, u32[]{:S(2)}) %all-to-all-start.1) | async-done | bytes 262176 | tf_op jit(solution)/shard_map/all_to_all | solution.py:11
  39.4 0.2 copy.39
  39.6 0.0 copy-done
  39.6 0.0 copy-done.2
  39.6 1.0 %fusion.16 = f32[64,8,1024]{2,0,1:T(8,128)S(1)} fusion(f32[64,1024]{1,0:T(8,128)S(1)} %bitcast.97, f32[1024]{0:T(1024)S(1)} %copy-done.2, bf16[64,8,1024]{2,1,0:T(8,128)(2,1)S(1)} %copy-done), kind=kOutput, calls=%fused_computation.22 | output fusion | flops 7340032 | bytes 3411968 | tf_op jit(solution)/shard_map/jit(cumsum)/reduce_window_sum | solution.py:18
  40.6 0.0 copy-start.1
  40.6 3.2 %fusion.13 = f32[64,8,1024]{2,0,1:T(8,128)S(1)} fusion(f32[64,8,1024]{2,0,1:T(8,128)S(1)} %fusion.16, f32[1024]{0:T(1024)S(1)} %bitcast.101, bf16[64,8,1024]{2,1,0:T(8,128)(2,1)S(1)} %copy-done, f32[8,8,8,1024]{3,2,1,0:T(8,128)S(1)} %get-tuple-element.16), kind=kOutput, calls=%fused_computation.19 | convolution fusion | flops 406851584 | bytes 7344128 | tf_op jit(solution)/shard_map/dot_general | solution.py:31
  43.8 0.0 copy-done.1
  43.8 7.2 %fusion.27 = (f32[8,1024]{1,0:T(8,128)S(1)}, f32[8,1024]{1,0:T(8,128)S(1)}, f32[8,1024]{1,0:T(8,128)S(1)}, f32[8,1024]{1,0:T(8,128)S(1)}, f32[8,1024]{1,0:T(8,12...) fusion(f32[]{:T(128)} %bitcast.9, bf16[64,8,1024]{2,1,0:T(8,128)(2,1)S(1)} %copy-done, ...), kind=kOutput, calls=%fused_computation.33 | convolution fusion | flops 419368960 | bytes 7610380 | tf_op jit(solution)/shard_map/dot_general | solution.py:31
  51.1 4.3 %copy.42 = f32[2,4,8,1024]{2,0,1,3:T(2,128)} copy(f32[2,4,8,1024]{3,2,1,0:T(8,128)S(1)} %pad_maximum_fusion) | data formatting | bytes 524288 | tf_op jit(solution)/shard_map/stack | solution.py:40
  55.4 5.5 %bitcast_bitcast_fusion = f32[1024,1,4,2,8]{4,3,2,1,0:T(2,128)} fusion(f32[2,4,8,1024]{2,0,1,3:T(2,128)} %copy.42), kind=kLoop, calls=%fused_computation.80 | loop fusion | bytes 524288
  61.0 8.3 %reshape.41 = f32[8,1,8192]{2,1,0:T(1,128)S(1)} reshape(f32[1024,1,4,2,8]{4,3,2,1,0:T(2,128)} %bitcast_bitcast_fusion) | data formatting | bytes 524288
  69.2 10.5 %all_to_all.52 = f32[8,1,8192]{2,1,0:T(1,128)S(1)} all-to-all(f32[8,1,8192]{2,1,0:T(1,128)S(1)} %reshape.41), channel_id=1, replica_groups=mesh['depth'=8,'light'=4] {'depth'}, dimensions={0} | all-to-all | bytes 524288 | tf_op jit(solution)/shard_map/all_to_all | solution.py:41
  79.7 1.2 %reduce.3 = f32[8,8192]{1,0:T(8,128)S(1)} reduce(f32[8,1,8192]{2,1,0:T(1,128)S(1)} %all_to_all.52, f32[]{:T(128)} %broadcast.20), dimensions={1}, to_apply=%all_to_all.44.reduce_sub_computation | reduce | bytes 524292 | tf_op jit(solution)/shard_map/all_to_all | solution.py:41
  80.9 8.3 %reshape.42 = f32[1024,1,4,2,8]{4,3,2,1,0:T(2,128)} reshape(f32[8,8192]{1,0:T(8,128)S(1)} %reduce.3) | data formatting | bytes 524288
  89.2 0.0 copy-start.4
  89.2 3.5 %copy.48 = f32[1,2,4,8,8,128]{5,4,3,1,2,0:T(8,128)S(1)} copy(f32[1,2,4,8,8,128]{3,1,2,5,4,0:T(2,128)} %bitcast.90) | data formatting | bytes 524288 | tf_op jit(solution)/shard_map/all_to_all | solution.py:41
  92.8 0.0 copy-done.4
  92.8 0.2 fusion.54
  93.0 0.1 fusion.57
  93.1 0.6 copy.44
  (6 shorter events, 0.1 us)
Async XLA Ops:
  6.9 24.8 %copy-start.3 = (f32[3]{0:T(128)S(1)}, f32[3]{0:T(128)}, u32[]{:S(2)}) copy-start(f32[3]{0:T(128)} %param.8) | copy-start | bytes 40
  22.3 17.3 %copy-start = (bf16[64,8,1024]{2,1,0:T(8,128)(2,1)S(1)}, bf16[64,8,1024]{2,1,0:T(8,128)(2,1)}, u32[]{:S(2)}) copy-start(bf16[64,8,1024]{2,1,0:T(8,128)(2,1)} %param.5) | copy-start | bytes 3145732
  22.3 17.3 %copy-start.2 = (f32[1024]{0:T(1024)S(1)}, f32[1024]{0:T(1024)}, u32[]{:S(2)}) copy-start(f32[1024]{0:T(1024)} %param.6) | copy-start | bytes 12292
  28.1 11.3 %all-to-all-start.1 = ((f32[4,64,256]{2,1,0:T(8,128)}), f32[4,64,256]{2,1,0:T(8,128)S(1)}, u32[]{:S(2)}, u32[]{:S(2)}) async-start(f32[4,64,256]{2,1,0:T(8,128)} %reduce-window_subtract_fusion), calls=%async_computation.1 | async-start | bytes 524288 | tf_op jit(solution)/shard_map/all_to_all | solution.py:11
  40.6 3.2 %copy-start.1 = (f32[8,8,8,1024]{3,2,1,0:T(8,128)S(1)}, f32[8,8,8,1024]{3,2,1,0:T(8,128)}, u32[]{:S(2)}) copy-start(f32[8,8,8,1024]{3,2,1,0:T(8,128)} %get-tuple-element.18) | copy-start | bytes 6291460
  89.2 3.5 %copy-start.4 = (s32[2,8]{1,0:T(2,128)S(1)}, s32[2,8]{1,0:T(2,128)}, u32[]{:S(2)}) copy-start(s32[2,8]{1,0:T(2,128)} %param.9) | copy-start | bytes 196
where the time goes:
time: 94.3 us; the launch traced here: 93.7 us
  local copies, waits for them, and re-layouts  36 us (38%)
  blocking collectives  25.6 us (27%)
  other arithmetic  10.7 us (11%)
  matrix products  10.6 us (11%)
  waiting for transfers between devices  7.13 us (8%)
  starting transfers between devices  3.58 us (4%)
    unnamed x17, local copies, waits for them, and re-layouts  24.5 us
    all_to_all x1, blocking collectives, shards(): lax.all_to_all(totals[None], 'light', split_axis=2, concat_axis=0, tiled=...  15.1 us
    all_to_all x1, blocking collectives, shards(): lax.all_to_all(packed[None], 'depth', split_axis=4, concat_axis=0, tiled=...  10.5 us
    dot_general x2, matrix products, shards(): jnp.dot(order_mat, depth_rate.reshape(shape[0], -1), precision=lax.Precis...  10.4 us
    all_to_all x1, waiting for transfers between devices, lower_sums(): lax.all_to_all(below, 'light', split_axis=0, concat_axis=2, tiled=True)  7.13 us
    unnamed x2, other arithmetic  5.22 us
    another operation x1, local copies, waits for them, and re-layouts, shards(): packed = jnp.stack(layers)  4.33 us
    all_to_all x1, starting transfers between devices, lower_sums(): lax.all_to_all(below, 'light', split_axis=0, concat_axis=2, tiled=True)  3.58 us
  transfers between devices with their start and end apart: 1, of which 1 were waited for; matrix products, arithmetic and copies ran while one was open for 1% of the time, Pallas kernels for 0%

commit v1 on v0

v1 whole, which is shorter than its diff:
```python
import functools
import math

import jax
import jax.numpy as jnp
from jax import lax
from jax.experimental import pallas as pl
from jax.experimental.pallas import tpu as pltpu
from jax.sharding import PartitionSpec as P

F32 = jnp.float32
LOG2E = math.log2(math.e)
LANES = 128


def row_sums_kernel(samples, rows, rho_ref, keep_ref, send_ref, total_ref):
    half = samples // 2
    odd = lax.axis_index("light") % 2
    wide = (samples, samples * rows)
    target = (lax.broadcasted_iota(jnp.int32, wide, 0) + half * odd) % samples
    source = lax.broadcasted_iota(jnp.int32, wide, 1)
    of_sample = (source // rows == target).astype(jnp.bfloat16)
    narrow = (rows, samples * rows)
    of_row = (
        lax.broadcasted_iota(jnp.int32, narrow, 1) % rows
        == lax.broadcasted_iota(jnp.int32, narrow, 0)
    ).astype(jnp.bfloat16)
    rho = rho_ref[...]
    sums = jnp.dot(of_sample, rho, preferred_element_type=F32)
    keep_ref[...] = sums[:half]
    send_ref[...] = sums[half:]
    total_ref[...] = jnp.dot(of_row, rho, preferred_element_type=F32)


def row_sums(rho, samples, rows):
    columns = rho.shape[1]
    half = jax.ShapeDtypeStruct((samples // 2, columns), F32)
    return pl.pallas_call(
        functools.partial(row_sums_kernel, samples, rows),
        out_shape=(half, half, jax.ShapeDtypeStruct((rows, columns), F32)),
    )(rho)


def main_kernel(
    samples, rows, width, rho_ref, mine_ref, other_ref, total_ref, light_ref, view_ref,
    center_ref, out_ref, above_ref, light_sum,
):
    half = samples // 2
    odd = lax.axis_index("light") % 2
    light_sum[pl.ds(pl.multiple_of(half * odd, half), half), :] = mine_ref[...]
    light_sum[pl.ds(pl.multiple_of(half * (1 - odd), half), half), :] = other_ref[...]
    columns = rho_ref.shape[1]

    block = 256
    square = (block, block)
    i = lax.broadcasted_iota(jnp.int32, square, 0)
    j = lax.broadcasted_iota(jnp.int32, square, 1)
    above = ((i // rows == j // rows) & (j < i)).astype(jnp.bfloat16)
    for start in range(0, samples * rows, block):
        above_ref[start : start + block, :] = jnp.dot(
            above, rho_ref[start : start + block, :], preferred_element_type=F32
        )

    shape = (rows, width)
    tone = [center_ref[k] * (16.0 * LOG2E) for k in range(3)]
    for first in range(0, columns, width):
        at = pl.ds(first, width)
        light = jnp.broadcast_to(light_ref[:, at] * LOG2E, shape)
        r0, r1 = view_ref[0:1, at], view_ref[1:2, at]
        fade = [jnp.broadcast_to(c, shape) for c in (r0, r0 * r0 * 0.5, r0 * r0 * r0 * (1 / 6))]
        grow = [jnp.broadcast_to(c, shape) for c in (r1, r1 * r1 * 0.5, r1 * r1 * r1 * (1 / 6))]

        def pair(step, carry):
            clear, behind, *sums = carry
            two = rho_ref[pl.ds(pl.multiple_of(step * 2 * rows, 2 * rows), 2 * rows), at].astype(F32)
            for part in range(2):
                rho = two[part * rows : (part + 1) * rows]
                s = step * 2 + part
                inner = above_ref[pl.ds(pl.multiple_of(s * rows, rows), rows), at]
                outer = light_sum[pl.ds(s, 1), at]
                tint = jnp.exp2(rho * rho * (-8.0 * LOG2E) - light * (inner + outer))
                w0 = clear * (rho * (fade[0] - rho * (fade[1] - rho * fade[2])))
                clear = clear - w0
                w1 = behind * (rho * (grow[0] + rho * (grow[1] + rho * grow[2])))
                behind = behind + w1
                w0, w1 = w0 * tint, w1 * tint
                for k in range(3):
                    e = jnp.exp2(rho * tone[k])
                    sums[k] = sums[k] + w0 * e
                    sums[3 + k] = sums[3 + k] + w1 * e
            return (clear, behind, *sums)

        zero = jnp.zeros(shape, F32)
        total = total_ref[:, at]
        start = (jnp.ones(shape, F32), jnp.exp2(total * view_ref[1:2, at] * -LOG2E)) + (zero,) * 6
        done = lax.fori_loop(0, samples // 2, pair, start, unroll=4)
        for k in range(3):
            c = jnp.full(shape, center_ref[k], F32)
            scale = 4.0 * jnp.exp2(c * c * (-8.0 * LOG2E))
            for view in range(2):
                value = done[2 + 3 * view + k] * scale
                for tile in range(width // LANES):
                    out_ref[first // LANES + tile, 3 * view + k] = value[:, tile * LANES : (tile + 1) * LANES]
        for tile in range(width // LANES):
            out_ref[first // LANES + tile, 6] = total[:, tile * LANES : (tile + 1) * LANES]


def brick_colors(rho, mine, other, total, light_rate, view_rate, centers, samples, rows):
    columns = rho.shape[1]
    vmem, smem = pl.BlockSpec(memory_space=pltpu.VMEM), pl.BlockSpec(memory_space=pltpu.SMEM)
    return pl.pallas_call(
        functools.partial(main_kernel, samples, rows, 256),
        out_shape=jax.ShapeDtypeStruct((columns // LANES, 7, rows, LANES), F32),
        in_specs=[vmem] * 6 + [smem],
        out_specs=vmem,
        scratch_shapes=[
            pltpu.VMEM((samples * rows, columns), F32),
            pltpu.VMEM((samples, columns), F32),
        ],
    )(rho, mine, other, total, light_rate.reshape(1, -1), view_rate, centers)


def composite_kernel(bricks, got_ref, rate_ref, rank_ref, out_ref, order_ref):
    shape = out_ref.shape[2:]
    for view in range(2):
        def place(d, carry, view=view):
            order_ref[view, rank_ref[view, d]] = d
            return carry

        lax.fori_loop(0, bricks, place, 0, unroll=bricks <= 8)
        rate = jnp.broadcast_to(rate_ref[view : view + 1, :], shape)

        def nearer(p, carry, view=view, rate=rate):
            front, red, green, blue = carry
            d = order_ref[view, p]
            seen = jnp.exp2(front * rate * -LOG2E)
            red = red + got_ref[d, 3 * view] * seen
            green = green + got_ref[d, 3 * view + 1] * seen
            blue = blue + got_ref[d, 3 * view + 2] * seen
            return front + got_ref[d, 6], red, green, blue

        zero = jnp.zeros(shape, F32)
        depth, *colors = lax.fori_loop(0, bricks, nearer, (zero,) * 4, unroll=bricks <= 8)
        for k in range(3):
            out_ref[view, k] = colors[k]
        depth = depth * rate
        small = jnp.full(shape, 1.0, F32)
        for n in range(8, 1, -1):
            small = 1.0 - depth * (1.0 / n) * small
        out_ref[view, 3] = jnp.where(depth < 0.35, depth * small, 1.0 - jnp.exp2(depth * -LOG2E))


def composite(got, rate, rank):
    bricks, _, rows, columns = got.shape
    vmem, smem = pl.BlockSpec(memory_space=pltpu.VMEM), pl.BlockSpec(memory_space=pltpu.SMEM)
    return pl.pallas_call(
        functools.partial(composite_kernel, bricks),
        out_shape=jax.ShapeDtypeStruct((2, 4, rows, columns), F32),
        in_specs=[vmem, vmem, smem],
        out_specs=vmem,
        scratch_shapes=[pltpu.SMEM((2, bricks), jnp.int32)],
    )(got, rate, rank)


def swap(x, stride, n):
    return lax.ppermute(x, "light", [(i, i ^ stride) for i in range(n)])


def lower_halves(keep, send, stride, n):
    odd = (lax.axis_index("light") // stride) % 2 == 1
    sibling = swap(send, stride, n)
    below = lower(keep + sibling, 2 * stride, n)
    other = swap(below + jnp.where(odd, 0.0, keep), stride, n)
    return below + jnp.where(odd, sibling, 0.0), other


def lower(x, stride, n):
    if stride == n:
        return jnp.zeros_like(x)
    odd = (lax.axis_index("light") // stride) % 2 == 1
    if 2 * stride == n:
        return jnp.where(odd, swap(x, stride, n), 0.0)
    half = x.shape[0] // 2
    first, last = x[:half], x[half:]
    mine, other = lower_halves(jnp.where(odd, last, first), jnp.where(odd, first, last), stride, n)
    return jnp.where(odd, jnp.concatenate([other, mine]), jnp.concatenate([mine, other]))


def shards(depth_n, light_n, density, light_rate, view_rate, centers, rank):
    samples, rows, columns = density.shape
    rho = density.reshape(samples * rows, columns)
    keep, send, total = row_sums(rho, samples, rows)
    mine, other = lower_halves(keep, send, 1, light_n)
    packed = brick_colors(rho, mine, other, total, light_rate, view_rate, centers, samples, rows)
    own = columns // depth_n
    if own % LANES == 0:
        parts = packed.reshape(depth_n, own // LANES, 7, rows, LANES)
        parts = parts[:, 0] if own == LANES else parts.transpose(0, 2, 3, 1, 4).reshape(depth_n, 7, rows, own)
    else:
        parts = packed.reshape(columns // LANES, 7, rows, LANES // own, own)
        parts = parts.transpose(0, 3, 1, 2, 4).reshape(depth_n, 7, rows, own)
    got = lax.all_to_all(parts, "depth", split_axis=0, concat_axis=0, tiled=True)
    rate = lax.dynamic_slice_in_dim(view_rate, lax.axis_index("depth") * own, own, axis=1)
    return composite(got, rate, rank)


def solution(mesh):
    return jax.shard_map(
        functools.partial(shards, mesh.shape["depth"], mesh.shape["light"]),
        mesh=mesh,
        in_specs=(P("depth", "light", None), P(), P(), P(), P()),
        out_specs=P(None, None, "light", "depth"),
        check_vma=False,
    )
```

time: 94.3 us -> 43.2 us (0.46)
  local copies, waits for them, and re-layouts: 36 us -> 2.6 us
  blocking collectives: 25.6 us -> 0 us
  waiting for transfers between devices: 7.13 us -> 19.1 us
  matrix products: 10.6 us -> 0 us
  Pallas kernels: 0 us -> 9.51 us
  other arithmetic: 10.7 us -> 1.67 us
  starting transfers between devices: 3.58 us -> 9.94 us
    all_to_all x2 -> x0, blocking collectives: 25.6 us -> none  [the longest x1 15.1 us: shards(): lax.all_to_all(totals[None], 'light', split_axis=2, concat_axis=0, tiled=...]
    unnamed x17 -> x6, local copies, waits for them, and re-layouts: 24.5 us -> 1.34 us
    ppermute x0 -> x3, waiting for transfers between devices: none -> 13.8 us  [swap(): return lax.ppermute(x, 'light', [(i, i ^ stride) for i in range(n)])]
    dot_general x3 -> x0, matrix products: 10.6 us -> none  [the longest x2 10.4 us: shards(): jnp.dot(order_mat, depth_rate.reshape(shape[0], -1), precision=lax.Precis...]
    pallas_call x0 -> x3, Pallas kernels: none -> 9.51 us  [the longest x1 5.61 us: brick_colors(): pl.pallas_call(functools.partial(main_kernel, samples, rows, 256), out_sh...]
    ppermute x0 -> x3, starting transfers between devices: none -> 6.37 us  [swap(): return lax.ppermute(x, 'light', [(i, i ^ stride) for i in range(n)])]
    unnamed x2 -> x0, other arithmetic: 5.22 us -> none
    all_to_all x3 -> x0, local copies, waits for them, and re-layouts: 4.86 us -> none  [the longest x1 3.47 us: shards(): lax.all_to_all(packed[None], 'depth', split_axis=4, concat_axis=0, tiled=...]
  transfers between devices with their start and end apart: 1 -> 4, of which waited for: 1 -> 4; matrix products, arithmetic and copies ran while one was open for 1% -> 3% of each run, Pallas kernels for 0% -> 0%
where the time goes in v1:
time: 43.2 us; the launch traced here: 42.8 us
  waiting for transfers between devices  19.1 us (44%)
  starting transfers between devices  9.94 us (23%)
  Pallas kernels  9.51 us (22%)
  local copies, waits for them, and re-layouts  2.6 us (6%)
  other arithmetic  1.67 us (4%)
    ppermute x3, waiting for transfers between devices, swap(): return lax.ppermute(x, 'light', [(i, i ^ stride) for i in range(n)])  13.8 us
    ppermute x3, starting transfers between devices, swap(): return lax.ppermute(x, 'light', [(i, i ^ stride) for i in range(n)])  6.37 us
    pallas_call x1, Pallas kernels, brick_colors(): pl.pallas_call(functools.partial(main_kernel, samples, rows, 256), out_sh...  5.61 us
    all_to_all x1, waiting for transfers between devices, shards(): lax.all_to_all(parts, 'depth', split_axis=0, concat_axis=0, tiled=True)  5.33 us
    all_to_all x1, starting transfers between devices, shards(): lax.all_to_all(parts, 'depth', split_axis=0, concat_axis=0, tiled=True)  3.57 us
    pallas_call x1, Pallas kernels, row_sums(): pl.pallas_call(functools.partial(row_sums_kernel, samples, rows), out_sha...  2.27 us
    pallas_call x1, Pallas kernels, composite(): pl.pallas_call(functools.partial(composite_kernel, bricks), out_shape=jax...  1.63 us
    unnamed x6, local copies, waits for them, and re-layouts  1.34 us
  transfers between devices with their start and end apart: 4, of which 4 were waited for; matrix products, arithmetic and copies ran while one was open for 3% of the time, Pallas kernels for 0%

profile of v1, /device:TPU:0, one launch (start us, length us, event | category | flops | bytes accessed | tf_op | source)
XLA Modules:
  0.0 42.8 jit_solution(17912548356885534870)
XLA Ops:
  0.0 2.3 %shard_map.55 = (f32[32,1024]{1,0:T(8,128)}, f32[32,1024]{1,0:T(8,128)}, f32[8,1024]{1,0:T(8,128)}) custom-call(bf16[512,1024]{1,0:T(8,128)(2,1)} %bitcast.2), custom_call_target="tpu_custom_call" | custom-call | tf_op jit(solution)/shard_map/pallas_call | solution.py:38
  2.3 3.0 %collective-permute-start = (f32[32,1024]{1,0:T(8,128)}, f32[32,1024]{1,0:T(8,128)S(1)}, u32[]{:S(2)}, u32[]{:S(2)}) collective-permute-start(f32[32,1024]{1,0:T(8,128)} %get-tuple-element.9), channel_id=1, source_target_pairs={{0,1},{1,0},{2,3},{3,2},{4,5},{5,4},{6,7},{7,6},{8,9},{9,8},{10,11... | collective-permute-start | bytes 393224 | tf_op jit(solution)/shard_map/ppermute | solution.py:166
  5.3 3.7 %collective-permute-done = f32[32,1024]{1,0:T(8,128)S(1)} collective-permute-done((f32[32,1024]{1,0:T(8,128)}, f32[32,1024]{1,0:T(8,128)S(1)}, u32[]{:S(2)}, u32[]{:S(2)}) %collective-permute-start) | collective-permute-done | bytes 131104 | tf_op jit(solution)/shard_map/ppermute | solution.py:166
  9.0 0.0 copy-start.1
  9.0 1.0 %add.22 = f32[32,1024]{1,0:T(8,128)S(1)} add(f32[32,1024]{1,0:T(8,128)} %get-tuple-element.8, f32[32,1024]{1,0:T(8,128)S(1)} %collective-permute-done) | non-fusion elementwise | flops 32768 | bytes 393216 | tf_op jit(solution)/shard_map/add | solution.py:172
  10.0 2.8 %collective-permute-start.1 = (f32[32,1024]{1,0:T(8,128)S(1)}, f32[32,1024]{1,0:T(8,128)S(1)}, u32[]{:S(2)}, u32[]{:S(2)}) collective-permute-start(f32[32,1024]{1,0:T(8,128)S(1)} %add.22), channel_id=1, source_target_pairs={{0,2},{1,3},{2,0},{3,1},{4,6},{5,7},{6,4},{7,5},{8,10},{9,11},{10,... | collective-permute-start | bytes 393224 | tf_op jit(solution)/shard_map/ppermute | solution.py:166
  12.8 5.6 %collective-permute-done.1 = f32[32,1024]{1,0:T(8,128)S(1)} collective-permute-done((f32[32,1024]{1,0:T(8,128)S(1)}, f32[32,1024]{1,0:T(8,128)S(1)}, u32[]{:S(2)}, u32[]{:S(2)}) %collective-permute-start.1) | collective-permute-done | bytes 131104 | tf_op jit(solution)/shard_map/ppermute | solution.py:166
  18.5 0.0 copy-done.1
  18.5 0.7 %select_add_fusion = (f32[32,1024]{1,0:T(8,128)S(1)}, f32[32,1024]{1,0:T(8,128)}) fusion(f32[32,1024]{1,0:T(8,128)S(1)} %copy-done.1, f32[32,1024]{1,0:T(8,128)S(1)} %collective-permute-done.1, pred[]{:T(512)S(6)} %eq.10, pred[]{:T(512)S(6)} %eq.9, f32[32,1024]{1,0:T(8,128)S(1)} %collective-permute-done), kind=kLoop, calls=%fused_computation | loop fusion | flops 163840 | bytes 655362 | tf_op jit(solution)/shard_map/add | solution.py:173
  19.1 0.5 %collective-permute-start.2 = (f32[32,1024]{1,0:T(8,128)S(1)}, f32[32,1024]{1,0:T(8,128)S(1)}, u32[]{:S(2)}, u32[]{:S(2)}) collective-permute-start(f32[32,1024]{1,0:T(8,128)S(1)} %get-tuple-element.11), channel_id=1, source_target_pairs={{0,1},{1,0},{2,3},{3,2},{4,5},{5,4},{6,7},{7,6},{8,9},{9,8},{10,11... | collective-permute-start | bytes 393224 | tf_op jit(solution)/shard_map/ppermute | solution.py:166
  19.7 4.4 %collective-permute-done.2.other_ref = f32[32,1024]{1,0:T(8,128)S(1)} collective-permute-done((f32[32,1024]{1,0:T(8,128)S(1)}, f32[32,1024]{1,0:T(8,128)S(1)}, u32[]{:S(2)}, u32[]{:S(2)}) %collective-permute-start.2) | collective-permute-done | bytes 131104 | tf_op jit(solution)/shard_map/ppermute | solution.py:166
  24.1 0.0 copy-start.2
  24.1 0.6 %copy-done.2 = f32[32,1024]{1,0:T(8,128)} copy-done((f32[32,1024]{1,0:T(8,128)}, f32[32,1024]{1,0:T(8,128)S(1)}, u32[]{:S(2)}) %copy-start.2) | copy-done | bytes 131096
  24.8 5.6 %shard_map.56 = f32[8,7,8,128]{3,2,1,0:T(8,128)} custom-call(bf16[512,1024]{1,0:T(8,128)(2,1)} %bitcast.3, f32[32,1024]{1,0:T(8,128)} %get-tuple-element.12.mine_ref, f32[32,1024]{1,0:T(8,128)} %copy-done.2, f32[8,1024]{1,0:T(8,128)} %get-tuple-element.10.total_ref, f32[1,1024]{1,0:T(1,128)} %bitcast.4, f32[2,1024]{1,0:T(2,128)} %view_ref.1, f32[3]{0:T(128)} %center_ref.1), custom_call_target="tpu_custom_call" | custom-call | tf_op jit(solution)/shard_map/pallas_call | solution.py:111
  30.4 3.6 %all-to-all-start = ((f32[8,7,8,128]{3,2,1,0:T(8,128)}), f32[8,7,8,128]{3,2,1,0:T(8,128)S(1)}, u32[]{:S(2)}, u32[]{:S(2)}) async-start(f32[8,7,8,128]{3,2,1,0:T(8,128)} %shard_map.56), calls=%async_computation | async-start | bytes 458752 | tf_op jit(solution)/shard_map/all_to_all | solution.py:202
  33.9 1.3 %constant_dynamic-slice_fusion.rate_ref = f32[2,128]{1,0:T(2,128)} fusion(f32[2,1024]{1,0:T(2,128)} %view_ref.1, s32[]{:T(128)S(6)} %select_n.47), kind=kLoop, calls=%fused_computation.2 | loop fusion | bytes 2052 | tf_op jit(solution)/shard_map/dynamic_slice | solution.py:203
  35.2 5.3 %all-to-all-done.got_ref = f32[8,7,8,128]{3,2,1,0:T(8,128)S(1)} async-done(((f32[8,7,8,128]{3,2,1,0:T(8,128)}), f32[8,7,8,128]{3,2,1,0:T(8,128)S(1)}, u32[]{:S(2)}, u32[]{:S(2)}) %all-to-all-start) | async-done | bytes 229408 | tf_op jit(solution)/shard_map/all_to_all | solution.py:202
  40.5 0.0 copy-start
  40.5 0.7 %copy-done = f32[8,7,8,128]{3,2,1,0:T(8,128)} copy-done((f32[8,7,8,128]{3,2,1,0:T(8,128)}, f32[8,7,8,128]{3,2,1,0:T(8,128)S(1)}, u32[]{:S(2)}) %copy-start) | copy-done | bytes 229400
  41.2 1.6 %shard_map.57 = f32[2,4,8,128]{3,2,1,0:T(8,128)} custom-call(f32[8,7,8,128]{3,2,1,0:T(8,128)} %copy-done, f32[2,128]{1,0:T(2,128)} %constant_dynamic-slice_fusion.rate_ref, s32[2,8]{1,0:T(2,128)} %rank_ref.1), custom_call_target="tpu_custom_call" | custom-call | tf_op jit(solution)/shard_map/pallas_call | solution.py:156
Async XLA Ops:
  2.3 6.7 %collective-permute-start = (f32[32,1024]{1,0:T(8,128)}, f32[32,1024]{1,0:T(8,128)S(1)}, u32[]{:S(2)}, u32[]{:S(2)}) collective-permute-start(f32[32,1024]{1,0:T(8,128)} %get-tuple-element.9), channel_id=1, source_target_pairs={{0,1},{1,0},{2,3},{3,2},{4,5},{5,4},{6,7},{7,6},{8,9},{9,8},{10,11... | collective-permute-start | bytes 393224 | tf_op jit(solution)/shard_map/ppermute | solution.py:166
  9.0 9.5 %copy-start.1 = (f32[32,1024]{1,0:T(8,128)S(1)}, f32[32,1024]{1,0:T(8,128)}, u32[]{:S(2)}) copy-start(f32[32,1024]{1,0:T(8,128)} %get-tuple-element.8) | copy-start | bytes 393220
  10.0 8.5 %collective-permute-start.1 = (f32[32,1024]{1,0:T(8,128)S(1)}, f32[32,1024]{1,0:T(8,128)S(1)}, u32[]{:S(2)}, u32[]{:S(2)}) collective-permute-start(f32[32,1024]{1,0:T(8,128)S(1)} %add.22), channel_id=1, source_target_pairs={{0,2},{1,3},{2,0},{3,1},{4,6},{5,7},{6,4},{7,5},{8,10},{9,11},{10,... | collective-permute-start | bytes 393224 | tf_op jit(solution)/shard_map/ppermute | solution.py:166
  19.1 5.0 %collective-permute-start.2 = (f32[32,1024]{1,0:T(8,128)S(1)}, f32[32,1024]{1,0:T(8,128)S(1)}, u32[]{:S(2)}, u32[]{:S(2)}) collective-permute-start(f32[32,1024]{1,0:T(8,128)S(1)} %get-tuple-element.11), channel_id=1, source_target_pairs={{0,1},{1,0},{2,3},{3,2},{4,5},{5,4},{6,7},{7,6},{8,9},{9,8},{10,11... | collective-permute-start | bytes 393224 | tf_op jit(solution)/shard_map/ppermute | solution.py:166
  24.1 0.7 %copy-start.2 = (f32[32,1024]{1,0:T(8,128)}, f32[32,1024]{1,0:T(8,128)S(1)}, u32[]{:S(2)}) copy-start(f32[32,1024]{1,0:T(8,128)S(1)} %collective-permute-done.2.other_ref) | copy-start | bytes 393220
  30.4 10.2 %all-to-all-start = ((f32[8,7,8,128]{3,2,1,0:T(8,128)}), f32[8,7,8,128]{3,2,1,0:T(8,128)S(1)}, u32[]{:S(2)}, u32[]{:S(2)}) async-start(f32[8,7,8,128]{3,2,1,0:T(8,128)} %shard_map.56), calls=%async_computation | async-start | bytes 458752 | tf_op jit(solution)/shard_map/all_to_all | solution.py:202
  40.5 0.7 %copy-start = (f32[8,7,8,128]{3,2,1,0:T(8,128)}, f32[8,7,8,128]{3,2,1,0:T(8,128)S(1)}, u32[]{:S(2)}) copy-start(f32[8,7,8,128]{3,2,1,0:T(8,128)S(1)} %all-to-all-done.got_ref) | copy-start | bytes 688132

commit v2 on v1

--- a/solution.py
+++ b/solution.py
@@ -13,44 +13,42 @@
 LANES = 128
 
 
-def row_sums_kernel(samples, rows, rho_ref, keep_ref, send_ref, total_ref):
-    half = samples // 2
+def sample_sums(rho, samples, rows):
+    wide = (samples, samples * rows)
+    target = lax.broadcasted_iota(jnp.int32, wide, 0)
+    source = lax.broadcasted_iota(jnp.int32, wide, 1)
+    return jnp.dot((source // rows == target).astype(jnp.bfloat16), rho, preferred_element_type=F32)
+
+
+def send_kernel(half, rows, rho_hbm, send_ref, rho_ref, sem):
     odd = lax.axis_index("light") % 2
-    wide = (samples, samples * rows)
-    target = (lax.broadcasted_iota(jnp.int32, wide, 0) + half * odd) % samples
-    source = lax.broadcasted_iota(jnp.int32, wide, 1)
-    of_sample = (source // rows == target).astype(jnp.bfloat16)
-    narrow = (rows, samples * rows)
+    first = pl.multiple_of((1 - odd) * half * rows, half * rows)
+    copy = pltpu.make_async_copy(rho_hbm.at[pl.ds(first, half * rows)], rho_ref, sem)
+    copy.start()
+    copy.wait()
+    send_ref[...] = sample_sums(rho_ref[...], half, rows)
+
+
+def keep_kernel(half, rows, rho_hbm, keep_ref, total_ref, rho_ref, sem):
+    odd = lax.axis_index("light") % 2
+    copy = pltpu.make_async_copy(rho_hbm, rho_ref, sem)
+    copy.start()
+    copy.wait()
+    first = pl.multiple_of(odd * half * rows, half * rows)
+    keep_ref[...] = sample_sums(rho_ref[pl.ds(first, half * rows), :], half, rows)
+    narrow = (rows, 2 * half * rows)
     of_row = (
         lax.broadcasted_iota(jnp.int32, narrow, 1) % rows
         == lax.broadcasted_iota(jnp.int32, narrow, 0)
     ).astype(jnp.bfloat16)
-    rho = rho_ref[...]
-    sums = jnp.dot(of_sample, rho, preferred_element_type=F32)
-    keep_ref[...] = sums[:half]
-    send_ref[...] = sums[half:]
-    total_ref[...] = jnp.dot(of_row, rho, preferred_element_type=F32)
-
-
-def row_sums(rho, samples, rows):
-    columns = rho.shape[1]
-    half = jax.ShapeDtypeStruct((samples // 2, columns), F32)
-    return pl.pallas_call(
-        functools.partial(row_sums_kernel, samples, rows),
-        out_shape=(half, half, jax.ShapeDtypeStruct((rows, columns), F32)),
-    )(rho)
-
-
-def main_kernel(
-    samples, rows, width, rho_ref, mine_ref, other_ref, total_ref, light_ref, view_ref,
-    center_ref, out_ref, above_ref, light_sum,
+    total_ref[...] = jnp.dot(of_row, rho_ref[...], preferred_element_type=F32)
+
+
+def pre_kernel(
+    samples, rows, width, rho_ref, total_ref, light_ref, view_ref, center_ref,
+    near_ref, far_ref, red_ref, green_ref, blue_ref, above_ref,
 ):
-    half = samples // 2
-    odd = lax.axis_index("light") % 2
-    light_sum[pl.ds(pl.multiple_of(half * odd, half), half), :] = mine_ref[...]
-    light_sum[pl.ds(pl.multiple_of(half * (1 - odd), half), half), :] = other_ref[...]
     columns = rho_ref.shape[1]
-
     block = 256
     square = (block, block)
     i = lax.broadcasted_iota(jnp.int32, square, 0)
@@ -71,53 +69,71 @@
         grow = [jnp.broadcast_to(c, shape) for c in (r1, r1 * r1 * 0.5, r1 * r1 * r1 * (1 / 6))]
 
         def pair(step, carry):
-            clear, behind, *sums = carry
+            clear, behind = carry
             two = rho_ref[pl.ds(pl.multiple_of(step * 2 * rows, 2 * rows), 2 * rows), at].astype(F32)
             for part in range(2):
                 rho = two[part * rows : (part + 1) * rows]
-                s = step * 2 + part
-                inner = above_ref[pl.ds(pl.multiple_of(s * rows, rows), rows), at]
-                outer = light_sum[pl.ds(s, 1), at]
-                tint = jnp.exp2(rho * rho * (-8.0 * LOG2E) - light * (inner + outer))
+                here = pl.ds(pl.multiple_of((step * 2 + part) * rows, rows), rows)
+                tint = jnp.exp2(rho * rho * (-8.0 * LOG2E) - light * above_ref[here, at])
                 w0 = clear * (rho * (fade[0] - rho * (fade[1] - rho * fade[2])))
                 clear = clear - w0
                 w1 = behind * (rho * (grow[0] + rho * (grow[1] + rho * grow[2])))
                 behind = behind + w1
-                w0, w1 = w0 * tint, w1 * tint
-                for k in range(3):
-                    e = jnp.exp2(rho * tone[k])
-                    sums[k] = sums[k] + w0 * e
-                    sums[3 + k] = sums[3 + k] + w1 * e
-            return (clear, behind, *sums)
-
-        zero = jnp.zeros(shape, F32)
-        total = total_ref[:, at]
-        start = (jnp.ones(shape, F32), jnp.exp2(total * view_ref[1:2, at] * -LOG2E)) + (zero,) * 6
-        done = lax.fori_loop(0, samples // 2, pair, start, unroll=4)
+                near_ref[here, at] = w0 * tint
+                far_ref[here, at] = w1 * tint
+                for k, color_ref in enumerate((red_ref, green_ref, blue_ref)):
+                    color_ref[here, at] = jnp.exp2(rho * tone[k])
+            return clear, behind
+
+        start = (jnp.ones(shape, F32), jnp.exp2(total_ref[:, at] * view_ref[1:2, at] * -LOG2E))
+        lax.fori_loop(0, samples // 2, pair, start, unroll=4)
+
+
+def post_kernel(
+    samples, rows, width, mine_ref, other_ref, total_ref, light_ref, center_ref,
+    near_ref, far_ref, red_ref, green_ref, blue_ref, out_ref, lit_ref,
+):
+    half = samples // 2
+    odd = lax.axis_index("light") % 2
+    columns = total_ref.shape[1]
+    light = light_ref[...] * -LOG2E
+    lit_ref[pl.ds(pl.multiple_of(half * odd, half), half), :] = jnp.exp2(mine_ref[...] * light)
+    lit_ref[pl.ds(pl.multiple_of(half * (1 - odd), half), half), :] = jnp.exp2(other_ref[...] * light)
+    shape = (rows, width)
+    for first in range(0, columns, width):
+        at = pl.ds(first, width)
+
+        def step(s, sums):
+            here = pl.ds(pl.multiple_of(s * rows, rows), rows)
+            lit = jnp.broadcast_to(lit_ref[pl.ds(s, 1), at], shape)
+            weights = near_ref[here, at] * lit, far_ref[here, at] * lit
+            colors = [ref[here, at] for ref in (red_ref, green_ref, blue_ref)]
+            return tuple(sums[3 * v + k] + weights[v] * colors[k] for v in range(2) for k in range(3))
+
+        done = lax.fori_loop(0, samples, step, (jnp.zeros(shape, F32),) * 6, unroll=8)
         for k in range(3):
             c = jnp.full(shape, center_ref[k], F32)
             scale = 4.0 * jnp.exp2(c * c * (-8.0 * LOG2E))
             for view in range(2):
-                value = done[2 + 3 * view + k] * scale
+                value = done[3 * view + k] * scale
                 for tile in range(width // LANES):
                     out_ref[first // LANES + tile, 3 * view + k] = value[:, tile * LANES : (tile + 1) * LANES]
         for tile in range(width // LANES):
-            out_ref[first // LANES + tile, 6] = total[:, tile * LANES : (tile + 1) * LANES]
-
-
-def brick_colors(rho, mine, other, total, light_rate, view_rate, centers, samples, rows):
-    columns = rho.shape[1]
-    vmem, smem = pl.BlockSpec(memory_space=pltpu.VMEM), pl.BlockSpec(memory_space=pltpu.SMEM)
+            out_ref[first // LANES + tile, 6] = total_ref[:, first + tile * LANES : first + (tile + 1) * LANES]
+
+
+def call(kernel, outs, spaces, scratch, flops, moved, *args, limit=8):
+    specs = {"v": pl.BlockSpec(memory_space=pltpu.VMEM), "s": pl.BlockSpec(memory_space=pltpu.SMEM), "a": pl.BlockSpec(memory_space=pl.ANY)}
+    args = [pltpu.with_memory_space_constraint(a, pltpu.VMEM) if k == "V" else a for a, k in zip(args, spaces, strict=True)]
     return pl.pallas_call(
-        functools.partial(main_kernel, samples, rows, 256),
-        out_shape=jax.ShapeDtypeStruct((columns // LANES, 7, rows, LANES), F32),
-        in_specs=[vmem] * 6 + [smem],
-        out_specs=vmem,
-        scratch_shapes=[
-            pltpu.VMEM((samples * rows, columns), F32),
-            pltpu.VMEM((samples, columns), F32),
-        ],
-    )(rho, mine, other, total, light_rate.reshape(1, -1), view_rate, centers)
+        kernel,
+        out_shape=tuple(pltpu.VMEM(o, t) for o, t in outs) if outs else None,
+        in_specs=[specs[k.lower()] for k in spaces],
+        out_specs=tuple([specs["v"]] * len(outs)),
+        scratch_shapes=scratch,
+        cost_estimate=pl.CostEstimate(flops=flops, bytes_accessed=moved, transcendentals=0),
+        compiler_params=pltpu.CompilerParams(vmem_limit_bytes=limit << 20),
+    )(*args)
 
 
 def composite_kernel(bricks, got_ref, rate_ref, rank_ref, out_ref, order_ref):
@@ -159,7 +175,8 @@
         in_specs=[vmem, vmem, smem],
         out_specs=vmem,
         scratch_shapes=[pltpu.SMEM((2, bricks), jnp.int32)],
-    )(got, rate, rank)
+        compiler_params=pltpu.CompilerParams(vmem_limit_bytes=8 << 20),
+    )(pltpu.with_memory_space_constraint(got, pltpu.VMEM), rate, rank)
 
 
 def swap(x, stride, n):
@@ -189,9 +206,34 @@
 def shards(depth_n, light_n, density, light_rate, view_rate, centers, rank):
     samples, rows, columns = density.shape
     rho = density.reshape(samples * rows, columns)
-    keep, send, total = row_sums(rho, samples, rows)
-    mine, other = lower_halves(keep, send, 1, light_n)
-    packed = brick_colors(rho, mine, other, total, light_rate, view_rate, centers, samples, rows)
+    half = samples // 2
+    light = light_rate.reshape(1, -1)
+    whole, part = (samples * rows, columns), (half, columns)
+    sem = pltpu.SemaphoreType.DMA
+    (send,) = call(
+        functools.partial(send_kernel, half, rows), [(part, F32)], "a",
+        [pltpu.VMEM((half * rows, columns), jnp.bfloat16), sem], 1 << 20, 1 << 19, rho,
+    )
+    keep, total, rho = call(
+        functools.partial(keep_kernel, half, rows), [(part, F32), ((rows, columns), F32), (whole, jnp.bfloat16)], "a",
+        [sem], 1 << 20, 1 << 20, rho,
+    )
+    odd = lax.axis_index("light") % 2 == 1
+    sibling = swap(send, 1, light_n)
+    sums = keep + sibling
+    sums, total = lax.optimization_barrier((sums, total))
+    near, far, red, green, blue = call(
+        functools.partial(pre_kernel, samples, rows, 256), [(whole, F32)] * 5, "VVvvs",
+        [pltpu.VMEM(whole, F32)], 1 << 20, 12 << 20, rho, total, light, view_rate, centers,
+    )
+    below = lower(sums, 2, light_n)
+    other = swap(below + jnp.where(odd, 0.0, keep), 1, light_n)
+    mine = below + jnp.where(odd, sibling, 0.0)
+    (packed,) = call(
+        functools.partial(post_kernel, samples, rows, 256), [((columns // LANES, 7, rows, LANES), F32)], "VVVvsVVVVV",
+        [pltpu.VMEM((samples, columns), F32)], 1 << 20, 10 << 20,
+        mine, other, total, light, centers, near, far, red, green, blue,
+    )
     own = columns // depth_n
     if own % LANES == 0:
         parts = packed.reshape(depth_n, own // LANES, 7, rows, LANES)

time: 43.2 us -> 35.7 us (0.83)
  waiting for transfers between devices: 19.1 us -> 15.9 us
  other arithmetic: 1.67 us -> 0.04 us
  local copies, waits for them, and re-layouts: 2.6 us -> 1.25 us
  Pallas kernels: 9.51 us -> 8.19 us
    ppermute x3, waiting for transfers between devices: 13.8 us -> 9.34 us  [swap(): return lax.ppermute(x, 'light', [(i, i ^ stride) for i in range(n)])]
    add x2, other arithmetic: 1.67 us -> 0.04 us  [the longest x1 0.03 us: shards(): other = swap(below + jnp.where(odd, 0.0, keep), 1, light_n)]
    dynamic_slice x1, local copies, waits for them, and re-layouts: 1.25 us -> 0.01 us  [shards(): lax.dynamic_slice_in_dim(view_rate, lax.axis_index('depth') * own, own, a...]
    all_to_all x1, waiting for transfers between devices: 5.33 us -> 6.58 us  [shards(): lax.all_to_all(parts, 'depth', split_axis=0, concat_axis=0, tiled=True)]
    pallas_call x2 -> x4, Pallas kernels: 7.88 us -> 6.96 us  [call(): pl.pallas_call(kernel, out_shape=tuple((pltpu.VMEM(o, t) for o, t in outs...]
    unnamed x6 -> x10, local copies, waits for them, and re-layouts: 1.34 us -> 1.25 us
  transfers between devices with their start and end apart: 4 -> 4, of which waited for: 4 -> 4; matrix products, arithmetic and copies ran while one was open for 3% -> 0% of each run, Pallas kernels for 0% -> 12%
where the time goes in v2:
time: 35.7 us; the launch traced here: 35.5 us
  waiting for transfers between devices  15.9 us (45%)
  starting transfers between devices  10.1 us (28%)
  Pallas kernels  8.19 us (23%)
  local copies, waits for them, and re-layouts  1.25 us (4%)
    ppermute x3, waiting for transfers between devices, swap(): return lax.ppermute(x, 'light', [(i, i ^ stride) for i in range(n)])  9.34 us
    pallas_call x4, Pallas kernels, call(): pl.pallas_call(kernel, out_shape=tuple((pltpu.VMEM(o, t) for o, t in outs...  6.96 us
    all_to_all x1, waiting for transfers between devices, shards(): lax.all_to_all(parts, 'depth', split_axis=0, concat_axis=0, tiled=True)  6.58 us
    ppermute x3, starting transfers between devices, swap(): return lax.ppermute(x, 'light', [(i, i ^ stride) for i in range(n)])  6.49 us
    all_to_all x1, starting transfers between devices, shards(): lax.all_to_all(parts, 'depth', split_axis=0, concat_axis=0, tiled=True)  3.57 us
    unnamed x10, local copies, waits for them, and re-layouts  1.25 us
    pallas_call x1, Pallas kernels, composite(): pl.pallas_call(functools.partial(composite_kernel, bricks), out_shape=jax...  1.23 us
  transfers between devices with their start and end apart: 4, of which 4 were waited for; matrix products, arithmetic and copies ran while one was open for 0% of the time, Pallas kernels for 12%

profile of v2, /device:TPU:0, one launch (start us, length us, event | category | flops | bytes accessed | tf_op | source)
XLA Modules:
  0.0 35.5 jit_solution(3270347699360009087)
XLA Ops:
  0.0 0.0 copy-start.3
  0.0 0.0 copy-start
  0.0 1.2 %copy-done = bf16[64,8,1024]{2,1,0:T(8,128)(2,1)S(1)} copy-done((bf16[64,8,1024]{2,1,0:T(8,128)(2,1)S(1)}, bf16[64,8,1024]{2,1,0:T(8,128)(2,1)}, u32[]{:S(2)}) %copy-start) | copy-done | bytes 1048600
  1.2 0.0 copy-start.1
  1.2 0.0 copy-start.2
  1.2 0.2 shard_map.56
  1.5 3.1 %collective-permute-start = (f32[32,1024]{1,0:T(8,128)S(1)}, f32[32,1024]{1,0:T(8,128)S(1)}, u32[]{:S(2)}, u32[]{:S(2)}) collective-permute-start(f32[32,1024]{1,0:T(8,128)S(1)} %shard_map.56), channel_id=1, source_target_pairs={{0,1},{1,0},{2,3},{3,2},{4,5},{5,4},{6,7},{7,6},{8,9},{9,8},{10,11... | collective-permute-start | bytes 393224 | tf_op jit(solution)/shard_map/ppermute | solution.py:183
  4.6 0.4 %shard_map.55 = (f32[32,1024]{1,0:T(8,128)S(1)}, f32[8,1024]{1,0:T(8,128)S(1)}, bf16[512,1024]{1,0:T(8,128)(2,1)S(1)}) custom-call(bf16[512,1024]{1,0:T(8,128)(2,1)S(1)} %bitcast.3), custom_call_target="tpu_custom_call" | custom-call | flops 1048576 | bytes 1048576 | tf_op jit(solution)/shard_map/pallas_call | solution.py:128
  5.0 3.1 %collective-permute-done = f32[32,1024]{1,0:T(8,128)S(1)} collective-permute-done((f32[32,1024]{1,0:T(8,128)S(1)}, f32[32,1024]{1,0:T(8,128)S(1)}, u32[]{:S(2)}, u32[]{:S(2)}) %collective-permute-start) | collective-permute-done | bytes 131104 | tf_op jit(solution)/shard_map/ppermute | solution.py:183
  8.1 2.8 %collective-permute-start.1 = (f32[32,1024]{1,0:T(8,128)S(1)}, f32[32,1024]{1,0:T(8,128)S(1)}, u32[]{:S(2)}, u32[]{:S(2)}) collective-permute-start(f32[32,1024]{1,0:T(8,128)S(1)} %add.21), channel_id=1, source_target_pairs={{0,2},{1,3},{2,0},{3,1},{4,6},{5,7},{6,4},{7,5},{8,10},{9,11},{10,... | collective-permute-start | bytes 393224 | tf_op jit(solution)/shard_map/ppermute | solution.py:183
  10.9 5.6 %collective-permute-done.1 = f32[32,1024]{1,0:T(8,128)S(1)} collective-permute-done((f32[32,1024]{1,0:T(8,128)S(1)}, f32[32,1024]{1,0:T(8,128)S(1)}, u32[]{:S(2)}, u32[]{:S(2)}) %collective-permute-start.1) | collective-permute-done | bytes 131104 | tf_op jit(solution)/shard_map/ppermute | solution.py:183
  16.6 0.6 %collective-permute-start.2 = (f32[32,1024]{1,0:T(8,128)S(1)}, f32[32,1024]{1,0:T(8,128)S(1)}, u32[]{:S(2)}, u32[]{:S(2)}) collective-permute-start(f32[32,1024]{1,0:T(8,128)S(1)} %get-tuple-element.25), channel_id=1, source_target_pairs={{0,1},{1,0},{2,3},{3,2},{4,5},{5,4},{6,7},{7,6},{8,9},{9,8},{10,11... | collective-permute-start | bytes 393224 | tf_op jit(solution)/shard_map/ppermute | solution.py:183
  17.2 0.0 copy-done.3
  17.2 0.0 copy-done.1
  17.2 0.0 copy-done.2
  17.2 3.8 %shard_map.57 = (f32[512,1024]{1,0:T(8,128)S(1)}, f32[512,1024]{1,0:T(8,128)S(1)}, f32[512,1024]{1,0:T(8,128)S(1)}, f32[512,1024]{1,0:T(8,128)S(1)}, f32[512,1024]{1,0:T(8,128)S(1)}) custom-call(bf16[512,1024]{1,0:T(8,128)(2,1)S(1)} %get-tuple-element.19.rho_ref, f32[8,1024]{1,0:T(8,128)S(1)} %get-tuple-element.18.total_ref, f32[1,1024]{1,0:T(1,128)S(1)} %bitcast.4, ...), custom_call_target="tpu_custom_call" | custom-call | flops 1048576 | bytes 12582912 | tf_op jit(solution)/shard_map/pallas_call | solution.py:128
  21.0 0.6 %collective-permute-done.2.other_ref = f32[32,1024]{1,0:T(8,128)S(1)} collective-permute-done((f32[32,1024]{1,0:T(8,128)S(1)}, f32[32,1024]{1,0:T(8,128)S(1)}, u32[]{:S(2)}, u32[]{:S(2)}) %collective-permute-start.2) | collective-permute-done | bytes 131104 | tf_op jit(solution)/shard_map/ppermute | solution.py:183
  21.6 0.0 copy-start.4
  21.6 2.5 %shard_map.58 = f32[8,7,8,128]{3,2,1,0:T(8,128)} custom-call(f32[32,1024]{1,0:T(8,128)S(1)} %get-tuple-element.26.mine_ref, f32[32,1024]{1,0:T(8,128)S(1)} %collective-permute-done.2.other_ref, f32[8,1024]{1,0:T(8,128)S(1)} %get-tuple-element.18.total_ref, f32[1,1024]{1,0:T(1,128)S(1)} %bitcast.5, f32[3]{0:T(128)S(1)} %copy-done.3, ...), custom_call_target="tpu_custom_call" | custom-call | flops 1048576 | bytes 10485760 | tf_op jit(solution)/shard_map/pallas_call | solution.py:128
  24.1 3.6 %all-to-all-start = ((f32[8,7,8,128]{3,2,1,0:T(8,128)}), f32[8,7,8,128]{3,2,1,0:T(8,128)S(1)}, u32[]{:S(2)}, u32[]{:S(2)}) async-start(f32[8,7,8,128]{3,2,1,0:T(8,128)} %shard_map.58), calls=%async_computation | async-start | bytes 458752 | tf_op jit(solution)/shard_map/all_to_all | solution.py:244
  27.7 6.6 %all-to-all-done.got_ref = f32[8,7,8,128]{3,2,1,0:T(8,128)S(1)} async-done(((f32[8,7,8,128]{3,2,1,0:T(8,128)}), f32[8,7,8,128]{3,2,1,0:T(8,128)S(1)}, u32[]{:S(2)}, u32[]{:S(2)}) %all-to-all-start) | async-done | bytes 229408 | tf_op jit(solution)/shard_map/all_to_all | solution.py:244
  34.3 0.0 copy-done.4
  34.3 1.2 %shard_map.59 = f32[2,4,8,128]{3,2,1,0:T(8,128)} custom-call(f32[8,7,8,128]{3,2,1,0:T(8,128)S(1)} %all-to-all-done.got_ref, f32[2,128]{1,0:T(2,128)S(1)} %constant_dynamic-slice_fusion.rate_ref, s32[2,8]{1,0:T(2,128)S(1)} %copy-done.4), custom_call_target="tpu_custom_call" | custom-call | tf_op jit(solution)/shard_map/pallas_call | solution.py:172
  (3 shorter events, 0.0 us)
Async XLA Ops:
  0.0 17.2 %copy-start.3 = (f32[3]{0:T(128)S(1)}, f32[3]{0:T(128)}, u32[]{:S(2)}) copy-start(f32[3]{0:T(128)} %center_ref.3) | copy-start | bytes 40
  0.0 1.2 %copy-start = (bf16[64,8,1024]{2,1,0:T(8,128)(2,1)S(1)}, bf16[64,8,1024]{2,1,0:T(8,128)(2,1)}, u32[]{:S(2)}) copy-start(bf16[64,8,1024]{2,1,0:T(8,128)(2,1)} %param.5) | copy-start | bytes 3145732
  1.2 15.9 %copy-start.1 = (f32[1024]{0:T(1024)S(1)}, f32[1024]{0:T(1024)}, u32[]{:S(2)}) copy-start(f32[1024]{0:T(1024)} %param.6) | copy-start | bytes 12292
  1.2 15.9 %copy-start.2 = (f32[2,1024]{1,0:T(2,128)S(1)}, f32[2,1024]{1,0:T(2,128)}, u32[]{:S(2)}) copy-start(f32[2,1024]{1,0:T(2,128)} %view_ref.1) | copy-start | bytes 24580
  1.5 6.6 %collective-permute-start = (f32[32,1024]{1,0:T(8,128)S(1)}, f32[32,1024]{1,0:T(8,128)S(1)}, u32[]{:S(2)}, u32[]{:S(2)}) collective-permute-start(f32[32,1024]{1,0:T(8,128)S(1)} %shard_map.56), channel_id=1, source_target_pairs={{0,1},{1,0},{2,3},{3,2},{4,5},{5,4},{6,7},{7,6},{8,9},{9,8},{10,11... | collective-permute-start | bytes 393224 | tf_op jit(solution)/shard_map/ppermute | solution.py:183
  8.1 8.5 %collective-permute-start.1 = (f32[32,1024]{1,0:T(8,128)S(1)}, f32[32,1024]{1,0:T(8,128)S(1)}, u32[]{:S(2)}, u32[]{:S(2)}) collective-permute-start(f32[32,1024]{1,0:T(8,128)S(1)} %add.21), channel_id=1, source_target_pairs={{0,2},{1,3},{2,0},{3,1},{4,6},{5,7},{6,4},{7,5},{8,10},{9,11},{10,... | collective-permute-start | bytes 393224 | tf_op jit(solution)/shard_map/ppermute | solution.py:183
  16.6 5.0 %collective-permute-start.2 = (f32[32,1024]{1,0:T(8,128)S(1)}, f32[32,1024]{1,0:T(8,128)S(1)}, u32[]{:S(2)}, u32[]{:S(2)}) collective-permute-start(f32[32,1024]{1,0:T(8,128)S(1)} %get-tuple-element.25), channel_id=1, source_target_pairs={{0,1},{1,0},{2,3},{3,2},{4,5},{5,4},{6,7},{7,6},{8,9},{9,8},{10,11... | collective-permute-start | bytes 393224 | tf_op jit(solution)/shard_map/ppermute | solution.py:183
  21.6 12.7 %copy-start.4 = (s32[2,8]{1,0:T(2,128)S(1)}, s32[2,8]{1,0:T(2,128)}, u32[]{:S(2)}) copy-start(s32[2,8]{1,0:T(2,128)} %rank_ref.1) | copy-start | bytes 196
  24.1 10.2 %all-to-all-start = ((f32[8,7,8,128]{3,2,1,0:T(8,128)}), f32[8,7,8,128]{3,2,1,0:T(8,128)S(1)}, u32[]{:S(2)}, u32[]{:S(2)}) async-start(f32[8,7,8,128]{3,2,1,0:T(8,128)} %shard_map.58), calls=%async_computation | async-start | bytes 458752 | tf_op jit(solution)/shard_map/all_to_all | solution.py:244

commit v3 on v2

--- a/solution.py
+++ b/solution.py
@@ -86,48 +86,53 @@
             return clear, behind
 
         start = (jnp.ones(shape, F32), jnp.exp2(total_ref[:, at] * view_ref[1:2, at] * -LOG2E))
-        lax.fori_loop(0, samples // 2, pair, start, unroll=4)
+        lax.fori_loop(0, samples // 2, pair, start, unroll=True)
 
 
 def post_kernel(
-    samples, rows, width, mine_ref, other_ref, total_ref, light_ref, center_ref,
-    near_ref, far_ref, red_ref, green_ref, blue_ref, out_ref, lit_ref,
+    rows, second, sliced, place_ref, below_ref, *refs
 ):
-    half = samples // 2
+    early_ref = refs[0] if second else None
+    light_ref, center_ref, near_ref, far_ref, red_ref, green_ref, blue_ref, rest_ref, out_ref, lit_ref = refs[second:]
+    half, columns = below_ref.shape
     odd = lax.axis_index("light") % 2
-    columns = total_ref.shape[1]
-    light = light_ref[...] * -LOG2E
-    lit_ref[pl.ds(pl.multiple_of(half * odd, half), half), :] = jnp.exp2(mine_ref[...] * light)
-    lit_ref[pl.ds(pl.multiple_of(half * (1 - odd), half), half), :] = jnp.exp2(other_ref[...] * light)
+    base = (1 - odd if second else odd) * half
+    chip, core = (place_ref[0] // 2, place_ref[0] % 2) if sliced else (0, 0)
+    below = below_ref[...]
+    if second:
+        below = below + jnp.where(odd == 1, early_ref[...], 0.0)
+    lit_ref[...] = jnp.exp2(below * (light_ref[...] * -LOG2E))
+    width = 2 * LANES
     shape = (rows, width)
-    for first in range(0, columns, width):
-        at = pl.ds(first, width)
-
-        def step(s, sums):
-            here = pl.ds(pl.multiple_of(s * rows, rows), rows)
-            lit = jnp.broadcast_to(lit_ref[pl.ds(s, 1), at], shape)
-            weights = near_ref[here, at] * lit, far_ref[here, at] * lit
-            colors = [ref[here, at] for ref in (red_ref, green_ref, blue_ref)]
-            return tuple(sums[3 * v + k] + weights[v] * colors[k] for v in range(2) for k in range(3))
-
-        done = lax.fori_loop(0, samples, step, (jnp.zeros(shape, F32),) * 6, unroll=8)
-        for k in range(3):
-            c = jnp.full(shape, center_ref[k], F32)
-            scale = 4.0 * jnp.exp2(c * c * (-8.0 * LOG2E))
-            for view in range(2):
-                value = done[3 * view + k] * scale
-                for tile in range(width // LANES):
-                    out_ref[first // LANES + tile, 3 * view + k] = value[:, tile * LANES : (tile + 1) * LANES]
-        for tile in range(width // LANES):
-            out_ref[first // LANES + tile, 6] = total_ref[:, first + tile * LANES : first + (tile + 1) * LANES]
+    scales = [4.0 * jnp.exp2(jnp.full((rows, LANES), center_ref[k], F32) ** 2 * (-8.0 * LOG2E)) for k in range(3)]
+    for slot in range(columns // width):
+        at = pl.ds(pl.multiple_of((slot ^ chip) * width, width), width)
+        sums = [jnp.zeros(shape, F32)] * 6
+        for group in range(half // 8):
+            lit = lit_ref[group * 8 : group * 8 + 8, at]
+            for part in range(8):
+                here = pl.ds(pl.multiple_of((base + group * 8 + part) * rows, rows), rows)
+                shade = jnp.broadcast_to(lit[part : part + 1], shape)
+                weights = near_ref[here, at] * shade, far_ref[here, at] * shade
+                colors = [ref[here, at] for ref in (red_ref, green_ref, blue_ref)]
+                sums = [sums[3 * v + k] + weights[v] * colors[k] for v in range(2) for k in range(3)]
+        for tile in range(2):
+            lanes = slice(tile * LANES, (tile + 1) * LANES)
+            for n in range(6):
+                value = sums[n][:, lanes] * scales[n % 3]
+                if second:
+                    value = value + rest_ref[tile ^ core, slot, n]
+                out_ref[tile ^ core, slot, n] = value
+            out_ref[tile ^ core, slot, 6] = rest_ref[tile ^ core, slot, 6] if second else rest_ref[:, at][:, lanes]
 
 
 def call(kernel, outs, spaces, scratch, flops, moved, *args, limit=8):
     specs = {"v": pl.BlockSpec(memory_space=pltpu.VMEM), "s": pl.BlockSpec(memory_space=pltpu.SMEM), "a": pl.BlockSpec(memory_space=pl.ANY)}
-    args = [pltpu.with_memory_space_constraint(a, pltpu.VMEM) if k == "V" else a for a, k in zip(args, spaces, strict=True)]
+    forced = {"V": pltpu.VMEM, "A": pltpu.HBM, "S": pltpu.SMEM}
+    args = [pltpu.with_memory_space_constraint(a, forced[k]) if k in forced else a for a, k in zip(args, spaces, strict=True)]
     return pl.pallas_call(
         kernel,
-        out_shape=tuple(pltpu.VMEM(o, t) for o, t in outs) if outs else None,
+        out_shape=tuple(pltpu.VMEM(o, t) for o, t in outs),
         in_specs=[specs[k.lower()] for k in spaces],
         out_specs=tuple([specs["v"]] * len(outs)),
         scratch_shapes=scratch,
@@ -159,11 +164,7 @@
         depth, *colors = lax.fori_loop(0, bricks, nearer, (zero,) * 4, unroll=bricks <= 8)
         for k in range(3):
             out_ref[view, k] = colors[k]
-        depth = depth * rate
-        small = jnp.full(shape, 1.0, F32)
-        for n in range(8, 1, -1):
-            small = 1.0 - depth * (1.0 / n) * small
-        out_ref[view, 3] = jnp.where(depth < 0.35, depth * small, 1.0 - jnp.exp2(depth * -LOG2E))
+        out_ref[view, 3] = opacity(depth * rate)
 
 
 def composite(got, rate, rank):
@@ -179,16 +180,58 @@
     )(pltpu.with_memory_space_constraint(got, pltpu.VMEM), rate, rank)
 
 
-def swap(x, stride, n):
-    return lax.ppermute(x, "light", [(i, i ^ stride) for i in range(n)])
-
-
-def lower_halves(keep, send, stride, n):
+def opacity(depth):
+    small = jnp.full(depth.shape, 1.0, F32)
+    for n in range(8, 1, -1):
+        small = 1.0 - depth * (1.0 / n) * small
+    return jnp.where(depth < 0.35, depth * small, 1.0 - jnp.exp2(depth * -LOG2E))
+
+
+def slots_kernel(place_ref, rank_ref, rate_ref, own_ref, sibling_ref, *refs):
+    *chip_refs, out_ref = refs
+    shape = out_ref.shape[2:]
+    blocks = [own_ref.at[0, 0], sibling_ref.at[0]] + [ref.at[t] for ref in chip_refs for t in range(2)]
+    depths = [block[6] for block in blocks]
+    for view in range(2):
+        rate = jnp.broadcast_to(rate_ref[view : view + 1, :], shape)
+        ranks = [rank_ref[view, place_ref[0] ^ slot] for slot in range(len(blocks))]
+        colors = [jnp.zeros(shape, F32)] * 3
+        for i, block in enumerate(blocks):
+            front = jnp.zeros(shape, F32)
+            for j, depth in enumerate(depths):
+                if j != i:
+                    front = front + depth * (ranks[j] < ranks[i]).astype(F32)
+            seen = jnp.exp2(front * rate * -LOG2E)
+            colors = [colors[k] + block[3 * view + k] * seen for k in range(3)]
+        for k in range(3):
+            out_ref[view, k] = colors[k]
+        out_ref[view, 3] = opacity(sum(depths) * rate)
+
+
+def composite_slots(place, rank, rate, own, sibling, chips):
+    vmem, smem = pl.BlockSpec(memory_space=pltpu.VMEM), pl.BlockSpec(memory_space=pltpu.SMEM)
+    blocks = [pltpu.with_memory_space_constraint(x, pltpu.VMEM) for x in (own, sibling, *chips)]
+    _, rows, columns = own.shape[2:]
+    return pl.pallas_call(
+        slots_kernel,
+        out_shape=jax.ShapeDtypeStruct((2, 4, rows, columns), F32),
+        in_specs=[smem, smem, vmem] + [vmem] * len(blocks),
+        out_specs=vmem,
+        compiler_params=pltpu.CompilerParams(vmem_limit_bytes=8 << 20),
+    )(*(pltpu.with_memory_space_constraint(x, pltpu.SMEM) for x in (place, rank)), pltpu.with_memory_space_constraint(rate, pltpu.VMEM), *blocks)
+
+
+def swap(x, stride, n, first=0, last=None):
+    return lax.ppermute(x, "light", [(i, i ^ stride) for i in range(first, n if last is None else last)])
+
+
+def halves_below(keep, sibling, sums, stride, n):
     odd = (lax.axis_index("light") // stride) % 2 == 1
-    sibling = swap(send, stride, n)
-    below = lower(keep + sibling, 2 * stride, n)
-    other = swap(below + jnp.where(odd, 0.0, keep), stride, n)
-    return below + jnp.where(odd, sibling, 0.0), other
+    below = lower(sums, 2 * stride, n)
+    first = swap(keep, stride, n, 0, 2 * stride)
+    mine = below + jnp.where(odd, sibling, 0.0)
+    other = swap(below + jnp.where(odd, 0.0, keep), stride, n, 2 * stride)
+    return mine, other, first
 
 
 def lower(x, stride, n):
@@ -199,7 +242,9 @@
         return jnp.where(odd, swap(x, stride, n), 0.0)
     half = x.shape[0] // 2
     first, last = x[:half], x[half:]
-    mine, other = lower_halves(jnp.where(odd, last, first), jnp.where(odd, first, last), stride, n)
+    keep, sibling = jnp.where(odd, last, first), swap(jnp.where(odd, first, last), stride, n)
+    mine, other, early = halves_below(keep, sibling, keep + sibling, stride, n)
+    other = other + jnp.where(odd, early, 0.0)
     return jnp.where(odd, jnp.concatenate([other, mine]), jnp.concatenate([mine, other]))
 
 
@@ -211,38 +256,45 @@
     whole, part = (samples * rows, columns), (half, columns)
     sem = pltpu.SemaphoreType.DMA
     (send,) = call(
-        functools.partial(send_kernel, half, rows), [(part, F32)], "a",
+        functools.partial(send_kernel, half, rows), [(part, F32)], "A",
         [pltpu.VMEM((half * rows, columns), jnp.bfloat16), sem], 1 << 20, 1 << 19, rho,
     )
     keep, total, rho = call(
-        functools.partial(keep_kernel, half, rows), [(part, F32), ((rows, columns), F32), (whole, jnp.bfloat16)], "a",
+        functools.partial(keep_kernel, half, rows), [(part, F32), ((rows, columns), F32), (whole, jnp.bfloat16)], "A",
         [sem], 1 << 20, 1 << 20, rho,
     )
-    odd = lax.axis_index("light") % 2 == 1
     sibling = swap(send, 1, light_n)
     sums = keep + sibling
-    sums, total = lax.optimization_barrier((sums, total))
     near, far, red, green, blue = call(
-        functools.partial(pre_kernel, samples, rows, 256), [(whole, F32)] * 5, "VVvvs",
+        functools.partial(pre_kernel, samples, rows, 256), [(whole, F32)] * 5, "VVVVS",
         [pltpu.VMEM(whole, F32)], 1 << 20, 12 << 20, rho, total, light, view_rate, centers,
     )
-    below = lower(sums, 2, light_n)
-    other = swap(below + jnp.where(odd, 0.0, keep), 1, light_n)
-    mine = below + jnp.where(odd, sibling, 0.0)
-    (packed,) = call(
-        functools.partial(post_kernel, samples, rows, 256), [((columns // LANES, 7, rows, LANES), F32)], "VVVvsVVVVV",
-        [pltpu.VMEM((samples, columns), F32)], 1 << 20, 10 << 20,
-        mine, other, total, light, centers, near, far, red, green, blue,
-    )
+    mine, other, early = halves_below(keep, sibling, sums, 1, light_n)
     own = columns // depth_n
+    place = lax.axis_index("depth")
+    rate = lax.dynamic_slice_in_dim(view_rate, place * own, own, axis=1)
+    place = place.reshape(1)
+    sliced = own == LANES and depth_n <= 8 and depth_n & (depth_n - 1) == 0
+    packed = total
+    for second, below in enumerate(([mine], [other, early])):
+        (packed,) = call(
+            functools.partial(post_kernel, rows, second, sliced), [((2, columns // (2 * LANES), 7, rows, LANES), F32)], "S" + "V" * len(below) + "VSVVVVVV",
+            [pltpu.VMEM(part, F32)], 1 << 10, 1 << 10,
+            place, *below, light, centers, near, far, red, green, blue, packed,
+        )
+    if sliced:
+        def send_to(x, stride):
+            return lax.ppermute(x, "depth", [(i, i ^ stride) for i in range(depth_n)])
+
+        got = send_to(packed[1], 1)
+        chips = [send_to(jnp.stack([packed[0, chip], got[chip]]), 2 * chip) for chip in range(1, depth_n // 2)]
+        return composite_slots(place, rank, rate, packed, got, chips)
+    parts = packed.transpose(1, 0, 2, 3, 4).reshape(columns // LANES, 7, rows, LANES)
     if own % LANES == 0:
-        parts = packed.reshape(depth_n, own // LANES, 7, rows, LANES)
-        parts = parts[:, 0] if own == LANES else parts.transpose(0, 2, 3, 1, 4).reshape(depth_n, 7, rows, own)
+        parts = parts.reshape(depth_n, own // LANES, 7, rows, LANES).transpose(0, 2, 3, 1, 4)
     else:
-        parts = packed.reshape(columns // LANES, 7, rows, LANES // own, own)
-        parts = parts.transpose(0, 3, 1, 2, 4).reshape(depth_n, 7, rows, own)
-    got = lax.all_to_all(parts, "depth", split_axis=0, concat_axis=0, tiled=True)
-    rate = lax.dynamic_slice_in_dim(view_rate, lax.axis_index("depth") * own, own, axis=1)
+        parts = parts.reshape(columns // LANES, 7, rows, LANES // own, own).transpose(0, 3, 1, 2, 4)
+    got = lax.all_to_all(parts.reshape(depth_n, 7, rows, own), "depth", split_axis=0, concat_axis=0, tiled=True)
     return composite(got, rate, rank)
 
 

time: 35.7 us -> 33.2 us (0.930)
  the two profiles are of different devices: /device:TPU:0 before, /device:TPU:20 now
where the time goes in v3:
time: 33.2 us; the launch traced here: 33 us
  waiting for transfers between devices  12.1 us (36%)
  starting transfers between devices  11.6 us (35%)
  Pallas kernels  8.98 us (27%)
    ppermute x4, starting transfers between devices, swap(): lax.ppermute(x, 'light', [(i, i ^ stride) for i in range(first, n if last...  7.97 us
    pallas_call x5, Pallas kernels, call(): pl.pallas_call(kernel, out_shape=tuple((pltpu.VMEM(o, t) for o, t in outs...  7.65 us
    ppermute x4, waiting for transfers between devices, swap(): lax.ppermute(x, 'light', [(i, i ^ stride) for i in range(first, n if last...  7.21 us
    ppermute x4, waiting for transfers between devices, send_to(): return lax.ppermute(x, 'depth', [(i, i ^ stride) for i in range(depth_n)])  4.93 us
    ppermute x4, starting transfers between devices, send_to(): return lax.ppermute(x, 'depth', [(i, i ^ stride) for i in range(depth_n)])  3.62 us
    pallas_call x1, Pallas kernels, composite_slots(): pl.pallas_call(slots_kernel, out_shape=jax.ShapeDtypeStruct((2, 4, rows,...  1.33 us
  transfers between devices with their start and end apart: 8, of which 6 were waited for; matrix products, arithmetic and copies ran while one was open for 0% of the time, Pallas kernels for 16%

profile of v3, /device:TPU:20, one launch (start us, length us, event | category | flops | bytes accessed | tf_op | source)
XLA Modules:
  0.0 33.0 jit_solution(6360843387519375020)
XLA Ops:
  0.0 0.0 copy-start
  0.0 0.0 copy-start.1
  0.0 0.0 copy-start.2
  0.0 1.3 %shard_map.56 = f32[32,1024]{1,0:T(8,128)S(1)} custom-call(bf16[512,1024]{1,0:T(8,128)(2,1)} %bitcast.14), custom_call_target="tpu_custom_call" | custom-call | flops 1048576 | bytes 524288 | tf_op jit(solution)/shard_map/pallas_call | solution.py:133
  1.3 1.6 %collective-permute-start = (f32[32,1024]{1,0:T(8,128)S(1)}, f32[32,1024]{1,0:T(8,128)S(1)}, u32[]{:S(2)}, u32[]{:S(2)}) collective-permute-start(f32[32,1024]{1,0:T(8,128)S(1)} %shard_map.56), channel_id=1, source_target_pairs={{0,1},{1,0},{2,3},{3,2},{4,5},{5,4},{6,7},{7,6},{8,9},{9,8},{10,11... | collective-permute-start | bytes 393224 | tf_op jit(solution)/shard_map/ppermute | solution.py:225
  2.9 1.6 %shard_map.55 = (f32[32,1024]{1,0:T(8,128)S(1)}, f32[8,1024]{1,0:T(8,128)S(1)}, bf16[512,1024]{1,0:T(8,128)(2,1)S(1)}) custom-call(bf16[512,1024]{1,0:T(8,128)(2,1)} %bitcast.15), custom_call_target="tpu_custom_call" | custom-call | flops 1048576 | bytes 1048576 | tf_op jit(solution)/shard_map/pallas_call | solution.py:133
  4.5 2.1 %collective-permute-done = f32[32,1024]{1,0:T(8,128)S(1)} collective-permute-done((f32[32,1024]{1,0:T(8,128)S(1)}, f32[32,1024]{1,0:T(8,128)S(1)}, u32[]{:S(2)}, u32[]{:S(2)}) %collective-permute-start) | collective-permute-done | bytes 131104 | tf_op jit(solution)/shard_map/ppermute | solution.py:225
  6.6 0.4 %collective-permute-start.1 = (f32[32,1024]{1,0:T(8,128)S(1)}, f32[32,1024]{1,0:T(8,128)S(1)}, u32[]{:S(2)}, u32[]{:S(2)}) collective-permute-start(f32[32,1024]{1,0:T(8,128)S(1)} %add.23), channel_id=1, source_target_pairs={{0,2},{1,3},{2,0},{3,1},{4,6},{5,7},{6,4},{7,5},{8,10},{9,11},{10,... | collective-permute-start | bytes 393224 | tf_op jit(solution)/shard_map/ppermute | solution.py:225
  7.0 0.7 %collective-permute-start.3 = (f32[32,1024]{1,0:T(8,128)S(1)}, f32[32,1024]{1,0:T(8,128)S(1)}, u32[]{:S(2)}, u32[]{:S(2)}) collective-permute-start(f32[32,1024]{1,0:T(8,128)S(1)} %get-tuple-element.13), channel_id=1, source_target_pairs={{0,1},{1,0},{4,5},{5,4},{8,9},{9,8},{12,13},{13,12},{16,17},{17,16... | collective-permute-start | bytes 393224 | tf_op jit(solution)/shard_map/ppermute | solution.py:225
  7.7 5.1 %collective-permute-done.1 = f32[32,1024]{1,0:T(8,128)S(1)} collective-permute-done((f32[32,1024]{1,0:T(8,128)S(1)}, f32[32,1024]{1,0:T(8,128)S(1)}, u32[]{:S(2)}, u32[]{:S(2)}) %collective-permute-start.1) | collective-permute-done | bytes 131104 | tf_op jit(solution)/shard_map/ppermute | solution.py:225
  12.9 5.3 %collective-permute-start.2 = (f32[32,1024]{1,0:T(8,128)S(1)}, f32[32,1024]{1,0:T(8,128)S(1)}, u32[]{:S(2)}, u32[]{:S(2)}) collective-permute-start(f32[32,1024]{1,0:T(8,128)S(1)} %get-tuple-element.25), channel_id=1, source_target_pairs={{2,3},{3,2},{6,7},{7,6},{10,11},{11,10},{14,15},{15,14},{18,19},{1... | collective-permute-start | bytes 393224 | tf_op jit(solution)/shard_map/ppermute | solution.py:225
  18.2 0.0 copy-done
  18.2 0.0 copy-done.1
  18.2 0.0 copy-done.2
  18.2 2.7 %shard_map.57 = (f32[512,1024]{1,0:T(8,128)S(1)}, f32[512,1024]{1,0:T(8,128)S(1)}, f32[512,1024]{1,0:T(8,128)S(1)}, f32[512,1024]{1,0:T(8,128)S(1)}, f32[512,1024]{1,0:T(8,128)S(1)}) custom-call(bf16[512,1024]{1,0:T(8,128)(2,1)S(1)} %get-tuple-element.14.rho_ref, f32[8,1024]{1,0:T(8,128)S(1)} %get-tuple-element.15.total_ref.refs_7_, f32[1,1024]{1,0:T(1,128)S(1)} %bitcast.11, ...), custom_call_target="tpu_custom_call" | custom-call | flops 1048576 | bytes 12582912 | tf_op jit(solution)/shard_map/pallas_call | solution.py:133
  20.9 1.0 %shard_map.58.refs_8_ = f32[2,4,7,8,128]{4,3,2,1,0:T(8,128)S(1)} custom-call(s32[1]{0:T(128)} %bitcast.place_ref, f32[32,1024]{1,0:T(8,128)S(1)} %get-tuple-element.24.below_ref, f32[1,1024]{1,0:T(1,128)S(1)} %bitcast.12, f32[3]{0:T(128)S(1)} %copy-done.2, f32[512,1024]{1,0:T(8,128)S(1)} %get-tuple-element.16.refs_2_.refs_3_, ...), custom_call_target="tpu_custom_call" | custom-call | flops 1024 | bytes 1024 | tf_op jit(solution)/shard_map/pallas_call | solution.py:133
  21.9 0.0 copy-start.3
  22.0 0.0 collective-permute-done.3.refs_0_
  22.0 0.0 collective-permute-done.2.below_ref
  22.0 1.1 %shard_map.59.own_ref = f32[2,4,7,8,128]{4,3,2,1,0:T(8,128)S(1)} custom-call(s32[1]{0:T(128)} %bitcast.place_ref, f32[32,1024]{1,0:T(8,128)S(1)} %collective-permute-done.2.below_ref, f32[32,1024]{1,0:T(8,128)S(1)} %collective-permute-done.3.refs_0_, f32[1,1024]{1,0:T(1,128)S(1)} %bitcast.13, f32[3]{0:T(128)S(1)} %copy-done.2, ...), custom_call_target="tpu_custom_call" | custom-call | flops 1024 | bytes 1024 | tf_op jit(solution)/shard_map/pallas_call | solution.py:133
  23.1 0.1 collective-permute-start.4
  23.2 1.3 %collective-permute-done.4.sibling_ref = f32[4,7,8,128]{3,2,1,0:T(8,128)S(1)} collective-permute-done((f32[4,7,8,128]{3,2,1,0:T(8,128)S(1)}, f32[4,7,8,128]{3,2,1,0:T(8,128)S(1)}, u32[]{:S(2)}, u32[]{:S(2)}) %collective-permute-start.4) | collective-permute-done | bytes 114720 | tf_op jit(solution)/shard_map/ppermute | solution.py:287
  24.5 1.5 %collective-permute-start.7 = (f32[2,7,8,128]{3,2,1,0:T(8,128)S(1)}, f32[2,7,8,128]{3,2,1,0:T(8,128)S(1)}, u32[]{:S(2)}, u32[]{:S(2)}) collective-permute-start(f32[2,7,8,128]{3,2,1,0:T(8,128)S(1)} %pad_maximum_fusion.2), channel_id=1, source_target_pairs={{0,24},{4,28},{8,16},{12,20},{16,8},{20,12},{24,0},{28,4},{1,25},{... | collective-permute-start | bytes 172040 | tf_op jit(solution)/shard_map/ppermute | solution.py:287
  26.0 1.5 %collective-permute-start.6 = (f32[2,7,8,128]{3,2,1,0:T(8,128)S(1)}, f32[2,7,8,128]{3,2,1,0:T(8,128)S(1)}, u32[]{:S(2)}, u32[]{:S(2)}) collective-permute-start(f32[2,7,8,128]{3,2,1,0:T(8,128)S(1)} %pad_maximum_fusion.1), channel_id=1, source_target_pairs={{0,16},{4,20},{8,24},{12,28},{16,0},{20,4},{24,8},{28,12},{1,17},{... | collective-permute-start | bytes 172040 | tf_op jit(solution)/shard_map/ppermute | solution.py:287
  27.5 0.5 %collective-permute-start.5 = (f32[2,7,8,128]{3,2,1,0:T(8,128)S(1)}, f32[2,7,8,128]{3,2,1,0:T(8,128)S(1)}, u32[]{:S(2)}, u32[]{:S(2)}) collective-permute-start(f32[2,7,8,128]{3,2,1,0:T(8,128)S(1)} %pad_maximum_fusion), channel_id=1, source_target_pairs={{0,8},{4,12},{8,0},{12,4},{16,24},{20,28},{24,16},{28,20},{1,9},{5... | collective-permute-start | bytes 172040 | tf_op jit(solution)/shard_map/ppermute | solution.py:287
  28.0 1.6 %collective-permute-done.7.refs_2_ = f32[2,7,8,128]{3,2,1,0:T(8,128)S(1)} collective-permute-done((f32[2,7,8,128]{3,2,1,0:T(8,128)S(1)}, f32[2,7,8,128]{3,2,1,0:T(8,128)S(1)}, u32[]{:S(2)}, u32[]{:S(2)}) %collective-permute-start.7) | collective-permute-done | bytes 57376 | tf_op jit(solution)/shard_map/ppermute | solution.py:287
  29.7 1.0 %collective-permute-done.6.refs_1_ = f32[2,7,8,128]{3,2,1,0:T(8,128)S(1)} collective-permute-done((f32[2,7,8,128]{3,2,1,0:T(8,128)S(1)}, f32[2,7,8,128]{3,2,1,0:T(8,128)S(1)}, u32[]{:S(2)}, u32[]{:S(2)}) %collective-permute-start.6) | collective-permute-done | bytes 57376 | tf_op jit(solution)/shard_map/ppermute | solution.py:287
  30.6 1.0 %collective-permute-done.5.refs_0_ = f32[2,7,8,128]{3,2,1,0:T(8,128)S(1)} collective-permute-done((f32[2,7,8,128]{3,2,1,0:T(8,128)S(1)}, f32[2,7,8,128]{3,2,1,0:T(8,128)S(1)}, u32[]{:S(2)}, u32[]{:S(2)}) %collective-permute-start.5) | collective-permute-done | bytes 57376 | tf_op jit(solution)/shard_map/ppermute | solution.py:287
  31.7 0.0 copy-done.3
  31.7 1.3 %shard_map.60 = f32[2,4,8,128]{3,2,1,0:T(8,128)} custom-call(s32[1]{0:T(128)} %bitcast.place_ref, s32[2,8]{1,0:T(2,128)S(1)} %copy-done.3, f32[2,128]{1,0:T(2,128)S(1)} %constant_dynamic-slice_fusion.rate_ref, f32[2,4,7,8,128]{4,3,2,1,0:T(8,128)S(1)} %shard_map.59.own_ref, f32[4,7,8,128]{3,2,1,0:T(8,128)S(1)} %collective-permute-done.4.sibling_ref, ...), custom_call_target="tpu_custom_call" | custom-call | tf_op jit(solution)/shard_map/pallas_call | solution.py:215
  (9 shorter events, 0.1 us)
Async XLA Ops:
  0.0 18.2 %copy-start = (f32[1024]{0:T(1024)S(1)}, f32[1024]{0:T(1024)}, u32[]{:S(2)}) copy-start(f32[1024]{0:T(1024)} %param.6) | copy-start | bytes 12292
  0.0 18.2 %copy-start.1 = (f32[2,1024]{1,0:T(2,128)S(1)}, f32[2,1024]{1,0:T(2,128)}, u32[]{:S(2)}) copy-start(f32[2,1024]{1,0:T(2,128)} %view_ref.1) | copy-start | bytes 24580
  0.0 18.2 %copy-start.2 = (f32[3]{0:T(128)S(1)}, f32[3]{0:T(128)}, u32[]{:S(2)}) copy-start(f32[3]{0:T(128)} %refs_2_.1) | copy-start | bytes 40
  1.3 5.3 %collective-permute-start = (f32[32,1024]{1,0:T(8,128)S(1)}, f32[32,1024]{1,0:T(8,128)S(1)}, u32[]{:S(2)}, u32[]{:S(2)}) collective-permute-start(f32[32,1024]{1,0:T(8,128)S(1)} %shard_map.56), channel_id=1, source_target_pairs={{0,1},{1,0},{2,3},{3,2},{4,5},{5,4},{6,7},{7,6},{8,9},{9,8},{10,11... | collective-permute-start | bytes 393224 | tf_op jit(solution)/shard_map/ppermute | solution.py:225
  6.6 6.2 %collective-permute-start.1 = (f32[32,1024]{1,0:T(8,128)S(1)}, f32[32,1024]{1,0:T(8,128)S(1)}, u32[]{:S(2)}, u32[]{:S(2)}) collective-permute-start(f32[32,1024]{1,0:T(8,128)S(1)} %add.23), channel_id=1, source_target_pairs={{0,2},{1,3},{2,0},{3,1},{4,6},{5,7},{6,4},{7,5},{8,10},{9,11},{10,... | collective-permute-start | bytes 393224 | tf_op jit(solution)/shard_map/ppermute | solution.py:225
  7.0 14.9 %collective-permute-start.3 = (f32[32,1024]{1,0:T(8,128)S(1)}, f32[32,1024]{1,0:T(8,128)S(1)}, u32[]{:S(2)}, u32[]{:S(2)}) collective-permute-start(f32[32,1024]{1,0:T(8,128)S(1)} %get-tuple-element.13), channel_id=1, source_target_pairs={{0,1},{1,0},{4,5},{5,4},{8,9},{9,8},{12,13},{13,12},{16,17},{17,16... | collective-permute-start | bytes 393224 | tf_op jit(solution)/shard_map/ppermute | solution.py:225
  12.9 9.1 %collective-permute-start.2 = (f32[32,1024]{1,0:T(8,128)S(1)}, f32[32,1024]{1,0:T(8,128)S(1)}, u32[]{:S(2)}, u32[]{:S(2)}) collective-permute-start(f32[32,1024]{1,0:T(8,128)S(1)} %get-tuple-element.25), channel_id=1, source_target_pairs={{2,3},{3,2},{6,7},{7,6},{10,11},{11,10},{14,15},{15,14},{18,19},{1... | collective-permute-start | bytes 393224 | tf_op jit(solution)/shard_map/ppermute | solution.py:225
  21.9 9.7 %copy-start.3 = (s32[2,8]{1,0:T(2,128)S(1)}, s32[2,8]{1,0:T(2,128)}, u32[]{:S(2)}) copy-start(s32[2,8]{1,0:T(2,128)} %rank_ref.1) | copy-start | bytes 196
  23.1 1.4 %collective-permute-start.4 = (f32[4,7,8,128]{3,2,1,0:T(8,128)S(1)}, f32[4,7,8,128]{3,2,1,0:T(8,128)S(1)}, u32[]{:S(2)}, u32[]{:S(2)}) collective-permute-start(f32[4,7,8,128]{3,2,1,0:T(8,128)S(1)} %slice_bitcast_fusion), channel_id=1, source_target_pairs={{0,4},{4,0},{8,12},{12,8},{16,20},{20,16},{24,28},{28,24},{1,5},{5... | collective-permute-start | bytes 344072 | tf_op jit(solution)/shard_map/ppermute | solution.py:287
  24.5 5.2 %collective-permute-start.7 = (f32[2,7,8,128]{3,2,1,0:T(8,128)S(1)}, f32[2,7,8,128]{3,2,1,0:T(8,128)S(1)}, u32[]{:S(2)}, u32[]{:S(2)}) collective-permute-start(f32[2,7,8,128]{3,2,1,0:T(8,128)S(1)} %pad_maximum_fusion.2), channel_id=1, source_target_pairs={{0,24},{4,28},{8,16},{12,20},{16,8},{20,12},{24,0},{28,4},{1,25},{... | collective-permute-start | bytes 172040 | tf_op jit(solution)/shard_map/ppermute | solution.py:287
  26.0 4.7 %collective-permute-start.6 = (f32[2,7,8,128]{3,2,1,0:T(8,128)S(1)}, f32[2,7,8,128]{3,2,1,0:T(8,128)S(1)}, u32[]{:S(2)}, u32[]{:S(2)}) collective-permute-start(f32[2,7,8,128]{3,2,1,0:T(8,128)S(1)} %pad_maximum_fusion.1), channel_id=1, source_target_pairs={{0,16},{4,20},{8,24},{12,28},{16,0},{20,4},{24,8},{28,12},{1,17},{... | collective-permute-start | bytes 172040 | tf_op jit(solution)/shard_map/ppermute | solution.py:287
  27.5 4.2 %collective-permute-start.5 = (f32[2,7,8,128]{3,2,1,0:T(8,128)S(1)}, f32[2,7,8,128]{3,2,1,0:T(8,128)S(1)}, u32[]{:S(2)}, u32[]{:S(2)}) collective-permute-start(f32[2,7,8,128]{3,2,1,0:T(8,128)S(1)} %pad_maximum_fusion), channel_id=1, source_target_pairs={{0,8},{4,12},{8,0},{12,4},{16,24},{20,28},{24,16},{28,20},{1,9},{5... | collective-permute-start | bytes 172040 | tf_op jit(solution)/shard_map/ppermute | solution.py:287

commit v4 on v3

--- a/solution.py
+++ b/solution.py
@@ -11,6 +11,7 @@
 F32 = jnp.float32
 LOG2E = math.log2(math.e)
 LANES = 128
+TONES = 8
 
 
 def sample_sums(rho, samples, rows):
@@ -29,23 +30,35 @@
     send_ref[...] = sample_sums(rho_ref[...], half, rows)
 
 
-def keep_kernel(half, rows, rho_hbm, keep_ref, total_ref, rho_ref, sem):
+def keep_kernel(half, rows, rho_hbm, keep_ref, rho_ref, sem):
     odd = lax.axis_index("light") % 2
     copy = pltpu.make_async_copy(rho_hbm, rho_ref, sem)
     copy.start()
     copy.wait()
     first = pl.multiple_of(odd * half * rows, half * rows)
     keep_ref[...] = sample_sums(rho_ref[pl.ds(first, half * rows), :], half, rows)
-    narrow = (rows, 2 * half * rows)
-    of_row = (
-        lax.broadcasted_iota(jnp.int32, narrow, 1) % rows
-        == lax.broadcasted_iota(jnp.int32, narrow, 0)
-    ).astype(jnp.bfloat16)
-    total_ref[...] = jnp.dot(of_row, rho_ref[...], preferred_element_type=F32)
+
+
+def table_kernel(sliced, rho_ref, rank_ref, center_ref, total_ref, table_ref):
+    rows = total_ref.shape[0]
+    narrow = (rows, rho_ref.shape[0])
+    of_row = lax.broadcasted_iota(jnp.int32, narrow, 1) % rows == lax.broadcasted_iota(jnp.int32, narrow, 0)
+    total_ref[...] = jnp.dot(of_row.astype(jnp.bfloat16), rho_ref[...], preferred_element_type=F32)
+    for k in range(3):
+        c = jnp.full((1, LANES), center_ref[k], F32)
+        table_ref[k : k + 1, :] = c * (16.0 * LOG2E)
+        table_ref[3 + k : 4 + k, :] = 4.0 * jnp.exp2(c * c * (-8.0 * LOG2E))
+    if sliced:
+        bricks = rank_ref.shape[1]
+        place = lax.axis_index("depth")
+        for view in range(2):
+            for slot in range(bricks):
+                row = TONES + bricks * view + slot
+                table_ref[row : row + 1, :] = jnp.full((1, LANES), rank_ref[view, place ^ slot].astype(F32))
 
 
 def pre_kernel(
-    samples, rows, width, rho_ref, total_ref, light_ref, view_ref, center_ref,
+    samples, rows, width, rho_ref, total_ref, light_ref, view_ref, table_ref,
     near_ref, far_ref, red_ref, green_ref, blue_ref, above_ref,
 ):
     columns = rho_ref.shape[1]
@@ -60,7 +73,7 @@
         )
 
     shape = (rows, width)
-    tone = [center_ref[k] * (16.0 * LOG2E) for k in range(3)]
+    tone = [jnp.broadcast_to(jnp.concatenate([table_ref[k : k + 1, :]] * (width // LANES), 1), shape) for k in range(3)]
     for first in range(0, columns, width):
         at = pl.ds(first, width)
         light = jnp.broadcast_to(light_ref[:, at] * LOG2E, shape)
@@ -90,21 +103,18 @@
 
 
 def post_kernel(
-    rows, second, sliced, place_ref, below_ref, *refs
+    rows, second, sliced, below_ref, light_ref, table_ref, near_ref, far_ref, red_ref, green_ref, blue_ref,
+    rest_ref, out_ref, lit_ref,
 ):
-    early_ref = refs[0] if second else None
-    light_ref, center_ref, near_ref, far_ref, red_ref, green_ref, blue_ref, rest_ref, out_ref, lit_ref = refs[second:]
     half, columns = below_ref.shape
     odd = lax.axis_index("light") % 2
     base = (1 - odd if second else odd) * half
-    chip, core = (place_ref[0] // 2, place_ref[0] % 2) if sliced else (0, 0)
-    below = below_ref[...]
-    if second:
-        below = below + jnp.where(odd == 1, early_ref[...], 0.0)
-    lit_ref[...] = jnp.exp2(below * (light_ref[...] * -LOG2E))
+    place = lax.axis_index("depth") if sliced else 0
+    chip, core = place // 2, place % 2
+    lit_ref[...] = jnp.exp2(below_ref[...] * (light_ref[...] * -LOG2E))
     width = 2 * LANES
     shape = (rows, width)
-    scales = [4.0 * jnp.exp2(jnp.full((rows, LANES), center_ref[k], F32) ** 2 * (-8.0 * LOG2E)) for k in range(3)]
+    scales = [jnp.broadcast_to(table_ref[3 + k : 4 + k, :], (rows, LANES)) for k in range(3)]
     for slot in range(columns // width):
         at = pl.ds(pl.multiple_of((slot ^ chip) * width, width), width)
         sums = [jnp.zeros(shape, F32)] * 6
@@ -187,20 +197,21 @@
     return jnp.where(depth < 0.35, depth * small, 1.0 - jnp.exp2(depth * -LOG2E))
 
 
-def slots_kernel(place_ref, rank_ref, rate_ref, own_ref, sibling_ref, *refs):
+def slots_kernel(table_ref, rate_ref, own_ref, sibling_ref, *refs):
     *chip_refs, out_ref = refs
     shape = out_ref.shape[2:]
     blocks = [own_ref.at[0, 0], sibling_ref.at[0]] + [ref.at[t] for ref in chip_refs for t in range(2)]
     depths = [block[6] for block in blocks]
     for view in range(2):
         rate = jnp.broadcast_to(rate_ref[view : view + 1, :], shape)
-        ranks = [rank_ref[view, place_ref[0] ^ slot] for slot in range(len(blocks))]
+        first = TONES + len(blocks) * view
+        ranks = [jnp.broadcast_to(table_ref[first + slot : first + slot + 1, :], shape) for slot in range(len(blocks))]
         colors = [jnp.zeros(shape, F32)] * 3
         for i, block in enumerate(blocks):
             front = jnp.zeros(shape, F32)
             for j, depth in enumerate(depths):
                 if j != i:
-                    front = front + depth * (ranks[j] < ranks[i]).astype(F32)
+                    front = front + jnp.where(ranks[j] < ranks[i], depth, 0.0)
             seen = jnp.exp2(front * rate * -LOG2E)
             colors = [colors[k] + block[3 * view + k] * seen for k in range(3)]
         for k in range(3):
@@ -208,30 +219,25 @@
         out_ref[view, 3] = opacity(sum(depths) * rate)
 
 
-def composite_slots(place, rank, rate, own, sibling, chips):
-    vmem, smem = pl.BlockSpec(memory_space=pltpu.VMEM), pl.BlockSpec(memory_space=pltpu.SMEM)
-    blocks = [pltpu.with_memory_space_constraint(x, pltpu.VMEM) for x in (own, sibling, *chips)]
+def composite_slots(table, rate, own, sibling, chips):
+    blocks = [own, sibling, *chips]
     _, rows, columns = own.shape[2:]
-    return pl.pallas_call(
-        slots_kernel,
-        out_shape=jax.ShapeDtypeStruct((2, 4, rows, columns), F32),
-        in_specs=[smem, smem, vmem] + [vmem] * len(blocks),
-        out_specs=vmem,
-        compiler_params=pltpu.CompilerParams(vmem_limit_bytes=8 << 20),
-    )(*(pltpu.with_memory_space_constraint(x, pltpu.SMEM) for x in (place, rank)), pltpu.with_memory_space_constraint(rate, pltpu.VMEM), *blocks)
-
-
-def swap(x, stride, n, first=0, last=None):
-    return lax.ppermute(x, "light", [(i, i ^ stride) for i in range(first, n if last is None else last)])
+    (image,) = call(
+        slots_kernel, [((2, 4, rows, columns), F32)], "VV" + "V" * len(blocks), [], 1 << 10, 1 << 10,
+        table, rate, *blocks,
+    )
+    return image
+
+
+def swap(x, stride, n):
+    return lax.ppermute(x, "light", [(i, i ^ stride) for i in range(n)])
 
 
 def halves_below(keep, sibling, sums, stride, n):
     odd = (lax.axis_index("light") // stride) % 2 == 1
     below = lower(sums, 2 * stride, n)
-    first = swap(keep, stride, n, 0, 2 * stride)
-    mine = below + jnp.where(odd, sibling, 0.0)
-    other = swap(below + jnp.where(odd, 0.0, keep), stride, n, 2 * stride)
-    return mine, other, first
+    other = swap(below + jnp.where(odd, 0.0, keep), stride, n)
+    return below + jnp.where(odd, sibling, 0.0), other
 
 
 def lower(x, stride, n):
@@ -243,8 +249,7 @@
     half = x.shape[0] // 2
     first, last = x[:half], x[half:]
     keep, sibling = jnp.where(odd, last, first), swap(jnp.where(odd, first, last), stride, n)
-    mine, other, early = halves_below(keep, sibling, keep + sibling, stride, n)
-    other = other + jnp.where(odd, early, 0.0)
+    mine, other = halves_below(keep, sibling, keep + sibling, stride, n)
     return jnp.where(odd, jnp.concatenate([other, mine]), jnp.concatenate([mine, other]))
 
 
@@ -259,28 +264,31 @@
         functools.partial(send_kernel, half, rows), [(part, F32)], "A",
         [pltpu.VMEM((half * rows, columns), jnp.bfloat16), sem], 1 << 20, 1 << 19, rho,
     )
-    keep, total, rho = call(
-        functools.partial(keep_kernel, half, rows), [(part, F32), ((rows, columns), F32), (whole, jnp.bfloat16)], "A",
-        [sem], 1 << 20, 1 << 20, rho,
+    own = columns // depth_n
+    sliced = own == LANES and depth_n <= 8 and depth_n & (depth_n - 1) == 0
+    table = (TONES + 2 * depth_n if sliced else TONES, LANES)
+    keep, rho = call(
+        functools.partial(keep_kernel, half, rows), [(part, F32), (whole, jnp.bfloat16)], "A", [sem], 1 << 20, 1 << 20, rho,
+    )
+    total, table = call(
+        functools.partial(table_kernel, sliced), [((rows, columns), F32), (table, F32)], "Vss", [], 1 << 20, 1 << 20,
+        rho, rank, centers,
     )
     sibling = swap(send, 1, light_n)
     sums = keep + sibling
     near, far, red, green, blue = call(
-        functools.partial(pre_kernel, samples, rows, 256), [(whole, F32)] * 5, "VVVVS",
-        [pltpu.VMEM(whole, F32)], 1 << 20, 12 << 20, rho, total, light, view_rate, centers,
-    )
-    mine, other, early = halves_below(keep, sibling, sums, 1, light_n)
-    own = columns // depth_n
+        functools.partial(pre_kernel, samples, rows, 256), [(whole, F32)] * 5, "VVVVV",
+        [pltpu.VMEM(whole, F32)], 1 << 20, 12 << 20, rho, total, light, view_rate, table,
+    )
+    mine, other = halves_below(keep, sibling, sums, 1, light_n)
     place = lax.axis_index("depth")
     rate = lax.dynamic_slice_in_dim(view_rate, place * own, own, axis=1)
-    place = place.reshape(1)
-    sliced = own == LANES and depth_n <= 8 and depth_n & (depth_n - 1) == 0
     packed = total
-    for second, below in enumerate(([mine], [other, early])):
+    for second, below in enumerate((mine, other)):
         (packed,) = call(
-            functools.partial(post_kernel, rows, second, sliced), [((2, columns // (2 * LANES), 7, rows, LANES), F32)], "S" + "V" * len(below) + "VSVVVVVV",
+            functools.partial(post_kernel, rows, second, sliced), [((2, columns // (2 * LANES), 7, rows, LANES), F32)], "VVVVVVVVV",
             [pltpu.VMEM(part, F32)], 1 << 10, 1 << 10,
-            place, *below, light, centers, near, far, red, green, blue, packed,
+            below, light, table, near, far, red, green, blue, packed,
         )
     if sliced:
         def send_to(x, stride):
@@ -288,7 +296,7 @@
 
         got = send_to(packed[1], 1)
         chips = [send_to(jnp.stack([packed[0, chip], got[chip]]), 2 * chip) for chip in range(1, depth_n // 2)]
-        return composite_slots(place, rank, rate, packed, got, chips)
+        return composite_slots(table, rate, packed, got, chips)
     parts = packed.transpose(1, 0, 2, 3, 4).reshape(columns // LANES, 7, rows, LANES)
     if own % LANES == 0:
         parts = parts.reshape(depth_n, own // LANES, 7, rows, LANES).transpose(0, 2, 3, 1, 4)

time: 33.2 us -> 31.3 us (0.943)
  the two profiles are of different devices: /device:TPU:20 before, /device:TPU:0 now
where the time goes in v4:
time: 31.3 us; the launch traced here: 31.2 us
  waiting for transfers between devices  13.5 us (43%)
  starting transfers between devices  10.1 us (32%)
  Pallas kernels  6.78 us (22%)
  local copies, waits for them, and re-layouts  0.66 us (2%)
    ppermute x3, waiting for transfers between devices, swap(): return lax.ppermute(x, 'light', [(i, i ^ stride) for i in range(n)])  8.67 us
    pallas_call x7, Pallas kernels, call(): pl.pallas_call(kernel, out_shape=tuple((pltpu.VMEM(o, t) for o, t in outs...  6.78 us
    ppermute x3, starting transfers between devices, swap(): return lax.ppermute(x, 'light', [(i, i ^ stride) for i in range(n)])  6.49 us
    ppermute x4, waiting for transfers between devices, send_to(): return lax.ppermute(x, 'depth', [(i, i ^ stride) for i in range(depth_n)])  4.78 us
    ppermute x4, starting transfers between devices, send_to(): return lax.ppermute(x, 'depth', [(i, i ^ stride) for i in range(depth_n)])  3.62 us
    unnamed x9, local copies, waits for them, and re-layouts  0.63 us
  transfers between devices with their start and end apart: 7, of which 7 were waited for; matrix products, arithmetic and copies ran while one was open for 0% of the time, Pallas kernels for 16%

profile of v4, /device:TPU:0, one launch (start us, length us, event | category | flops | bytes accessed | tf_op | source)
XLA Modules:
  0.0 31.2 jit_solution(3467416198059903678)
XLA Ops:
  0.0 0.0 copy-start.3
  0.0 0.0 copy-start.2
  0.0 0.0 copy-start
  0.0 0.0 copy-start.1
  0.0 1.3 %shard_map.57 = f32[32,1024]{1,0:T(8,128)S(1)} custom-call(bf16[512,1024]{1,0:T(8,128)(2,1)} %bitcast.13), custom_call_target="tpu_custom_call" | custom-call | flops 1048576 | bytes 524288 | tf_op jit(solution)/shard_map/pallas_call | solution.py:143
  1.3 3.1 %collective-permute-start = (f32[32,1024]{1,0:T(8,128)S(1)}, f32[32,1024]{1,0:T(8,128)S(1)}, u32[]{:S(2)}, u32[]{:S(2)}) collective-permute-start(f32[32,1024]{1,0:T(8,128)S(1)} %shard_map.57), channel_id=1, source_target_pairs={{0,1},{1,0},{2,3},{3,2},{4,5},{5,4},{6,7},{7,6},{8,9},{9,8},{10,11... | collective-permute-start | bytes 393224 | tf_op jit(solution)/shard_map/ppermute | solution.py:233
  4.4 1.4 %shard_map.55 = (f32[32,1024]{1,0:T(8,128)S(1)}, bf16[512,1024]{1,0:T(8,128)(2,1)S(1)}) custom-call(bf16[512,1024]{1,0:T(8,128)(2,1)} %bitcast.14), custom_call_target="tpu_custom_call" | custom-call | flops 1048576 | bytes 1048576 | tf_op jit(solution)/shard_map/pallas_call | solution.py:143
  5.9 2.1 %collective-permute-done = f32[32,1024]{1,0:T(8,128)S(1)} collective-permute-done((f32[32,1024]{1,0:T(8,128)S(1)}, f32[32,1024]{1,0:T(8,128)S(1)}, u32[]{:S(2)}, u32[]{:S(2)}) %collective-permute-start) | collective-permute-done | bytes 131104 | tf_op jit(solution)/shard_map/ppermute | solution.py:233
  7.9 2.8 %collective-permute-start.1 = (f32[32,1024]{1,0:T(8,128)S(1)}, f32[32,1024]{1,0:T(8,128)S(1)}, u32[]{:S(2)}, u32[]{:S(2)}) collective-permute-start(f32[32,1024]{1,0:T(8,128)S(1)} %add.23), channel_id=1, source_target_pairs={{0,2},{1,3},{2,0},{3,1},{4,6},{5,7},{6,4},{7,5},{8,10},{9,11},{10,... | collective-permute-start | bytes 393224 | tf_op jit(solution)/shard_map/ppermute | solution.py:233
  10.7 5.6 %collective-permute-done.1 = f32[32,1024]{1,0:T(8,128)S(1)} collective-permute-done((f32[32,1024]{1,0:T(8,128)S(1)}, f32[32,1024]{1,0:T(8,128)S(1)}, u32[]{:S(2)}, u32[]{:S(2)}) %collective-permute-start.1) | collective-permute-done | bytes 131104 | tf_op jit(solution)/shard_map/ppermute | solution.py:233
  16.4 0.6 %collective-permute-start.2 = (f32[32,1024]{1,0:T(8,128)S(1)}, f32[32,1024]{1,0:T(8,128)S(1)}, u32[]{:S(2)}, u32[]{:S(2)}) collective-permute-start(f32[32,1024]{1,0:T(8,128)S(1)} %get-tuple-element.27), channel_id=1, source_target_pairs={{0,1},{1,0},{2,3},{3,2},{4,5},{5,4},{6,7},{7,6},{8,9},{9,8},{10,11... | collective-permute-start | bytes 393224 | tf_op jit(solution)/shard_map/ppermute | solution.py:233
  17.0 0.0 copy-done.3
  17.0 0.0 copy-done.2
  17.0 0.8 %shard_map.56 = (f32[8,1024]{1,0:T(8,128)S(1)}, f32[24,128]{1,0:T(8,128)S(1)}) custom-call(bf16[512,1024]{1,0:T(8,128)(2,1)S(1)} %get-tuple-element.14.rho_ref, s32[2,8]{1,0:T(2,128)S(1)} %copy-done.2, f32[3]{0:T(128)S(1)} %copy-done.3), custom_call_target="tpu_custom_call" | custom-call | flops 1048576 | bytes 1048576 | tf_op jit(solution)/shard_map/pallas_call | solution.py:143
  17.8 0.0 copy-done
  17.8 0.0 copy-done.1
  17.8 2.1 %shard_map.58 = (f32[512,1024]{1,0:T(8,128)S(1)}, f32[512,1024]{1,0:T(8,128)S(1)}, f32[512,1024]{1,0:T(8,128)S(1)}, f32[512,1024]{1,0:T(8,128)S(1)}, f32[512,1024]{1,0:T(8,128)S(1)}) custom-call(bf16[512,1024]{1,0:T(8,128)(2,1)S(1)} %get-tuple-element.14.rho_ref, f32[8,1024]{1,0:T(8,128)S(1)} %get-tuple-element.17.total_ref.rest_ref, ...), custom_call_target="tpu_custom_call" | custom-call | flops 1048576 | bytes 12582912 | tf_op jit(solution)/shard_map/pallas_call | solution.py:143
  20.0 0.5 %shard_map.59.rest_ref = f32[2,4,7,8,128]{4,3,2,1,0:T(8,128)S(1)} custom-call(f32[32,1024]{1,0:T(8,128)S(1)} %get-tuple-element.26.below_ref, f32[1,1024]{1,0:T(1,128)S(1)} %bitcast.11, f32[24,128]{1,0:T(8,128)S(1)} %get-tuple-element.15.table_ref, f32[512,1024]{1,0:T(8,128)S(1)} %get-tuple-element.18.near_ref, f32[512,1024]{1,0:T(8,128)S(1)} %get-tuple-element.19.far_ref, ...), custom_call_target="tpu_custom_call" | custom-call | flops 1024 | bytes 1024 | tf_op jit(solution)/shard_map/pallas_call | solution.py:143
  20.5 1.0 %collective-permute-done.2.below_ref = f32[32,1024]{1,0:T(8,128)S(1)} collective-permute-done((f32[32,1024]{1,0:T(8,128)S(1)}, f32[32,1024]{1,0:T(8,128)S(1)}, u32[]{:S(2)}, u32[]{:S(2)}) %collective-permute-start.2) | collective-permute-done | bytes 131104 | tf_op jit(solution)/shard_map/ppermute | solution.py:233
  21.5 0.5 %shard_map.60.own_ref = f32[2,4,7,8,128]{4,3,2,1,0:T(8,128)S(1)} custom-call(f32[32,1024]{1,0:T(8,128)S(1)} %collective-permute-done.2.below_ref, f32[1,1024]{1,0:T(1,128)S(1)} %bitcast.12, f32[24,128]{1,0:T(8,128)S(1)} %get-tuple-element.15.table_ref, f32[512,1024]{1,0:T(8,128)S(1)} %get-tuple-element.18.near_ref, ...), custom_call_target="tpu_custom_call" | custom-call | flops 1024 | bytes 1024 | tf_op jit(solution)/shard_map/pallas_call | solution.py:143
  22.0 0.1 collective-permute-start.3
  22.1 1.3 %collective-permute-done.3.sibling_ref = f32[4,7,8,128]{3,2,1,0:T(8,128)S(1)} collective-permute-done((f32[4,7,8,128]{3,2,1,0:T(8,128)S(1)}, f32[4,7,8,128]{3,2,1,0:T(8,128)S(1)}, u32[]{:S(2)}, u32[]{:S(2)}) %collective-permute-start.3) | collective-permute-done | bytes 114720 | tf_op jit(solution)/shard_map/ppermute | solution.py:295
  23.4 2.4 %collective-permute-start.6 = (f32[2,7,8,128]{3,2,1,0:T(8,128)S(1)}, f32[2,7,8,128]{3,2,1,0:T(8,128)S(1)}, u32[]{:S(2)}, u32[]{:S(2)}) collective-permute-start(f32[2,7,8,128]{3,2,1,0:T(8,128)S(1)} %pad_maximum_fusion.2), channel_id=1, source_target_pairs={{0,24},{4,28},{8,16},{12,20},{16,8},{20,12},{24,0},{28,4},{1,25},{... | collective-permute-start | bytes 172040 | tf_op jit(solution)/shard_map/ppermute | solution.py:295
  25.8 0.5 %collective-permute-start.5 = (f32[2,7,8,128]{3,2,1,0:T(8,128)S(1)}, f32[2,7,8,128]{3,2,1,0:T(8,128)S(1)}, u32[]{:S(2)}, u32[]{:S(2)}) collective-permute-start(f32[2,7,8,128]{3,2,1,0:T(8,128)S(1)} %pad_maximum_fusion.1), channel_id=1, source_target_pairs={{0,16},{4,20},{8,24},{12,28},{16,0},{20,4},{24,8},{28,12},{1,17},{... | collective-permute-start | bytes 172040 | tf_op jit(solution)/shard_map/ppermute | solution.py:295
  26.3 0.7 %collective-permute-start.4 = (f32[2,7,8,128]{3,2,1,0:T(8,128)S(1)}, f32[2,7,8,128]{3,2,1,0:T(8,128)S(1)}, u32[]{:S(2)}, u32[]{:S(2)}) collective-permute-start(f32[2,7,8,128]{3,2,1,0:T(8,128)S(1)} %pad_maximum_fusion), channel_id=1, source_target_pairs={{0,8},{4,12},{8,0},{12,4},{16,24},{20,28},{24,16},{28,20},{1,9},{5... | collective-permute-start | bytes 172040 | tf_op jit(solution)/shard_map/ppermute | solution.py:295
  27.0 1.6 %collective-permute-done.6.refs_2_ = f32[2,7,8,128]{3,2,1,0:T(8,128)S(1)} collective-permute-done((f32[2,7,8,128]{3,2,1,0:T(8,128)S(1)}, f32[2,7,8,128]{3,2,1,0:T(8,128)S(1)}, u32[]{:S(2)}, u32[]{:S(2)}) %collective-permute-start.6) | collective-permute-done | bytes 57376 | tf_op jit(solution)/shard_map/ppermute | solution.py:295
  28.6 1.4 %collective-permute-done.5.refs_1_ = f32[2,7,8,128]{3,2,1,0:T(8,128)S(1)} collective-permute-done((f32[2,7,8,128]{3,2,1,0:T(8,128)S(1)}, f32[2,7,8,128]{3,2,1,0:T(8,128)S(1)}, u32[]{:S(2)}, u32[]{:S(2)}) %collective-permute-start.5) | collective-permute-done | bytes 57376 | tf_op jit(solution)/shard_map/ppermute | solution.py:295
  29.9 0.5 %collective-permute-done.4.refs_0_ = f32[2,7,8,128]{3,2,1,0:T(8,128)S(1)} collective-permute-done((f32[2,7,8,128]{3,2,1,0:T(8,128)S(1)}, f32[2,7,8,128]{3,2,1,0:T(8,128)S(1)}, u32[]{:S(2)}, u32[]{:S(2)}) %collective-permute-start.4) | collective-permute-done | bytes 57376 | tf_op jit(solution)/shard_map/ppermute | solution.py:295
  30.5 0.1 shard_map.61
  30.5 0.6 %copy.6 = f32[2,4,8,128]{3,2,1,0:T(8,128)} copy(f32[2,4,8,128]{3,2,1,0:T(8,128)S(1)} %shard_map.61) | data formatting | bytes 65536
  (9 shorter events, 0.1 us)
Async XLA Ops:
  0.0 17.0 %copy-start.3 = (f32[3]{0:T(128)S(1)}, f32[3]{0:T(128)}, u32[]{:S(2)}) copy-start(f32[3]{0:T(128)} %center_ref.1) | copy-start | bytes 40
  0.0 17.0 %copy-start.2 = (s32[2,8]{1,0:T(2,128)S(1)}, s32[2,8]{1,0:T(2,128)}, u32[]{:S(2)}) copy-start(s32[2,8]{1,0:T(2,128)} %rank_ref.1) | copy-start | bytes 196
  0.0 17.8 %copy-start = (f32[1024]{0:T(1024)S(1)}, f32[1024]{0:T(1024)}, u32[]{:S(2)}) copy-start(f32[1024]{0:T(1024)} %param.6) | copy-start | bytes 12292
  0.0 17.8 %copy-start.1 = (f32[2,1024]{1,0:T(2,128)S(1)}, f32[2,1024]{1,0:T(2,128)}, u32[]{:S(2)}) copy-start(f32[2,1024]{1,0:T(2,128)} %view_ref.1) | copy-start | bytes 24580
  1.3 6.6 %collective-permute-start = (f32[32,1024]{1,0:T(8,128)S(1)}, f32[32,1024]{1,0:T(8,128)S(1)}, u32[]{:S(2)}, u32[]{:S(2)}) collective-permute-start(f32[32,1024]{1,0:T(8,128)S(1)} %shard_map.57), channel_id=1, source_target_pairs={{0,1},{1,0},{2,3},{3,2},{4,5},{5,4},{6,7},{7,6},{8,9},{9,8},{10,11... | collective-permute-start | bytes 393224 | tf_op jit(solution)/shard_map/ppermute | solution.py:233
  7.9 8.5 %collective-permute-start.1 = (f32[32,1024]{1,0:T(8,128)S(1)}, f32[32,1024]{1,0:T(8,128)S(1)}, u32[]{:S(2)}, u32[]{:S(2)}) collective-permute-start(f32[32,1024]{1,0:T(8,128)S(1)} %add.23), channel_id=1, source_target_pairs={{0,2},{1,3},{2,0},{3,1},{4,6},{5,7},{6,4},{7,5},{8,10},{9,11},{10,... | collective-permute-start | bytes 393224 | tf_op jit(solution)/shard_map/ppermute | solution.py:233
  16.4 5.0 %collective-permute-start.2 = (f32[32,1024]{1,0:T(8,128)S(1)}, f32[32,1024]{1,0:T(8,128)S(1)}, u32[]{:S(2)}, u32[]{:S(2)}) collective-permute-start(f32[32,1024]{1,0:T(8,128)S(1)} %get-tuple-element.27), channel_id=1, source_target_pairs={{0,1},{1,0},{2,3},{3,2},{4,5},{5,4},{6,7},{7,6},{8,9},{9,8},{10,11... | collective-permute-start | bytes 393224 | tf_op jit(solution)/shard_map/ppermute | solution.py:233
  22.0 1.4 %collective-permute-start.3 = (f32[4,7,8,128]{3,2,1,0:T(8,128)S(1)}, f32[4,7,8,128]{3,2,1,0:T(8,128)S(1)}, u32[]{:S(2)}, u32[]{:S(2)}) collective-permute-start(f32[4,7,8,128]{3,2,1,0:T(8,128)S(1)} %slice_bitcast_fusion), channel_id=1, source_target_pairs={{0,4},{4,0},{8,12},{12,8},{16,20},{20,16},{24,28},{28,24},{1,5},{5... | collective-permute-start | bytes 344072 | tf_op jit(solution)/shard_map/ppermute | solution.py:295
  23.4 5.2 %collective-permute-start.6 = (f32[2,7,8,128]{3,2,1,0:T(8,128)S(1)}, f32[2,7,8,128]{3,2,1,0:T(8,128)S(1)}, u32[]{:S(2)}, u32[]{:S(2)}) collective-permute-start(f32[2,7,8,128]{3,2,1,0:T(8,128)S(1)} %pad_maximum_fusion.2), channel_id=1, source_target_pairs={{0,24},{4,28},{8,16},{12,20},{16,8},{20,12},{24,0},{28,4},{1,25},{... | collective-permute-start | bytes 172040 | tf_op jit(solution)/shard_map/ppermute | solution.py:295
  25.8 4.2 %collective-permute-start.5 = (f32[2,7,8,128]{3,2,1,0:T(8,128)S(1)}, f32[2,7,8,128]{3,2,1,0:T(8,128)S(1)}, u32[]{:S(2)}, u32[]{:S(2)}) collective-permute-start(f32[2,7,8,128]{3,2,1,0:T(8,128)S(1)} %pad_maximum_fusion.1), channel_id=1, source_target_pairs={{0,16},{4,20},{8,24},{12,28},{16,0},{20,4},{24,8},{28,12},{1,17},{... | collective-permute-start | bytes 172040 | tf_op jit(solution)/shard_map/ppermute | solution.py:295
  26.3 4.2 %collective-permute-start.4 = (f32[2,7,8,128]{3,2,1,0:T(8,128)S(1)}, f32[2,7,8,128]{3,2,1,0:T(8,128)S(1)}, u32[]{:S(2)}, u32[]{:S(2)}) collective-permute-start(f32[2,7,8,128]{3,2,1,0:T(8,128)S(1)} %pad_maximum_fusion), channel_id=1, source_target_pairs={{0,8},{4,12},{8,0},{12,4},{16,24},{20,28},{24,16},{28,20},{1,9},{5... | collective-permute-start | bytes 172040 | tf_op jit(solution)/shard_map/ppermute | solution.py:295

commit v5 on v4

--- a/solution.py
+++ b/solution.py
@@ -21,29 +21,15 @@
     return jnp.dot((source // rows == target).astype(jnp.bfloat16), rho, preferred_element_type=F32)
 
 
-def send_kernel(half, rows, rho_hbm, send_ref, rho_ref, sem):
-    odd = lax.axis_index("light") % 2
-    first = pl.multiple_of((1 - odd) * half * rows, half * rows)
-    copy = pltpu.make_async_copy(rho_hbm.at[pl.ds(first, half * rows)], rho_ref, sem)
+def sums_kernel(rows, places, sliced, rho_hbm, rank_hbm, center_hbm, *refs):
+    *out_refs, table_ref, rho_ref, sums_ref, rank_ref, center_ref, sems = refs
+    copy = pltpu.make_async_copy(rho_hbm, rho_ref, sems.at[0])
+    small = pltpu.make_async_copy(rank_hbm, rank_ref, sems.at[1]), pltpu.make_async_copy(center_hbm, center_ref, sems.at[2])
     copy.start()
-    copy.wait()
-    send_ref[...] = sample_sums(rho_ref[...], half, rows)
-
-
-def keep_kernel(half, rows, rho_hbm, keep_ref, rho_ref, sem):
-    odd = lax.axis_index("light") % 2
-    copy = pltpu.make_async_copy(rho_hbm, rho_ref, sem)
-    copy.start()
-    copy.wait()
-    first = pl.multiple_of(odd * half * rows, half * rows)
-    keep_ref[...] = sample_sums(rho_ref[pl.ds(first, half * rows), :], half, rows)
-
-
-def table_kernel(sliced, rho_ref, rank_ref, center_ref, total_ref, table_ref):
-    rows = total_ref.shape[0]
-    narrow = (rows, rho_ref.shape[0])
-    of_row = lax.broadcasted_iota(jnp.int32, narrow, 1) % rows == lax.broadcasted_iota(jnp.int32, narrow, 0)
-    total_ref[...] = jnp.dot(of_row.astype(jnp.bfloat16), rho_ref[...], preferred_element_type=F32)
+    for part in small:
+        part.start()
+    for part in small:
+        part.wait()
     for k in range(3):
         c = jnp.full((1, LANES), center_ref[k], F32)
         table_ref[k : k + 1, :] = c * (16.0 * LOG2E)
@@ -55,13 +41,40 @@
             for slot in range(bricks):
                 row = TONES + bricks * view + slot
                 table_ref[row : row + 1, :] = jnp.full((1, LANES), rank_ref[view, place ^ slot].astype(F32))
+    copy.wait()
+    samples = sums_ref.shape[0]
+    half = samples // 2
+    for first in (0, half):
+        sums_ref[first : first + half, :] = sample_sums(rho_ref[first * rows : (first + half) * rows, :], half, rows)
+    odd = lax.axis_index("light") % 2
+    for out_ref, (even_first, odd_first) in zip(out_refs, places, strict=True):
+        first = pl.multiple_of(even_first + odd * (odd_first - even_first), 8)
+        out_ref[...] = sums_ref[pl.ds(first, out_ref.shape[0]), :]
+
+
+def pair_kernel(hold_ref, given_ref, cross_ref, pair_ref, late_ref):
+    many = hold_ref.shape[0]
+    pair_ref[...] = hold_ref[...] + given_ref[...]
+    late_ref[:many, :] = hold_ref[...]
+    late_ref[many:, :] = cross_ref[...]
+
+
+def upper_kernel(straight_ref, across_ref, same_ref, cross_ref, below_ref, send_ref):
+    me = lax.axis_index("light")
+    few = same_ref.shape[0]
+    below = jnp.where(me >= 2, straight_ref[...] + across_ref[...], 0.0)
+    below_ref[...] = below
+    send_ref[:few, :] = below + jnp.where(me % 2 == 1, 0.0, same_ref[...])
 
 
 def pre_kernel(
-    samples, rows, width, rho_ref, total_ref, light_ref, view_ref, table_ref,
-    near_ref, far_ref, red_ref, green_ref, blue_ref, above_ref,
+    samples, rows, width, rho_ref, light_ref, view_ref, table_ref,
+    near_ref, far_ref, red_ref, green_ref, blue_ref, total_ref, above_ref,
 ):
     columns = rho_ref.shape[1]
+    narrow = (rows, samples * rows)
+    of_row = lax.broadcasted_iota(jnp.int32, narrow, 1) % rows == lax.broadcasted_iota(jnp.int32, narrow, 0)
+    total_ref[...] = jnp.dot(of_row.astype(jnp.bfloat16), rho_ref[...], preferred_element_type=F32)
     block = 256
     square = (block, block)
     i = lax.broadcasted_iota(jnp.int32, square, 0)
@@ -102,26 +115,51 @@
         lax.fori_loop(0, samples // 2, pair, start, unroll=True)
 
 
+def straight_below(refs, below_ref):
+    same, given = (ref[...] for ref in refs)
+    me = lax.axis_index("light")
+    below_ref[...] = jnp.where(me >= 2, same, 0.0) + jnp.where(me % 2 == 1, given, 0.0)
+
+
+def crossed_below(refs, below_ref):
+    mine, other, cross, late = (ref[...] for ref in refs)
+    few, many = mine.shape[0], cross.shape[0]
+    me = lax.axis_index("light")
+    odd = me % 2 == 1
+    below_ref[:few, :] = jnp.where(odd, other[:few], mine)
+    below_ref[few : 2 * few, :] = jnp.where(odd, mine + late[many:], other[:few])
+    below_ref[2 * few :, :] = jnp.where(me >= 2, cross, 0.0) + jnp.where(odd, late[:many], 0.0)
+
+
+def whole_below(refs, below_ref):
+    first = 0
+    for ref in refs:
+        below_ref[first : first + ref.shape[0], :] = ref[...]
+        first += ref.shape[0]
+
+
 def post_kernel(
-    rows, second, sliced, below_ref, light_ref, table_ref, near_ref, far_ref, red_ref, green_ref, blue_ref,
-    rest_ref, out_ref, lit_ref,
+    rows, second, runs, sliced, assemble, light_ref, table_ref, near_ref, far_ref, red_ref, green_ref, blue_ref, rest_ref, *refs
 ):
-    half, columns = below_ref.shape
-    odd = lax.axis_index("light") % 2
-    base = (1 - odd if second else odd) * half
+    *refs, out_ref, lit_ref = refs
+    assemble(refs, lit_ref)
+    _, columns = lit_ref.shape
     place = lax.axis_index("depth") if sliced else 0
     chip, core = place // 2, place % 2
-    lit_ref[...] = jnp.exp2(below_ref[...] * (light_ref[...] * -LOG2E))
+    odd = lax.axis_index("light") % 2
+    firsts = [even_first + odd * (odd_first - even_first) for even_first, odd_first, _ in runs]
+    groups = [(first, start) for first, (_, _, count) in zip(firsts, runs, strict=True) for start in range(0, count, 8)]
+    lit_ref[...] = jnp.exp2(lit_ref[...] * (light_ref[...] * -LOG2E))
     width = 2 * LANES
     shape = (rows, width)
     scales = [jnp.broadcast_to(table_ref[3 + k : 4 + k, :], (rows, LANES)) for k in range(3)]
     for slot in range(columns // width):
         at = pl.ds(pl.multiple_of((slot ^ chip) * width, width), width)
         sums = [jnp.zeros(shape, F32)] * 6
-        for group in range(half // 8):
+        for group, (first, start) in enumerate(groups):
             lit = lit_ref[group * 8 : group * 8 + 8, at]
             for part in range(8):
-                here = pl.ds(pl.multiple_of((base + group * 8 + part) * rows, rows), rows)
+                here = pl.ds(pl.multiple_of((first + start + part) * rows, rows), rows)
                 shade = jnp.broadcast_to(lit[part : part + 1], shape)
                 weights = near_ref[here, at] * shade, far_ref[here, at] * shade
                 colors = [ref[here, at] for ref in (red_ref, green_ref, blue_ref)]
@@ -233,13 +271,6 @@
     return lax.ppermute(x, "light", [(i, i ^ stride) for i in range(n)])
 
 
-def halves_below(keep, sibling, sums, stride, n):
-    odd = (lax.axis_index("light") // stride) % 2 == 1
-    below = lower(sums, 2 * stride, n)
-    other = swap(below + jnp.where(odd, 0.0, keep), stride, n)
-    return below + jnp.where(odd, sibling, 0.0), other
-
-
 def lower(x, stride, n):
     if stride == n:
         return jnp.zeros_like(x)
@@ -249,46 +280,69 @@
     half = x.shape[0] // 2
     first, last = x[:half], x[half:]
     keep, sibling = jnp.where(odd, last, first), swap(jnp.where(odd, first, last), stride, n)
-    mine, other = halves_below(keep, sibling, keep + sibling, stride, n)
+    below = lower(keep + sibling, 2 * stride, n)
+    other = swap(below + jnp.where(odd, 0.0, keep), stride, n)
+    mine = below + jnp.where(odd, sibling, 0.0)
     return jnp.where(odd, jnp.concatenate([other, mine]), jnp.concatenate([mine, other]))
+
+
+def lower_of_four(give, hold, same, cross):
+    given = swap(give, 1, 4)
+    straight, across = swap(same, 2, 4), swap(cross, 3, 4)
+    columns = same.shape[1]
+    pair, late = call(
+        pair_kernel, [(hold.shape, F32), ((hold.shape[0] + cross.shape[0], columns), F32)], "VVV", [], 1 << 10, 1 << 10, hold, given, cross
+    )
+    from_same, from_cross = swap(pair, 2, 4), swap(pair, 3, 4)
+    late = swap(late, 1, 4)
+    mine, send = call(
+        upper_kernel, [(same.shape, F32), ((same.shape[0], columns), F32)], "VVVV", [], 1 << 34, 1 << 10, straight, across, same, cross
+    )
+    other = swap(send, 1, 4)
+    return (from_same, given), (mine, other, from_cross, late)
 
 
 def shards(depth_n, light_n, density, light_rate, view_rate, centers, rank):
     samples, rows, columns = density.shape
     rho = density.reshape(samples * rows, columns)
-    half = samples // 2
     light = light_rate.reshape(1, -1)
-    whole, part = (samples * rows, columns), (half, columns)
-    sem = pltpu.SemaphoreType.DMA
-    (send,) = call(
-        functools.partial(send_kernel, half, rows), [(part, F32)], "A",
-        [pltpu.VMEM((half * rows, columns), jnp.bfloat16), sem], 1 << 20, 1 << 19, rho,
-    )
+    whole = (samples * rows, columns)
+    few, many = samples // 8, 3 * samples // 8
+    places = ((2 * few + many, 2 * few), (2 * few, 2 * few + many), (0, few), (few, 0)) if light_n == 4 else ((0, 0),)
+    sizes = (many, many, few, few) if light_n == 4 else (samples,)
     own = columns // depth_n
     sliced = own == LANES and depth_n <= 8 and depth_n & (depth_n - 1) == 0
     table = (TONES + 2 * depth_n if sliced else TONES, LANES)
-    keep, rho = call(
-        functools.partial(keep_kernel, half, rows), [(part, F32), (whole, jnp.bfloat16)], "A", [sem], 1 << 20, 1 << 20, rho,
-    )
-    total, table = call(
-        functools.partial(table_kernel, sliced), [((rows, columns), F32), (table, F32)], "Vss", [], 1 << 20, 1 << 20,
-        rho, rank, centers,
-    )
-    sibling = swap(send, 1, light_n)
-    sums = keep + sibling
-    near, far, red, green, blue = call(
-        functools.partial(pre_kernel, samples, rows, 256), [(whole, F32)] * 5, "VVVVV",
-        [pltpu.VMEM(whole, F32)], 1 << 20, 12 << 20, rho, total, light, view_rate, table,
-    )
-    mine, other = halves_below(keep, sibling, sums, 1, light_n)
+    *sums, table, rho = call(
+        functools.partial(sums_kernel, rows, places, sliced),
+        [((n, columns), F32) for n in sizes] + [(table, F32), (whole, jnp.bfloat16)], "AAA",
+        [pltpu.VMEM((samples, columns), F32), pltpu.SMEM(rank.shape, jnp.int32), pltpu.SMEM(centers.shape, F32), pltpu.SemaphoreType.DMA((3,))],
+        1 << 20, 1 << 20, rho, rank, centers,
+    )
+    if light_n == 4:
+        pieces = lower_of_four(*sums)
+        assemble = straight_below, crossed_below
+    else:
+        below = lower(sums[0], 1, light_n)
+        pieces = [below[2 * few : 2 * few + many]], [below[: 2 * few], below[2 * few + many :]]
+        assemble = whole_below, whole_below
+    near, far, red, green, blue, total = call(
+        functools.partial(pre_kernel, samples, rows, 256), [(whole, F32)] * 5 + [((rows, columns), F32)], "VVVV",
+        [pltpu.VMEM(whole, F32)], 1 << 20, 12 << 20, rho, light, view_rate, table,
+    )
     place = lax.axis_index("depth")
     rate = lax.dynamic_slice_in_dim(view_rate, place * own, own, axis=1)
     packed = total
-    for second, below in enumerate((mine, other)):
+    late = 2 * few + many
+    runs = ((2 * few, late, many),), ((0, 0, 2 * few), (late, 2 * few, many))
+    if light_n != 4:
+        runs = ((2 * few, 2 * few, many),), ((0, 0, 2 * few), (late, late, many))
+    for second in range(2):
         (packed,) = call(
-            functools.partial(post_kernel, rows, second, sliced), [((2, columns // (2 * LANES), 7, rows, LANES), F32)], "VVVVVVVVV",
-            [pltpu.VMEM(part, F32)], 1 << 10, 1 << 10,
-            below, light, table, near, far, red, green, blue, packed,
+            functools.partial(post_kernel, rows, second, runs[second], sliced, assemble[second]),
+            [((2, columns // (2 * LANES), 7, rows, LANES), F32)], "V" * (8 + len(pieces[second])),
+            [pltpu.VMEM((sum(run[2] for run in runs[second]), columns), F32)], 1 << 10, 1 << 10,
+            light, table, near, far, red, green, blue, packed, *pieces[second],
         )
     if sliced:
         def send_to(x, stride):

time: 31.3 us -> 30.6 us (0.978)
  starting transfers between devices: 10.1 us -> 14.8 us
  waiting for transfers between devices: 13.5 us -> 9.91 us
  Pallas kernels: 6.78 us -> 4.93 us
    ppermute x3 -> x7, starting transfers between devices: 6.49 us -> 11.2 us  [swap(): return lax.ppermute(x, 'light', [(i, i ^ stride) for i in range(n)])]
    ppermute x3 -> x7, waiting for transfers between devices: 8.67 us -> 4.98 us  [swap(): return lax.ppermute(x, 'light', [(i, i ^ stride) for i in range(n)])]
    pallas_call x7, Pallas kernels: 6.78 us -> 4.93 us  [call(): pl.pallas_call(kernel, out_shape=tuple((pltpu.VMEM(o, t) for o, t in outs...]
    unnamed x9 -> x5, local copies, waits for them, and re-layouts: 0.63 us -> 0.62 us
  transfers between devices with their start and end apart: 7 -> 11, of which waited for: 7 -> 8; matrix products, arithmetic and copies ran while one was open for 0% -> 0% of each run, Pallas kernels for 16% -> 9%
where the time goes in v5:
time: 30.6 us; the launch traced here: 30.4 us
  starting transfers between devices  14.8 us (48%)
  waiting for transfers between devices  9.91 us (32%)
  Pallas kernels  4.93 us (16%)
  local copies, waits for them, and re-layouts  0.65 us (2%)
    ppermute x7, starting transfers between devices, swap(): return lax.ppermute(x, 'light', [(i, i ^ stride) for i in range(n)])  11.2 us
    ppermute x7, waiting for transfers between devices, swap(): return lax.ppermute(x, 'light', [(i, i ^ stride) for i in range(n)])  4.98 us
    ppermute x4, waiting for transfers between devices, send_to(): return lax.ppermute(x, 'depth', [(i, i ^ stride) for i in range(depth_n)])  4.93 us
    pallas_call x7, Pallas kernels, call(): pl.pallas_call(kernel, out_shape=tuple((pltpu.VMEM(o, t) for o, t in outs...  4.93 us
    ppermute x4, starting transfers between devices, send_to(): return lax.ppermute(x, 'depth', [(i, i ^ stride) for i in range(depth_n)])  3.62 us
    unnamed x5, local copies, waits for them, and re-layouts  0.62 us
  transfers between devices with their start and end apart: 11, of which 8 were waited for; matrix products, arithmetic and copies ran while one was open for 0% of the time, Pallas kernels for 9%

profile of v5, /device:TPU:0, one launch (start us, length us, event | category | flops | bytes accessed | tf_op | source)
XLA Modules:
  0.0 30.4 jit_solution(17709093614121547590)
XLA Ops:
  0.0 1.6 %shard_map.55 = (f32[24,1024]{1,0:T(8,128)S(1)}, f32[24,1024]{1,0:T(8,128)S(1)}, f32[8,1024]{1,0:T(8,128)S(1)}, f32[8,1024]{1,0:T(8,128)S(1)}, f32[24,128]{1,0:T(8,128)S(1)}, /*index=5*/bf16[512,1024]{1,0:T(8,128)(2,1)S(1)}) custom-call(bf16[512,1024]{1,0:T(8,128)(2,1)} %bitcast.13, s32[2,8]{1,0:T(2,128)} %rank_hbm.1, f32[3]{0:T(128)} %center_hbm.1), custom_call_target="tpu_custom_call" | custom-call | flops 1048576 | bytes 1048576 | tf_op jit(solution)/shard_map/pallas_call | solution.py:181
  1.6 3.1 %collective-permute-start = (f32[24,1024]{1,0:T(8,128)S(1)}, f32[24,1024]{1,0:T(8,128)S(1)}, u32[]{:S(2)}, u32[]{:S(2)}) collective-permute-start(f32[24,1024]{1,0:T(8,128)S(1)} %get-tuple-element.30), channel_id=1, source_target_pairs={{0,1},{1,0},{2,3},{3,2},{4,5},{5,4},{6,7},{7,6},{8,9},{9,8},{10,11... | collective-permute-start | bytes 294920 | tf_op jit(solution)/shard_map/ppermute | solution.py:271
  4.7 2.5 %collective-permute-start.3 = (f32[8,1024]{1,0:T(8,128)S(1)}, f32[8,1024]{1,0:T(8,128)S(1)}, u32[]{:S(2)}, u32[]{:S(2)}) collective-permute-start(f32[8,1024]{1,0:T(8,128)S(1)} %get-tuple-element.31.cross_ref), channel_id=1, source_target_pairs={{0,3},{1,2},{2,1},{3,0},{4,7},{5,6},{6,5},{7,4},{8,11},{9,10},{10,... | collective-permute-start | bytes 98312 | tf_op jit(solution)/shard_map/ppermute | solution.py:271
  7.1 0.1 collective-permute-start.2
  7.2 0.2 collective-permute-done.given_ref.refs_1_
  7.5 3.2 %collective-permute-start.1 = (f32[24,1024]{1,0:T(8,128)S(1)}, f32[24,1024]{1,0:T(8,128)S(1)}, u32[]{:S(2)}, u32[]{:S(2)}) collective-permute-start(f32[24,1024]{1,0:T(8,128)S(1)} %get-tuple-element.32), channel_id=1, source_target_pairs={{0,2},{1,3},{2,0},{3,1},{4,6},{5,7},{6,4},{7,5},{8,10},{9,11},{10,... | collective-permute-start | bytes 294920 | tf_op jit(solution)/shard_map/ppermute | solution.py:271
  10.7 1.2 %collective-permute-start.5 = (f32[24,1024]{1,0:T(8,128)S(1)}, f32[24,1024]{1,0:T(8,128)S(1)}, u32[]{:S(2)}, u32[]{:S(2)}) collective-permute-start(f32[24,1024]{1,0:T(8,128)S(1)} %get-tuple-element.32), channel_id=1, source_target_pairs={{0,3},{1,2},{2,1},{3,0},{4,7},{5,6},{6,5},{7,4},{8,11},{9,10},{10,... | collective-permute-start | bytes 294920 | tf_op jit(solution)/shard_map/ppermute | solution.py:271
  11.8 0.0 copy-start
  11.8 0.0 copy-start.1
  11.9 0.5 %collective-permute-start.6 = (f32[32,1024]{1,0:T(8,128)S(1)}, f32[32,1024]{1,0:T(8,128)S(1)}, u32[]{:S(2)}, u32[]{:S(2)}) collective-permute-start(f32[32,1024]{1,0:T(8,128)S(1)} %get-tuple-element.36), channel_id=1, source_target_pairs={{0,1},{1,0},{2,3},{3,2},{4,5},{5,4},{6,7},{7,6},{8,9},{9,8},{10,11... | collective-permute-start | bytes 393224 | tf_op jit(solution)/shard_map/ppermute | solution.py:271
  12.3 0.0 collective-permute-done.3.across_ref
  12.3 1.0 %collective-permute-done.2.straight_ref = f32[8,1024]{1,0:T(8,128)S(1)} collective-permute-done((f32[8,1024]{1,0:T(8,128)S(1)}, f32[8,1024]{1,0:T(8,128)S(1)}, u32[]{:S(2)}, u32[]{:S(2)}) %collective-permute-start.2) | collective-permute-done | bytes 32800 | tf_op jit(solution)/shard_map/ppermute | solution.py:271
  13.3 0.7 %collective-permute-start.4 = (f32[8,1024]{1,0:T(8,128)S(1)}, f32[8,1024]{1,0:T(8,128)S(1)}, u32[]{:S(2)}, u32[]{:S(2)}) collective-permute-start(f32[8,1024]{1,0:T(8,128)S(1)} %get-tuple-element.35), channel_id=1, source_target_pairs={{0,1},{1,0},{2,3},{3,2},{4,5},{5,4},{6,7},{7,6},{8,9},{9,8},{10,11... | collective-permute-start | bytes 98312 | tf_op jit(solution)/shard_map/ppermute | solution.py:271
  14.0 0.0 copy-done
  14.0 0.0 copy-done.1
  14.0 2.2 %shard_map.56 = (f32[512,1024]{1,0:T(8,128)S(1)}, f32[512,1024]{1,0:T(8,128)S(1)}, f32[512,1024]{1,0:T(8,128)S(1)}, f32[512,1024]{1,0:T(8,128)S(1)}, f32[512,1024]{1,0:T(8,128)S(1)}, /*index=5*/f32[8,1024]{1,0:T(8,128)S(1)}) custom-call(bf16[512,1024]{1,0:T(8,128)(2,1)S(1)} %get-tuple-element.22.rho_ref, f32[1,1024]{1,0:T(1,128)S(1)} %bitcast.10, ...), custom_call_target="tpu_custom_call" | custom-call | flops 1048576 | bytes 12582912 | tf_op jit(solution)/shard_map/pallas_call | solution.py:181
  16.2 2.3 %collective-permute-done.1.refs_0_ = f32[24,1024]{1,0:T(8,128)S(1)} collective-permute-done((f32[24,1024]{1,0:T(8,128)S(1)}, f32[24,1024]{1,0:T(8,128)S(1)}, u32[]{:S(2)}, u32[]{:S(2)}) %collective-permute-start.1) | collective-permute-done | bytes 98336 | tf_op jit(solution)/shard_map/ppermute | solution.py:271
  18.5 0.4 %shard_map.58.rest_ref = f32[2,4,7,8,128]{4,3,2,1,0:T(8,128)S(1)} custom-call(f32[1,1024]{1,0:T(1,128)S(1)} %bitcast.11, f32[24,128]{1,0:T(8,128)S(1)} %get-tuple-element.21.table_ref, f32[512,1024]{1,0:T(8,128)S(1)} %get-tuple-element.23.near_ref, f32[512,1024]{1,0:T(8,128)S(1)} %get-tuple-element.24.far_ref, f32[512,1024]{1,0:T(8,128)S(1)} %get-tuple-element.25.red_ref, ...), custom_call_target="tpu_custom_call" | custom-call | flops 1024 | bytes 1024 | tf_op jit(solution)/shard_map/pallas_call | solution.py:181
  18.9 1.5 %collective-permute-done.4.refs_1_ = f32[8,1024]{1,0:T(8,128)S(1)} collective-permute-done((f32[8,1024]{1,0:T(8,128)S(1)}, f32[8,1024]{1,0:T(8,128)S(1)}, u32[]{:S(2)}, u32[]{:S(2)}) %collective-permute-start.4) | collective-permute-done | bytes 32800 | tf_op jit(solution)/shard_map/ppermute | solution.py:271
  20.4 0.0 collective-permute-done.5.refs_2_
  20.4 0.0 collective-permute-done.6.refs_3_
  20.4 0.6 %shard_map.60.own_ref = f32[2,4,7,8,128]{4,3,2,1,0:T(8,128)S(1)} custom-call(f32[1,1024]{1,0:T(1,128)S(1)} %bitcast.12, f32[24,128]{1,0:T(8,128)S(1)} %get-tuple-element.21.table_ref, f32[512,1024]{1,0:T(8,128)S(1)} %get-tuple-element.23.near_ref, f32[512,1024]{1,0:T(8,128)S(1)} %get-tuple-element.24.far_ref, f32[512,1024]{1,0:T(8,128)S(1)} %get-tuple-element.25.red_ref, ...), custom_call_target="tpu_custom_call" | custom-call | flops 1024 | bytes 1024 | tf_op jit(solution)/shard_map/pallas_call | solution.py:181
  21.1 0.1 collective-permute-start.7
  21.2 1.3 %collective-permute-done.7.sibling_ref = f32[4,7,8,128]{3,2,1,0:T(8,128)S(1)} collective-permute-done((f32[4,7,8,128]{3,2,1,0:T(8,128)S(1)}, f32[4,7,8,128]{3,2,1,0:T(8,128)S(1)}, u32[]{:S(2)}, u32[]{:S(2)}) %collective-permute-start.7) | collective-permute-done | bytes 114720 | tf_op jit(solution)/shard_map/ppermute | solution.py:349
  22.5 2.5 %collective-permute-start.10 = (f32[2,7,8,128]{3,2,1,0:T(8,128)S(1)}, f32[2,7,8,128]{3,2,1,0:T(8,128)S(1)}, u32[]{:S(2)}, u32[]{:S(2)}) collective-permute-start(f32[2,7,8,128]{3,2,1,0:T(8,128)S(1)} %pad_maximum_fusion.2), channel_id=1, source_target_pairs={{0,24},{4,28},{8,16},{12,20},{16,8},{20,12},{24,0},{28,4},{1,25},{... | collective-permute-start | bytes 172040 | tf_op jit(solution)/shard_map/ppermute | solution.py:349
  25.0 0.5 %collective-permute-start.9 = (f32[2,7,8,128]{3,2,1,0:T(8,128)S(1)}, f32[2,7,8,128]{3,2,1,0:T(8,128)S(1)}, u32[]{:S(2)}, u32[]{:S(2)}) collective-permute-start(f32[2,7,8,128]{3,2,1,0:T(8,128)S(1)} %pad_maximum_fusion.1), channel_id=1, source_target_pairs={{0,16},{4,20},{8,24},{12,28},{16,0},{20,4},{24,8},{28,12},{1,17},{... | collective-permute-start | bytes 172040 | tf_op jit(solution)/shard_map/ppermute | solution.py:349
  25.5 0.5 %collective-permute-start.8 = (f32[2,7,8,128]{3,2,1,0:T(8,128)S(1)}, f32[2,7,8,128]{3,2,1,0:T(8,128)S(1)}, u32[]{:S(2)}, u32[]{:S(2)}) collective-permute-start(f32[2,7,8,128]{3,2,1,0:T(8,128)S(1)} %pad_maximum_fusion), channel_id=1, source_target_pairs={{0,8},{4,12},{8,0},{12,4},{16,24},{20,28},{24,16},{28,20},{1,9},{5... | collective-permute-start | bytes 172040 | tf_op jit(solution)/shard_map/ppermute | solution.py:349
  26.1 1.6 %collective-permute-done.10.refs_2_ = f32[2,7,8,128]{3,2,1,0:T(8,128)S(1)} collective-permute-done((f32[2,7,8,128]{3,2,1,0:T(8,128)S(1)}, f32[2,7,8,128]{3,2,1,0:T(8,128)S(1)}, u32[]{:S(2)}, u32[]{:S(2)}) %collective-permute-start.10) | collective-permute-done | bytes 57376 | tf_op jit(solution)/shard_map/ppermute | solution.py:349
  27.7 1.5 %collective-permute-done.9.refs_1_ = f32[2,7,8,128]{3,2,1,0:T(8,128)S(1)} collective-permute-done((f32[2,7,8,128]{3,2,1,0:T(8,128)S(1)}, f32[2,7,8,128]{3,2,1,0:T(8,128)S(1)}, u32[]{:S(2)}, u32[]{:S(2)}) %collective-permute-start.9) | collective-permute-done | bytes 57376 | tf_op jit(solution)/shard_map/ppermute | solution.py:349
  29.2 0.5 %collective-permute-done.8.refs_0_ = f32[2,7,8,128]{3,2,1,0:T(8,128)S(1)} collective-permute-done((f32[2,7,8,128]{3,2,1,0:T(8,128)S(1)}, f32[2,7,8,128]{3,2,1,0:T(8,128)S(1)}, u32[]{:S(2)}, u32[]{:S(2)}) %collective-permute-start.8) | collective-permute-done | bytes 57376 | tf_op jit(solution)/shard_map/ppermute | solution.py:349
  29.7 0.1 shard_map.61
  29.8 0.6 %copy.6 = f32[2,4,8,128]{3,2,1,0:T(8,128)} copy(f32[2,4,8,128]{3,2,1,0:T(8,128)S(1)} %shard_map.61) | data formatting | bytes 65536
  (9 shorter events, 0.1 us)
Async XLA Ops:
  1.6 5.9 %collective-permute-start = (f32[24,1024]{1,0:T(8,128)S(1)}, f32[24,1024]{1,0:T(8,128)S(1)}, u32[]{:S(2)}, u32[]{:S(2)}) collective-permute-start(f32[24,1024]{1,0:T(8,128)S(1)} %get-tuple-element.30), channel_id=1, source_target_pairs={{0,1},{1,0},{2,3},{3,2},{4,5},{5,4},{6,7},{7,6},{8,9},{9,8},{10,11... | collective-permute-start | bytes 294920 | tf_op jit(solution)/shard_map/ppermute | solution.py:271
  4.7 7.7 %collective-permute-start.3 = (f32[8,1024]{1,0:T(8,128)S(1)}, f32[8,1024]{1,0:T(8,128)S(1)}, u32[]{:S(2)}, u32[]{:S(2)}) collective-permute-start(f32[8,1024]{1,0:T(8,128)S(1)} %get-tuple-element.31.cross_ref), channel_id=1, source_target_pairs={{0,3},{1,2},{2,1},{3,0},{4,7},{5,6},{6,5},{7,4},{8,11},{9,10},{10,... | collective-permute-start | bytes 98312 | tf_op jit(solution)/shard_map/ppermute | solution.py:271
  7.1 6.2 %collective-permute-start.2 = (f32[8,1024]{1,0:T(8,128)S(1)}, f32[8,1024]{1,0:T(8,128)S(1)}, u32[]{:S(2)}, u32[]{:S(2)}) collective-permute-start(f32[8,1024]{1,0:T(8,128)S(1)} %get-tuple-element.33.same_ref), channel_id=1, source_target_pairs={{0,2},{1,3},{2,0},{3,1},{4,6},{5,7},{6,4},{7,5},{8,10},{9,11},{10,... | collective-permute-start | bytes 98312 | tf_op jit(solution)/shard_map/ppermute | solution.py:271
  7.5 11.0 %collective-permute-start.1 = (f32[24,1024]{1,0:T(8,128)S(1)}, f32[24,1024]{1,0:T(8,128)S(1)}, u32[]{:S(2)}, u32[]{:S(2)}) collective-permute-start(f32[24,1024]{1,0:T(8,128)S(1)} %get-tuple-element.32), channel_id=1, source_target_pairs={{0,2},{1,3},{2,0},{3,1},{4,6},{5,7},{6,4},{7,5},{8,10},{9,11},{10,... | collective-permute-start | bytes 294920 | tf_op jit(solution)/shard_map/ppermute | solution.py:271
  10.7 9.8 %collective-permute-start.5 = (f32[24,1024]{1,0:T(8,128)S(1)}, f32[24,1024]{1,0:T(8,128)S(1)}, u32[]{:S(2)}, u32[]{:S(2)}) collective-permute-start(f32[24,1024]{1,0:T(8,128)S(1)} %get-tuple-element.32), channel_id=1, source_target_pairs={{0,3},{1,2},{2,1},{3,0},{4,7},{5,6},{6,5},{7,4},{8,11},{9,10},{10,... | collective-permute-start | bytes 294920 | tf_op jit(solution)/shard_map/ppermute | solution.py:271
  11.8 2.1 %copy-start = (f32[1024]{0:T(1024)S(1)}, f32[1024]{0:T(1024)}, u32[]{:S(2)}) copy-start(f32[1024]{0:T(1024)} %param.6) | copy-start | bytes 12292
  11.8 2.1 %copy-start.1 = (f32[2,1024]{1,0:T(2,128)S(1)}, f32[2,1024]{1,0:T(2,128)}, u32[]{:S(2)}) copy-start(f32[2,1024]{1,0:T(2,128)} %view_ref.1) | copy-start | bytes 24580
  11.9 8.6 %collective-permute-start.6 = (f32[32,1024]{1,0:T(8,128)S(1)}, f32[32,1024]{1,0:T(8,128)S(1)}, u32[]{:S(2)}, u32[]{:S(2)}) collective-permute-start(f32[32,1024]{1,0:T(8,128)S(1)} %get-tuple-element.36), channel_id=1, source_target_pairs={{0,1},{1,0},{2,3},{3,2},{4,5},{5,4},{6,7},{7,6},{8,9},{9,8},{10,11... | collective-permute-start | bytes 393224 | tf_op jit(solution)/shard_map/ppermute | solution.py:271
  13.3 7.1 %collective-permute-start.4 = (f32[8,1024]{1,0:T(8,128)S(1)}, f32[8,1024]{1,0:T(8,128)S(1)}, u32[]{:S(2)}, u32[]{:S(2)}) collective-permute-start(f32[8,1024]{1,0:T(8,128)S(1)} %get-tuple-element.35), channel_id=1, source_target_pairs={{0,1},{1,0},{2,3},{3,2},{4,5},{5,4},{6,7},{7,6},{8,9},{9,8},{10,11... | collective-permute-start | bytes 98312 | tf_op jit(solution)/shard_map/ppermute | solution.py:271
  21.1 1.4 %collective-permute-start.7 = (f32[4,7,8,128]{3,2,1,0:T(8,128)S(1)}, f32[4,7,8,128]{3,2,1,0:T(8,128)S(1)}, u32[]{:S(2)}, u32[]{:S(2)}) collective-permute-start(f32[4,7,8,128]{3,2,1,0:T(8,128)S(1)} %slice_bitcast_fusion), channel_id=1, source_target_pairs={{0,4},{4,0},{8,12},{12,8},{16,20},{20,16},{24,28},{28,24},{1,5},{5... | collective-permute-start | bytes 344072 | tf_op jit(solution)/shard_map/ppermute | solution.py:349
  22.5 5.2 %collective-permute-start.10 = (f32[2,7,8,128]{3,2,1,0:T(8,128)S(1)}, f32[2,7,8,128]{3,2,1,0:T(8,128)S(1)}, u32[]{:S(2)}, u32[]{:S(2)}) collective-permute-start(f32[2,7,8,128]{3,2,1,0:T(8,128)S(1)} %pad_maximum_fusion.2), channel_id=1, source_target_pairs={{0,24},{4,28},{8,16},{12,20},{16,8},{20,12},{24,0},{28,4},{1,25},{... | collective-permute-start | bytes 172040 | tf_op jit(solution)/shard_map/ppermute | solution.py:349
  25.0 4.2 %collective-permute-start.9 = (f32[2,7,8,128]{3,2,1,0:T(8,128)S(1)}, f32[2,7,8,128]{3,2,1,0:T(8,128)S(1)}, u32[]{:S(2)}, u32[]{:S(2)}) collective-permute-start(f32[2,7,8,128]{3,2,1,0:T(8,128)S(1)} %pad_maximum_fusion.1), channel_id=1, source_target_pairs={{0,16},{4,20},{8,24},{12,28},{16,0},{20,4},{24,8},{28,12},{1,17},{... | collective-permute-start | bytes 172040 | tf_op jit(solution)/shard_map/ppermute | solution.py:349
  25.5 4.2 %collective-permute-start.8 = (f32[2,7,8,128]{3,2,1,0:T(8,128)S(1)}, f32[2,7,8,128]{3,2,1,0:T(8,128)S(1)}, u32[]{:S(2)}, u32[]{:S(2)}) collective-permute-start(f32[2,7,8,128]{3,2,1,0:T(8,128)S(1)} %pad_maximum_fusion), channel_id=1, source_target_pairs={{0,8},{4,12},{8,0},{12,4},{16,24},{20,28},{24,16},{28,20},{1,9},{5... | collective-permute-start | bytes 172040 | tf_op jit(solution)/shard_map/ppermute | solution.py:349

commit v6 on v5

--- a/solution.py
+++ b/solution.py
@@ -52,19 +52,24 @@
         out_ref[...] = sums_ref[pl.ds(first, out_ref.shape[0]), :]
 
 
-def pair_kernel(hold_ref, given_ref, cross_ref, pair_ref, late_ref):
-    many = hold_ref.shape[0]
+def pair_kernel(hold_ref, given_ref, pair_ref):
     pair_ref[...] = hold_ref[...] + given_ref[...]
-    late_ref[:many, :] = hold_ref[...]
-    late_ref[many:, :] = cross_ref[...]
 
 
 def upper_kernel(straight_ref, across_ref, same_ref, cross_ref, below_ref, send_ref):
     me = lax.axis_index("light")
+    odd = me % 2 == 1
     few = same_ref.shape[0]
     below = jnp.where(me >= 2, straight_ref[...] + across_ref[...], 0.0)
     below_ref[...] = below
-    send_ref[:few, :] = below + jnp.where(me % 2 == 1, 0.0, same_ref[...])
+    send_ref[:few, :] = below + jnp.where(odd, 0.0, same_ref[...])
+    send_ref[few:, :] = cross_ref[...]
+
+
+def late_kernel(late_ref, send_ref, add_ref, out_ref):
+    odd = lax.axis_index("light") % 2 == 1
+    add_ref[...] = jnp.where(odd, late_ref[...], 0.0)
+    out_ref[...] = send_ref[...]
 
 
 def pre_kernel(
@@ -123,12 +128,12 @@
 
 def crossed_below(refs, below_ref):
     mine, other, cross, late = (ref[...] for ref in refs)
-    few, many = mine.shape[0], cross.shape[0]
+    few = mine.shape[0]
     me = lax.axis_index("light")
     odd = me % 2 == 1
     below_ref[:few, :] = jnp.where(odd, other[:few], mine)
-    below_ref[few : 2 * few, :] = jnp.where(odd, mine + late[many:], other[:few])
-    below_ref[2 * few :, :] = jnp.where(me >= 2, cross, 0.0) + jnp.where(odd, late[:many], 0.0)
+    below_ref[few : 2 * few, :] = jnp.where(odd, mine + other[few:], other[:few])
+    below_ref[2 * few :, :] = jnp.where(me >= 2, cross, 0.0) + late
 
 
 def whole_below(refs, below_ref):
@@ -290,14 +295,14 @@
     given = swap(give, 1, 4)
     straight, across = swap(same, 2, 4), swap(cross, 3, 4)
     columns = same.shape[1]
-    pair, late = call(
-        pair_kernel, [(hold.shape, F32), ((hold.shape[0] + cross.shape[0], columns), F32)], "VVV", [], 1 << 10, 1 << 10, hold, given, cross
-    )
+    late = swap(hold, 1, 4)
+    (pair,) = call(pair_kernel, [(hold.shape, F32)], "VV", [], 1 << 10, 1 << 10, hold, given)
     from_same, from_cross = swap(pair, 2, 4), swap(pair, 3, 4)
-    late = swap(late, 1, 4)
+    sent = 2 * same.shape[0], columns
     mine, send = call(
-        upper_kernel, [(same.shape, F32), ((same.shape[0], columns), F32)], "VVVV", [], 1 << 34, 1 << 10, straight, across, same, cross
-    )
+        upper_kernel, [(same.shape, F32), (sent, F32)], "VVVV", [], 1 << 30, 1 << 10, straight, across, same, cross
+    )
+    late, send = call(late_kernel, [(late.shape, F32), (sent, F32)], "VV", [], 1 << 10, 1 << 10, late, send)
     other = swap(send, 1, 4)
     return (from_same, given), (mine, other, from_cross, late)
 

time: 30.6 us -> 29.7 us (0.971)
  starting transfers between devices: 14.8 us -> 13.9 us
    ppermute x7, starting transfers between devices: 11.2 us -> 10.2 us  [swap(): return lax.ppermute(x, 'light', [(i, i ^ stride) for i in range(n)])]
    pallas_call x7 -> x8, Pallas kernels: 4.93 us -> 4.96 us  [call(): pl.pallas_call(kernel, out_shape=tuple((pltpu.VMEM(o, t) for o, t in outs...]
  transfers between devices with their start and end apart: 11 -> 11, of which waited for: 8 -> 7; matrix products, arithmetic and copies ran while one was open for 0% -> 0% of each run, Pallas kernels for 9% -> 9%
where the time goes in v6:
time: 29.7 us; the launch traced here: 29.5 us
  starting transfers between devices  13.9 us (47%)
  waiting for transfers between devices  9.9 us (33%)
  Pallas kernels  4.96 us (17%)
  local copies, waits for them, and re-layouts  0.66 us (2%)
    ppermute x7, starting transfers between devices, swap(): return lax.ppermute(x, 'light', [(i, i ^ stride) for i in range(n)])  10.2 us
    ppermute x7, waiting for transfers between devices, swap(): return lax.ppermute(x, 'light', [(i, i ^ stride) for i in range(n)])  4.96 us
    pallas_call x8, Pallas kernels, call(): pl.pallas_call(kernel, out_shape=tuple((pltpu.VMEM(o, t) for o, t in outs...  4.96 us
    ppermute x4, waiting for transfers between devices, send_to(): return lax.ppermute(x, 'depth', [(i, i ^ stride) for i in range(depth_n)])  4.94 us
    ppermute x4, starting transfers between devices, send_to(): return lax.ppermute(x, 'depth', [(i, i ^ stride) for i in range(depth_n)])  3.62 us
    unnamed x5, local copies, waits for them, and re-layouts  0.63 us
  transfers between devices with their start and end apart: 11, of which 7 were waited for; matrix products, arithmetic and copies ran while one was open for 0% of the time, Pallas kernels for 9%

profile of v6, /device:TPU:0, one launch (start us, length us, event | category | flops | bytes accessed | tf_op | source)
XLA Modules:
  0.0 29.5 jit_solution(1731559343431480534)
XLA Ops:
  0.0 1.6 %shard_map.55 = (f32[24,1024]{1,0:T(8,128)S(1)}, f32[24,1024]{1,0:T(8,128)S(1)}, f32[8,1024]{1,0:T(8,128)S(1)}, f32[8,1024]{1,0:T(8,128)S(1)}, f32[24,128]{1,0:T(8,128)S(1)}, /*index=5*/bf16[512,1024]{1,0:T(8,128)(2,1)S(1)}) custom-call(bf16[512,1024]{1,0:T(8,128)(2,1)} %bitcast.13, s32[2,8]{1,0:T(2,128)} %rank_hbm.1, f32[3]{0:T(128)} %center_hbm.1), custom_call_target="tpu_custom_call" | custom-call | flops 1048576 | bytes 1048576 | tf_op jit(solution)/shard_map/pallas_call | solution.py:186
  1.6 3.1 %collective-permute-start = (f32[24,1024]{1,0:T(8,128)S(1)}, f32[24,1024]{1,0:T(8,128)S(1)}, u32[]{:S(2)}, u32[]{:S(2)}) collective-permute-start(f32[24,1024]{1,0:T(8,128)S(1)} %get-tuple-element.30), channel_id=1, source_target_pairs={{0,1},{1,0},{2,3},{3,2},{4,5},{5,4},{6,7},{7,6},{8,9},{9,8},{10,11... | collective-permute-start | bytes 294920 | tf_op jit(solution)/shard_map/ppermute | solution.py:276
  4.7 2.6 %collective-permute-start.2 = (f32[8,1024]{1,0:T(8,128)S(1)}, f32[8,1024]{1,0:T(8,128)S(1)}, u32[]{:S(2)}, u32[]{:S(2)}) collective-permute-start(f32[8,1024]{1,0:T(8,128)S(1)} %get-tuple-element.31.same_ref), channel_id=1, source_target_pairs={{0,2},{1,3},{2,0},{3,1},{4,6},{5,7},{6,4},{7,5},{8,10},{9,11},{10,... | collective-permute-start | bytes 98312 | tf_op jit(solution)/shard_map/ppermute | solution.py:276
  7.2 0.0 collective-permute-start.3
  7.2 0.9 %collective-permute-start.4 = (f32[24,1024]{1,0:T(8,128)S(1)}, f32[24,1024]{1,0:T(8,128)S(1)}, u32[]{:S(2)}, u32[]{:S(2)}) collective-permute-start(f32[24,1024]{1,0:T(8,128)S(1)} %get-tuple-element.29.hold_ref), channel_id=1, source_target_pairs={{0,1},{1,0},{2,3},{3,2},{4,5},{5,4},{6,7},{7,6},{8,9},{9,8},{10,11... | collective-permute-start | bytes 294920 | tf_op jit(solution)/shard_map/ppermute | solution.py:276
  8.1 0.0 collective-permute-done.given_ref.refs_1_
  8.2 0.0 copy-start
  8.2 0.0 copy-start.1
  8.2 3.6 %collective-permute-start.1 = (f32[24,1024]{1,0:T(8,128)S(1)}, f32[24,1024]{1,0:T(8,128)S(1)}, u32[]{:S(2)}, u32[]{:S(2)}) collective-permute-start(f32[24,1024]{1,0:T(8,128)S(1)} %shard_map.57), channel_id=1, source_target_pairs={{0,2},{1,3},{2,0},{3,1},{4,6},{5,7},{6,4},{7,5},{8,10},{9,11},{10,... | collective-permute-start | bytes 294920 | tf_op jit(solution)/shard_map/ppermute | solution.py:276
  11.7 0.0 collective-permute-start.6
  11.8 0.0 collective-permute-done.2.straight_ref
  11.8 1.7 %collective-permute-done.3.across_ref = f32[8,1024]{1,0:T(8,128)S(1)} collective-permute-done((f32[8,1024]{1,0:T(8,128)S(1)}, f32[8,1024]{1,0:T(8,128)S(1)}, u32[]{:S(2)}, u32[]{:S(2)}) %collective-permute-start.3) | collective-permute-done | bytes 32800 | tf_op jit(solution)/shard_map/ppermute | solution.py:276
  13.5 0.1 collective-permute-done.4.late_ref
  13.6 0.1 collective-permute-start.5
  13.7 0.0 copy-done
  13.7 0.0 copy-done.1
  13.7 2.2 %shard_map.56 = (f32[512,1024]{1,0:T(8,128)S(1)}, f32[512,1024]{1,0:T(8,128)S(1)}, f32[512,1024]{1,0:T(8,128)S(1)}, f32[512,1024]{1,0:T(8,128)S(1)}, f32[512,1024]{1,0:T(8,128)S(1)}, /*index=5*/f32[8,1024]{1,0:T(8,128)S(1)}) custom-call(bf16[512,1024]{1,0:T(8,128)(2,1)S(1)} %get-tuple-element.22.rho_ref, f32[1,1024]{1,0:T(1,128)S(1)} %bitcast.10, ...), custom_call_target="tpu_custom_call" | custom-call | flops 1048576 | bytes 12582912 | tf_op jit(solution)/shard_map/pallas_call | solution.py:186
  16.0 3.1 %collective-permute-done.1.refs_0_ = f32[24,1024]{1,0:T(8,128)S(1)} collective-permute-done((f32[24,1024]{1,0:T(8,128)S(1)}, f32[24,1024]{1,0:T(8,128)S(1)}, u32[]{:S(2)}, u32[]{:S(2)}) %collective-permute-start.1) | collective-permute-done | bytes 98336 | tf_op jit(solution)/shard_map/ppermute | solution.py:276
  19.1 0.4 %shard_map.58.rest_ref = f32[2,4,7,8,128]{4,3,2,1,0:T(8,128)S(1)} custom-call(f32[1,1024]{1,0:T(1,128)S(1)} %bitcast.11, f32[24,128]{1,0:T(8,128)S(1)} %get-tuple-element.21.table_ref, f32[512,1024]{1,0:T(8,128)S(1)} %get-tuple-element.23.near_ref, f32[512,1024]{1,0:T(8,128)S(1)} %get-tuple-element.24.far_ref, f32[512,1024]{1,0:T(8,128)S(1)} %get-tuple-element.25.red_ref, ...), custom_call_target="tpu_custom_call" | custom-call | flops 1024 | bytes 1024 | tf_op jit(solution)/shard_map/pallas_call | solution.py:186
  19.5 0.0 collective-permute-done.5.refs_1_
  19.5 0.0 collective-permute-done.6.refs_2_
  19.5 0.7 %shard_map.61.own_ref = f32[2,4,7,8,128]{4,3,2,1,0:T(8,128)S(1)} custom-call(f32[1,1024]{1,0:T(1,128)S(1)} %bitcast.12, f32[24,128]{1,0:T(8,128)S(1)} %get-tuple-element.21.table_ref, f32[512,1024]{1,0:T(8,128)S(1)} %get-tuple-element.23.near_ref, f32[512,1024]{1,0:T(8,128)S(1)} %get-tuple-element.24.far_ref, f32[512,1024]{1,0:T(8,128)S(1)} %get-tuple-element.25.red_ref, ...), custom_call_target="tpu_custom_call" | custom-call | flops 1024 | bytes 1024 | tf_op jit(solution)/shard_map/pallas_call | solution.py:186
  20.2 0.1 collective-permute-start.7
  20.3 1.3 %collective-permute-done.7.sibling_ref = f32[4,7,8,128]{3,2,1,0:T(8,128)S(1)} collective-permute-done((f32[4,7,8,128]{3,2,1,0:T(8,128)S(1)}, f32[4,7,8,128]{3,2,1,0:T(8,128)S(1)}, u32[]{:S(2)}, u32[]{:S(2)}) %collective-permute-start.7) | collective-permute-done | bytes 114720 | tf_op jit(solution)/shard_map/ppermute | solution.py:354
  21.6 2.5 %collective-permute-start.10 = (f32[2,7,8,128]{3,2,1,0:T(8,128)S(1)}, f32[2,7,8,128]{3,2,1,0:T(8,128)S(1)}, u32[]{:S(2)}, u32[]{:S(2)}) collective-permute-start(f32[2,7,8,128]{3,2,1,0:T(8,128)S(1)} %pad_maximum_fusion.2), channel_id=1, source_target_pairs={{0,24},{4,28},{8,16},{12,20},{16,8},{20,12},{24,0},{28,4},{1,25},{... | collective-permute-start | bytes 172040 | tf_op jit(solution)/shard_map/ppermute | solution.py:354
  24.1 0.5 %collective-permute-start.9 = (f32[2,7,8,128]{3,2,1,0:T(8,128)S(1)}, f32[2,7,8,128]{3,2,1,0:T(8,128)S(1)}, u32[]{:S(2)}, u32[]{:S(2)}) collective-permute-start(f32[2,7,8,128]{3,2,1,0:T(8,128)S(1)} %pad_maximum_fusion.1), channel_id=1, source_target_pairs={{0,16},{4,20},{8,24},{12,28},{16,0},{20,4},{24,8},{28,12},{1,17},{... | collective-permute-start | bytes 172040 | tf_op jit(solution)/shard_map/ppermute | solution.py:354
  24.6 0.5 %collective-permute-start.8 = (f32[2,7,8,128]{3,2,1,0:T(8,128)S(1)}, f32[2,7,8,128]{3,2,1,0:T(8,128)S(1)}, u32[]{:S(2)}, u32[]{:S(2)}) collective-permute-start(f32[2,7,8,128]{3,2,1,0:T(8,128)S(1)} %pad_maximum_fusion), channel_id=1, source_target_pairs={{0,8},{4,12},{8,0},{12,4},{16,24},{20,28},{24,16},{28,20},{1,9},{5... | collective-permute-start | bytes 172040 | tf_op jit(solution)/shard_map/ppermute | solution.py:354
  25.2 1.6 %collective-permute-done.10.refs_2_ = f32[2,7,8,128]{3,2,1,0:T(8,128)S(1)} collective-permute-done((f32[2,7,8,128]{3,2,1,0:T(8,128)S(1)}, f32[2,7,8,128]{3,2,1,0:T(8,128)S(1)}, u32[]{:S(2)}, u32[]{:S(2)}) %collective-permute-start.10) | collective-permute-done | bytes 57376 | tf_op jit(solution)/shard_map/ppermute | solution.py:354
  26.8 1.5 %collective-permute-done.9.refs_1_ = f32[2,7,8,128]{3,2,1,0:T(8,128)S(1)} collective-permute-done((f32[2,7,8,128]{3,2,1,0:T(8,128)S(1)}, f32[2,7,8,128]{3,2,1,0:T(8,128)S(1)}, u32[]{:S(2)}, u32[]{:S(2)}) %collective-permute-start.9) | collective-permute-done | bytes 57376 | tf_op jit(solution)/shard_map/ppermute | solution.py:354
  28.3 0.5 %collective-permute-done.8.refs_0_ = f32[2,7,8,128]{3,2,1,0:T(8,128)S(1)} collective-permute-done((f32[2,7,8,128]{3,2,1,0:T(8,128)S(1)}, f32[2,7,8,128]{3,2,1,0:T(8,128)S(1)}, u32[]{:S(2)}, u32[]{:S(2)}) %collective-permute-start.8) | collective-permute-done | bytes 57376 | tf_op jit(solution)/shard_map/ppermute | solution.py:354
  28.8 0.1 shard_map.62
  28.9 0.6 %copy.6 = f32[2,4,8,128]{3,2,1,0:T(8,128)} copy(f32[2,4,8,128]{3,2,1,0:T(8,128)S(1)} %shard_map.62) | data formatting | bytes 65536
  (10 shorter events, 0.1 us)
Async XLA Ops:
  1.6 6.6 %collective-permute-start = (f32[24,1024]{1,0:T(8,128)S(1)}, f32[24,1024]{1,0:T(8,128)S(1)}, u32[]{:S(2)}, u32[]{:S(2)}) collective-permute-start(f32[24,1024]{1,0:T(8,128)S(1)} %get-tuple-element.30), channel_id=1, source_target_pairs={{0,1},{1,0},{2,3},{3,2},{4,5},{5,4},{6,7},{7,6},{8,9},{9,8},{10,11... | collective-permute-start | bytes 294920 | tf_op jit(solution)/shard_map/ppermute | solution.py:276
  4.7 7.1 %collective-permute-start.2 = (f32[8,1024]{1,0:T(8,128)S(1)}, f32[8,1024]{1,0:T(8,128)S(1)}, u32[]{:S(2)}, u32[]{:S(2)}) collective-permute-start(f32[8,1024]{1,0:T(8,128)S(1)} %get-tuple-element.31.same_ref), channel_id=1, source_target_pairs={{0,2},{1,3},{2,0},{3,1},{4,6},{5,7},{6,4},{7,5},{8,10},{9,11},{10,... | collective-permute-start | bytes 98312 | tf_op jit(solution)/shard_map/ppermute | solution.py:276
  7.2 6.2 %collective-permute-start.3 = (f32[8,1024]{1,0:T(8,128)S(1)}, f32[8,1024]{1,0:T(8,128)S(1)}, u32[]{:S(2)}, u32[]{:S(2)}) collective-permute-start(f32[8,1024]{1,0:T(8,128)S(1)} %get-tuple-element.32.cross_ref), channel_id=1, source_target_pairs={{0,3},{1,2},{2,1},{3,0},{4,7},{5,6},{6,5},{7,4},{8,11},{9,10},{10,... | collective-permute-start | bytes 98312 | tf_op jit(solution)/shard_map/ppermute | solution.py:276
  7.2 6.4 %collective-permute-start.4 = (f32[24,1024]{1,0:T(8,128)S(1)}, f32[24,1024]{1,0:T(8,128)S(1)}, u32[]{:S(2)}, u32[]{:S(2)}) collective-permute-start(f32[24,1024]{1,0:T(8,128)S(1)} %get-tuple-element.29.hold_ref), channel_id=1, source_target_pairs={{0,1},{1,0},{2,3},{3,2},{4,5},{5,4},{6,7},{7,6},{8,9},{9,8},{10,11... | collective-permute-start | bytes 294920 | tf_op jit(solution)/shard_map/ppermute | solution.py:276
  8.2 5.6 %copy-start = (f32[1024]{0:T(1024)S(1)}, f32[1024]{0:T(1024)}, u32[]{:S(2)}) copy-start(f32[1024]{0:T(1024)} %param.6) | copy-start | bytes 12292
  8.2 5.6 %copy-start.1 = (f32[2,1024]{1,0:T(2,128)S(1)}, f32[2,1024]{1,0:T(2,128)}, u32[]{:S(2)}) copy-start(f32[2,1024]{1,0:T(2,128)} %view_ref.1) | copy-start | bytes 24580
  8.2 10.9 %collective-permute-start.1 = (f32[24,1024]{1,0:T(8,128)S(1)}, f32[24,1024]{1,0:T(8,128)S(1)}, u32[]{:S(2)}, u32[]{:S(2)}) collective-permute-start(f32[24,1024]{1,0:T(8,128)S(1)} %shard_map.57), channel_id=1, source_target_pairs={{0,2},{1,3},{2,0},{3,1},{4,6},{5,7},{6,4},{7,5},{8,10},{9,11},{10,... | collective-permute-start | bytes 294920 | tf_op jit(solution)/shard_map/ppermute | solution.py:276
  11.7 7.8 %collective-permute-start.6 = (f32[24,1024]{1,0:T(8,128)S(1)}, f32[24,1024]{1,0:T(8,128)S(1)}, u32[]{:S(2)}, u32[]{:S(2)}) collective-permute-start(f32[24,1024]{1,0:T(8,128)S(1)} %shard_map.57), channel_id=1, source_target_pairs={{0,3},{1,2},{2,1},{3,0},{4,7},{5,6},{6,5},{7,4},{8,11},{9,10},{10,... | collective-permute-start | bytes 294920 | tf_op jit(solution)/shard_map/ppermute | solution.py:276
  13.6 5.9 %collective-permute-start.5 = (f32[16,1024]{1,0:T(8,128)S(1)}, f32[16,1024]{1,0:T(8,128)S(1)}, u32[]{:S(2)}, u32[]{:S(2)}) collective-permute-start(f32[16,1024]{1,0:T(8,128)S(1)} %get-tuple-element.35), channel_id=1, source_target_pairs={{0,1},{1,0},{2,3},{3,2},{4,5},{5,4},{6,7},{7,6},{8,9},{9,8},{10,11... | collective-permute-start | bytes 196616 | tf_op jit(solution)/shard_map/ppermute | solution.py:276
  20.2 1.4 %collective-permute-start.7 = (f32[4,7,8,128]{3,2,1,0:T(8,128)S(1)}, f32[4,7,8,128]{3,2,1,0:T(8,128)S(1)}, u32[]{:S(2)}, u32[]{:S(2)}) collective-permute-start(f32[4,7,8,128]{3,2,1,0:T(8,128)S(1)} %slice_bitcast_fusion), channel_id=1, source_target_pairs={{0,4},{4,0},{8,12},{12,8},{16,20},{20,16},{24,28},{28,24},{1,5},{5... | collective-permute-start | bytes 344072 | tf_op jit(solution)/shard_map/ppermute | solution.py:354
  21.6 5.2 %collective-permute-start.10 = (f32[2,7,8,128]{3,2,1,0:T(8,128)S(1)}, f32[2,7,8,128]{3,2,1,0:T(8,128)S(1)}, u32[]{:S(2)}, u32[]{:S(2)}) collective-permute-start(f32[2,7,8,128]{3,2,1,0:T(8,128)S(1)} %pad_maximum_fusion.2), channel_id=1, source_target_pairs={{0,24},{4,28},{8,16},{12,20},{16,8},{20,12},{24,0},{28,4},{1,25},{... | collective-permute-start | bytes 172040 | tf_op jit(solution)/shard_map/ppermute | solution.py:354
  24.1 4.2 %collective-permute-start.9 = (f32[2,7,8,128]{3,2,1,0:T(8,128)S(1)}, f32[2,7,8,128]{3,2,1,0:T(8,128)S(1)}, u32[]{:S(2)}, u32[]{:S(2)}) collective-permute-start(f32[2,7,8,128]{3,2,1,0:T(8,128)S(1)} %pad_maximum_fusion.1), channel_id=1, source_target_pairs={{0,16},{4,20},{8,24},{12,28},{16,0},{20,4},{24,8},{28,12},{1,17},{... | collective-permute-start | bytes 172040 | tf_op jit(solution)/shard_map/ppermute | solution.py:354
  24.6 4.2 %collective-permute-start.8 = (f32[2,7,8,128]{3,2,1,0:T(8,128)S(1)}, f32[2,7,8,128]{3,2,1,0:T(8,128)S(1)}, u32[]{:S(2)}, u32[]{:S(2)}) collective-permute-start(f32[2,7,8,128]{3,2,1,0:T(8,128)S(1)} %pad_maximum_fusion), channel_id=1, source_target_pairs={{0,8},{4,12},{8,0},{12,4},{16,24},{20,28},{24,16},{28,20},{1,9},{5... | collective-permute-start | bytes 172040 | tf_op jit(solution)/shard_map/ppermute | solution.py:354

commit v7 on v6

--- a/solution.py
+++ b/solution.py
@@ -47,33 +47,32 @@
     for first in (0, half):
         sums_ref[first : first + half, :] = sample_sums(rho_ref[first * rows : (first + half) * rows, :], half, rows)
     odd = lax.axis_index("light") % 2
-    for out_ref, (even_first, odd_first) in zip(out_refs, places, strict=True):
-        first = pl.multiple_of(even_first + odd * (odd_first - even_first), 8)
-        out_ref[...] = sums_ref[pl.ds(first, out_ref.shape[0]), :]
+    for out_ref, pieces in zip(out_refs, places, strict=True):
+        row, width = 0, out_ref.shape[1]
+        for even_first, odd_first, count, column in pieces:
+            first = pl.multiple_of(even_first + odd * (odd_first - even_first), 8)
+            out_ref[row : row + count, :] = sums_ref[pl.ds(first, count), column : column + width]
+            row += count
 
 
 def pair_kernel(hold_ref, given_ref, pair_ref):
     pair_ref[...] = hold_ref[...] + given_ref[...]
 
 
-def upper_kernel(straight_ref, across_ref, same_ref, cross_ref, below_ref, send_ref):
+def upper_kernel(straight_ref, across_ref, same_ref, below_ref, send_ref):
     me = lax.axis_index("light")
     odd = me % 2 == 1
-    few = same_ref.shape[0]
     below = jnp.where(me >= 2, straight_ref[...] + across_ref[...], 0.0)
     below_ref[...] = below
-    send_ref[:few, :] = below + jnp.where(odd, 0.0, same_ref[...])
-    send_ref[few:, :] = cross_ref[...]
-
-
-def late_kernel(late_ref, send_ref, add_ref, out_ref):
-    odd = lax.axis_index("light") % 2 == 1
-    add_ref[...] = jnp.where(odd, late_ref[...], 0.0)
-    out_ref[...] = send_ref[...]
+    send_ref[...] = below + jnp.where(odd, 0.0, same_ref[...])
+
+
+def late_kernel(late_ref, add_ref):
+    add_ref[...] = jnp.where(lax.axis_index("light") % 2 == 1, late_ref[...], 0.0)
 
 
 def pre_kernel(
-    samples, rows, width, rho_ref, light_ref, view_ref, table_ref,
+    samples, rows, width, rho_ref, light_ref, view_ref, table_ref, _,
     near_ref, far_ref, red_ref, green_ref, blue_ref, total_ref, above_ref,
 ):
     columns = rho_ref.shape[1]
@@ -126,21 +125,23 @@
     below_ref[...] = jnp.where(me >= 2, same, 0.0) + jnp.where(me % 2 == 1, given, 0.0)
 
 
+def first_below(refs, below_ref):
+    mine, other, late = (ref[...] for ref in refs)
+    few = mine.shape[0]
+    odd = lax.axis_index("light") % 2 == 1
+    below_ref[:few, :] = jnp.where(odd, other, mine)
+    below_ref[few:, :] = jnp.where(odd, mine + late[-few:], other)
+
+
 def crossed_below(refs, below_ref):
-    mine, other, cross, late = (ref[...] for ref in refs)
-    few = mine.shape[0]
-    me = lax.axis_index("light")
-    odd = me % 2 == 1
-    below_ref[:few, :] = jnp.where(odd, other[:few], mine)
-    below_ref[few : 2 * few, :] = jnp.where(odd, mine + other[few:], other[:few])
-    below_ref[2 * few :, :] = jnp.where(me >= 2, cross, 0.0) + late
+    cross, late = (ref[...] for ref in refs)
+    below_ref[...] = jnp.where(lax.axis_index("light") >= 2, cross, 0.0) + late[: cross.shape[0]]
 
 
 def whole_below(refs, below_ref):
-    first = 0
-    for ref in refs:
-        below_ref[first : first + ref.shape[0], :] = ref[...]
-        first += ref.shape[0]
+    count, columns = refs[0].shape
+    below_ref[:count, :] = refs[0][:, : columns // 2]
+    below_ref[count:, :] = refs[0][:, columns // 2 :]
 
 
 def post_kernel(
@@ -148,27 +149,33 @@
 ):
     *refs, out_ref, lit_ref = refs
     assemble(refs, lit_ref)
-    _, columns = lit_ref.shape
+    columns = near_ref.shape[1]
     place = lax.axis_index("depth") if sliced else 0
     chip, core = place // 2, place % 2
     odd = lax.axis_index("light") % 2
-    firsts = [even_first + odd * (odd_first - even_first) for even_first, odd_first, _ in runs]
-    groups = [(first, start) for first, (_, _, count) in zip(firsts, runs, strict=True) for start in range(0, count, 8)]
-    lit_ref[...] = jnp.exp2(lit_ref[...] * (light_ref[...] * -LOG2E))
     width = 2 * LANES
     shape = (rows, width)
     scales = [jnp.broadcast_to(table_ref[3 + k : 4 + k, :], (rows, LANES)) for k in range(3)]
-    for slot in range(columns // width):
-        at = pl.ds(pl.multiple_of((slot ^ chip) * width, width), width)
+    for side, pieces in enumerate(runs):
+        start = side * columns // 2
+        light = light_ref[:, start : start + columns // 2] * -LOG2E
+        for _, _, count, row in pieces:
+            lit_ref[row : row + count, :] = jnp.exp2(lit_ref[row : row + count, :] * light)
+    for block in range(columns // width):
+        at = slice(block * width, (block + 1) * width)
+        side, here_at = divmod(block * width, columns // 2)
         sums = [jnp.zeros(shape, F32)] * 6
-        for group, (first, start) in enumerate(groups):
-            lit = lit_ref[group * 8 : group * 8 + 8, at]
-            for part in range(8):
-                here = pl.ds(pl.multiple_of((first + start + part) * rows, rows), rows)
-                shade = jnp.broadcast_to(lit[part : part + 1], shape)
-                weights = near_ref[here, at] * shade, far_ref[here, at] * shade
-                colors = [ref[here, at] for ref in (red_ref, green_ref, blue_ref)]
-                sums = [sums[3 * v + k] + weights[v] * colors[k] for v in range(2) for k in range(3)]
+        for even_first, odd_first, count, row in runs[side]:
+            first = even_first + odd * (odd_first - even_first)
+            for group in range(0, count, 8):
+                lit = lit_ref[row + group : row + group + 8, here_at : here_at + width]
+                for part in range(8):
+                    here = pl.ds(pl.multiple_of((first + group + part) * rows, rows), rows)
+                    shade = jnp.broadcast_to(lit[part : part + 1], shape)
+                    weights = near_ref[here, at] * shade, far_ref[here, at] * shade
+                    colors = [ref[here, at] for ref in (red_ref, green_ref, blue_ref)]
+                    sums = [sums[3 * v + k] + weights[v] * colors[k] for v in range(2) for k in range(3)]
+        slot = block ^ chip
         for tile in range(2):
             lanes = slice(tile * LANES, (tile + 1) * LANES)
             for n in range(6):
@@ -291,20 +298,17 @@
     return jnp.where(odd, jnp.concatenate([other, mine]), jnp.concatenate([mine, other]))
 
 
-def lower_of_four(give, hold, same, cross):
+def lower_of_four(give, hold, same, cross, late):
     given = swap(give, 1, 4)
     straight, across = swap(same, 2, 4), swap(cross, 3, 4)
     columns = same.shape[1]
-    late = swap(hold, 1, 4)
+    late = swap(late, 1, 4)
     (pair,) = call(pair_kernel, [(hold.shape, F32)], "VV", [], 1 << 10, 1 << 10, hold, given)
     from_same, from_cross = swap(pair, 2, 4), swap(pair, 3, 4)
-    sent = 2 * same.shape[0], columns
-    mine, send = call(
-        upper_kernel, [(same.shape, F32), (sent, F32)], "VVVV", [], 1 << 30, 1 << 10, straight, across, same, cross
-    )
-    late, send = call(late_kernel, [(late.shape, F32), (sent, F32)], "VV", [], 1 << 10, 1 << 10, late, send)
+    mine, send = call(upper_kernel, [(same.shape, F32)] * 2, "VVV", [], 1 << 31, 1 << 10, straight, across, same)
+    (late,) = call(late_kernel, [(late.shape, F32)], "V", [], 1 << 10, 1 << 10, late)
     other = swap(send, 1, 4)
-    return (from_same, given), (mine, other, from_cross, late)
+    return (from_same, given), (mine, other, late), (from_cross, late)
 
 
 def shards(depth_n, light_n, density, light_rate, view_rate, centers, rank):
@@ -312,41 +316,55 @@
     rho = density.reshape(samples * rows, columns)
     light = light_rate.reshape(1, -1)
     whole = (samples * rows, columns)
-    few, many = samples // 8, 3 * samples // 8
-    places = ((2 * few + many, 2 * few), (2 * few, 2 * few + many), (0, few), (few, 0)) if light_n == 4 else ((0, 0),)
-    sizes = (many, many, few, few) if light_n == 4 else (samples,)
+    sizes = [(samples // 8 * (side + 1), samples // 8 * (3 - side), columns // 2 * side) for side in range(2)]
+    give = [(2 * few + many, 2 * few, many, at) for few, many, at in sizes]
+    hold = [(2 * few, 2 * few + many, many, at) for few, many, at in sizes]
+    same = [(0, few, few, at) for few, many, at in sizes]
+    cross = [(few, 0, few, at) for few, many, at in sizes]
+    places, width = [give, hold, same, cross, hold + cross], columns // 2
+    if light_n != 4:
+        places, width = [[(0, 0, samples, 0)]], columns
     own = columns // depth_n
     sliced = own == LANES and depth_n <= 8 and depth_n & (depth_n - 1) == 0
     table = (TONES + 2 * depth_n if sliced else TONES, LANES)
     *sums, table, rho = call(
         functools.partial(sums_kernel, rows, places, sliced),
-        [((n, columns), F32) for n in sizes] + [(table, F32), (whole, jnp.bfloat16)], "AAA",
+        [((sum(piece[2] for piece in pieces), width), F32) for pieces in places] + [(table, F32), (whole, jnp.bfloat16)], "AAA",
         [pltpu.VMEM((samples, columns), F32), pltpu.SMEM(rank.shape, jnp.int32), pltpu.SMEM(centers.shape, F32), pltpu.SemaphoreType.DMA((3,))],
         1 << 20, 1 << 20, rho, rank, centers,
     )
     if light_n == 4:
         pieces = lower_of_four(*sums)
-        assemble = straight_below, crossed_below
+        assemble = straight_below, first_below, crossed_below
     else:
         below = lower(sums[0], 1, light_n)
-        pieces = [below[2 * few : 2 * few + many]], [below[: 2 * few], below[2 * few + many :]]
+        pieces = [below[: samples // 2]], [below[samples // 2 :]]
         assemble = whole_below, whole_below
     near, far, red, green, blue, total = call(
-        functools.partial(pre_kernel, samples, rows, 256), [(whole, F32)] * 5 + [((rows, columns), F32)], "VVVV",
-        [pltpu.VMEM(whole, F32)], 1 << 20, 12 << 20, rho, light, view_rate, table,
+        functools.partial(pre_kernel, samples, rows, 256), [(whole, F32)] * 5 + [((rows, columns), F32)], "VVVVV",
+        [pltpu.VMEM(whole, F32)], 1 << 20, 12 << 20, rho, light, view_rate, table, pieces[1][-1],
     )
     place = lax.axis_index("depth")
     rate = lax.dynamic_slice_in_dim(view_rate, place * own, own, axis=1)
     packed = total
-    late = 2 * few + many
-    runs = ((2 * few, late, many),), ((0, 0, 2 * few), (late, 2 * few, many))
+    runs = [[], []], [[], []], [[], []]
+    first, last = sum(few for few, _, _ in sizes), sum(many for _, many, _ in sizes)
+    row, much = 0, 0
+    for side, (few, many, _) in enumerate(sizes):
+        runs[0][side].append((2 * few, 2 * few + many, many, much))
+        runs[1][side] += [(0, 0, few, row), (few, few, few, first + row)]
+        runs[2][side].append((2 * few + many, 2 * few, many, much))
+        row, much = row + few, much + many
+    rows_of = last, 2 * first, last
     if light_n != 4:
-        runs = ((2 * few, 2 * few, many),), ((0, 0, 2 * few), (late, late, many))
-    for second in range(2):
+        half = samples // 2
+        runs = [[[(start, start, half, half * side)] for side in range(2)] for start in (0, half)]
+        rows_of = samples, samples
+    for second in range(len(runs)):
         (packed,) = call(
-            functools.partial(post_kernel, rows, second, runs[second], sliced, assemble[second]),
+            functools.partial(post_kernel, rows, second > 0, runs[second], sliced, assemble[second]),
             [((2, columns // (2 * LANES), 7, rows, LANES), F32)], "V" * (8 + len(pieces[second])),
-            [pltpu.VMEM((sum(run[2] for run in runs[second]), columns), F32)], 1 << 10, 1 << 10,
+            [pltpu.VMEM((rows_of[second], columns // 2), F32)], 1 << 10, 1 << 10,
             light, table, near, far, red, green, blue, packed, *pieces[second],
         )
     if sliced:

time: 29.7 us -> 28.8 us (0.970)
  waiting for transfers between devices: 9.9 us -> 8.71 us
  Pallas kernels: 4.96 us -> 5.32 us
    ppermute x7, waiting for transfers between devices: 4.96 us -> 3.78 us  [swap(): return lax.ppermute(x, 'light', [(i, i ^ stride) for i in range(n)])]
    pallas_call x8 -> x9, Pallas kernels: 4.96 us -> 5.32 us  [call(): pl.pallas_call(kernel, out_shape=tuple((pltpu.VMEM(o, t) for o, t in outs...]
  transfers between devices with their start and end apart: 11 -> 11, of which waited for: 7 -> 8; matrix products, arithmetic and copies ran while one was open for 0% -> 0% of each run, Pallas kernels for 9% -> 11%
where the time goes in v7:
time: 28.8 us; the launch traced here: 28.7 us
  starting transfers between devices  13.8 us (48%)
  waiting for transfers between devices  8.71 us (30%)
  Pallas kernels  5.32 us (18%)
  local copies, waits for them, and re-layouts  0.66 us (2%)
    ppermute x7, starting transfers between devices, swap(): return lax.ppermute(x, 'light', [(i, i ^ stride) for i in range(n)])  10.2 us
    pallas_call x9, Pallas kernels, call(): pl.pallas_call(kernel, out_shape=tuple((pltpu.VMEM(o, t) for o, t in outs...  5.32 us
    ppermute x4, waiting for transfers between devices, send_to(): return lax.ppermute(x, 'depth', [(i, i ^ stride) for i in range(depth_n)])  4.93 us
    ppermute x7, waiting for transfers between devices, swap(): return lax.ppermute(x, 'light', [(i, i ^ stride) for i in range(n)])  3.78 us
    ppermute x4, starting transfers between devices, send_to(): return lax.ppermute(x, 'depth', [(i, i ^ stride) for i in range(depth_n)])  3.62 us
    unnamed x5, local copies, waits for them, and re-layouts  0.63 us
  transfers between devices with their start and end apart: 11, of which 8 were waited for; matrix products, arithmetic and copies ran while one was open for 0% of the time, Pallas kernels for 11%

profile of v7, /device:TPU:0, one launch (start us, length us, event | category | flops | bytes accessed | tf_op | source)
XLA Modules:
  0.0 28.7 jit_solution(4392865945514024821)
XLA Ops:
  0.0 1.6 %shard_map.55 = (f32[40,512]{1,0:T(8,128)S(1)}, f32[40,512]{1,0:T(8,128)S(1)}, f32[24,512]{1,0:T(8,128)S(1)}, f32[24,512]{1,0:T(8,128)S(1)}, f32[64,512]{1,0:T(8...) custom-call(bf16[512,1024]{1,0:T(8,128)(2,1)} %bitcast.14, s32[2,8]{1,0:T(2,128)} %rank_hbm.1, f32[3]{0:T(128)} %center_hbm.1), custom_call_target="tpu_custom_call" | custom-call | flops 1048576 | bytes 1048576 | tf_op jit(solution)/shard_map/pallas_call | solution.py:193
  1.6 3.1 %collective-permute-start.1 = (f32[40,512]{1,0:T(8,128)S(1)}, f32[40,512]{1,0:T(8,128)S(1)}, u32[]{:S(2)}, u32[]{:S(2)}) collective-permute-start(f32[40,512]{1,0:T(8,128)S(1)} %get-tuple-element.30), channel_id=1, source_target_pairs={{0,1},{1,0},{2,3},{3,2},{4,5},{5,4},{6,7},{7,6},{8,9},{9,8},{10,11... | collective-permute-start | bytes 245768 | tf_op jit(solution)/shard_map/ppermute | solution.py:283
  4.7 2.6 %collective-permute-start.3 = (f32[24,512]{1,0:T(8,128)S(1)}, f32[24,512]{1,0:T(8,128)S(1)}, u32[]{:S(2)}, u32[]{:S(2)}) collective-permute-start(f32[24,512]{1,0:T(8,128)S(1)} %get-tuple-element.31.same_ref), channel_id=1, source_target_pairs={{0,2},{1,3},{2,0},{3,1},{4,6},{5,7},{6,4},{7,5},{8,10},{9,11},{10,... | collective-permute-start | bytes 147464 | tf_op jit(solution)/shard_map/ppermute | solution.py:283
  7.2 0.0 collective-permute-start.4
  7.2 0.9 %collective-permute-start = (f32[64,512]{1,0:T(8,128)S(1)}, f32[64,512]{1,0:T(8,128)S(1)}, u32[]{:S(2)}, u32[]{:S(2)}) collective-permute-start(f32[64,512]{1,0:T(8,128)S(1)} %get-tuple-element.22), channel_id=1, source_target_pairs={{0,1},{1,0},{2,3},{3,2},{4,5},{5,4},{6,7},{7,6},{8,9},{9,8},{10,11... | collective-permute-start | bytes 393224 | tf_op jit(solution)/shard_map/ppermute | solution.py:283
  8.1 0.0 collective-permute-done.1.given_ref.refs_1_
  8.2 0.0 copy-start
  8.2 0.0 copy-start.1
  8.2 3.6 %collective-permute-start.2 = (f32[40,512]{1,0:T(8,128)S(1)}, f32[40,512]{1,0:T(8,128)S(1)}, u32[]{:S(2)}, u32[]{:S(2)}) collective-permute-start(f32[40,512]{1,0:T(8,128)S(1)} %shard_map.58), channel_id=1, source_target_pairs={{0,2},{1,3},{2,0},{3,1},{4,6},{5,7},{6,4},{7,5},{8,10},{9,11},{10,... | collective-permute-start | bytes 245768 | tf_op jit(solution)/shard_map/ppermute | solution.py:283
  11.7 0.0 collective-permute-start.6
  11.8 0.0 collective-permute-done.3.straight_ref
  11.8 2.1 %collective-permute-done.4.across_ref = f32[24,512]{1,0:T(8,128)S(1)} collective-permute-done((f32[24,512]{1,0:T(8,128)S(1)}, f32[24,512]{1,0:T(8,128)S(1)}, u32[]{:S(2)}, u32[]{:S(2)}) %collective-permute-start.4) | collective-permute-done | bytes 49184 | tf_op jit(solution)/shard_map/ppermute | solution.py:283
  13.8 0.1 collective-permute-start.5
  13.9 0.9 %collective-permute-done.late_ref = f32[64,512]{1,0:T(8,128)S(1)} collective-permute-done((f32[64,512]{1,0:T(8,128)S(1)}, f32[64,512]{1,0:T(8,128)S(1)}, u32[]{:S(2)}, u32[]{:S(2)}) %collective-permute-start) | collective-permute-done | bytes 131104 | tf_op jit(solution)/shard_map/ppermute | solution.py:283
  14.9 0.0 copy-done
  14.9 0.0 copy-done.1
  14.9 2.2 %shard_map.57 = (f32[512,1024]{1,0:T(8,128)S(1)}, f32[512,1024]{1,0:T(8,128)S(1)}, f32[512,1024]{1,0:T(8,128)S(1)}, f32[512,1024]{1,0:T(8,128)S(1)}, f32[512,1024]{1,0:T(8,128)S(1)}, /*index=5*/f32[8,1024]{1,0:T(8,128)S(1)}) custom-call(bf16[512,1024]{1,0:T(8,128)(2,1)S(1)} %get-tuple-element.21.rho_ref, f32[1,1024]{1,0:T(1,128)S(1)} %bitcast.10, ...), custom_call_target="tpu_custom_call" | custom-call | flops 1048576 | bytes 12582912 | tf_op jit(solution)/shard_map/pallas_call | solution.py:193
  17.2 0.0 collective-permute-done.2.refs_0_
  17.2 0.5 %shard_map.59.rest_ref = f32[2,4,7,8,128]{4,3,2,1,0:T(8,128)S(1)} custom-call(f32[1,1024]{1,0:T(1,128)S(1)} %bitcast.11, f32[24,128]{1,0:T(8,128)S(1)} %get-tuple-element.20.table_ref, f32[512,1024]{1,0:T(8,128)S(1)} %get-tuple-element.23.near_ref, f32[512,1024]{1,0:T(8,128)S(1)} %get-tuple-element.24.far_ref, f32[512,1024]{1,0:T(8,128)S(1)} %get-tuple-element.25.red_ref, ...), custom_call_target="tpu_custom_call" | custom-call | flops 1024 | bytes 1024 | tf_op jit(solution)/shard_map/pallas_call | solution.py:193
  17.6 0.4 %collective-permute-done.5.refs_1_ = f32[24,512]{1,0:T(8,128)S(1)} collective-permute-done((f32[24,512]{1,0:T(8,128)S(1)}, f32[24,512]{1,0:T(8,128)S(1)}, u32[]{:S(2)}, u32[]{:S(2)}) %collective-permute-start.5) | collective-permute-done | bytes 49184 | tf_op jit(solution)/shard_map/ppermute | solution.py:283
  18.0 0.5 %shard_map.61.rest_ref = f32[2,4,7,8,128]{4,3,2,1,0:T(8,128)S(1)} custom-call(f32[1,1024]{1,0:T(1,128)S(1)} %bitcast.12, f32[24,128]{1,0:T(8,128)S(1)} %get-tuple-element.20.table_ref, f32[512,1024]{1,0:T(8,128)S(1)} %get-tuple-element.23.near_ref, f32[512,1024]{1,0:T(8,128)S(1)} %get-tuple-element.24.far_ref, f32[512,1024]{1,0:T(8,128)S(1)} %get-tuple-element.25.red_ref, ...), custom_call_target="tpu_custom_call" | custom-call | flops 1024 | bytes 1024 | tf_op jit(solution)/shard_map/pallas_call | solution.py:193
  18.5 0.4 %collective-permute-done.6.refs_0_ = f32[40,512]{1,0:T(8,128)S(1)} collective-permute-done((f32[40,512]{1,0:T(8,128)S(1)}, f32[40,512]{1,0:T(8,128)S(1)}, u32[]{:S(2)}, u32[]{:S(2)}) %collective-permute-start.6) | collective-permute-done | bytes 81952 | tf_op jit(solution)/shard_map/ppermute | solution.py:283
  18.9 0.5 %shard_map.62.own_ref = f32[2,4,7,8,128]{4,3,2,1,0:T(8,128)S(1)} custom-call(f32[1,1024]{1,0:T(1,128)S(1)} %bitcast.13, f32[24,128]{1,0:T(8,128)S(1)} %get-tuple-element.20.table_ref, f32[512,1024]{1,0:T(8,128)S(1)} %get-tuple-element.23.near_ref, f32[512,1024]{1,0:T(8,128)S(1)} %get-tuple-element.24.far_ref, f32[512,1024]{1,0:T(8,128)S(1)} %get-tuple-element.25.red_ref, ...), custom_call_target="tpu_custom_call" | custom-call | flops 1024 | bytes 1024 | tf_op jit(solution)/shard_map/pallas_call | solution.py:193
  19.4 0.1 collective-permute-start.7
  19.5 1.3 %collective-permute-done.7.sibling_ref = f32[4,7,8,128]{3,2,1,0:T(8,128)S(1)} collective-permute-done((f32[4,7,8,128]{3,2,1,0:T(8,128)S(1)}, f32[4,7,8,128]{3,2,1,0:T(8,128)S(1)}, u32[]{:S(2)}, u32[]{:S(2)}) %collective-permute-start.7) | collective-permute-done | bytes 114720 | tf_op jit(solution)/shard_map/ppermute | solution.py:372
  20.8 2.5 %collective-permute-start.10 = (f32[2,7,8,128]{3,2,1,0:T(8,128)S(1)}, f32[2,7,8,128]{3,2,1,0:T(8,128)S(1)}, u32[]{:S(2)}, u32[]{:S(2)}) collective-permute-start(f32[2,7,8,128]{3,2,1,0:T(8,128)S(1)} %pad_maximum_fusion.2), channel_id=1, source_target_pairs={{0,24},{4,28},{8,16},{12,20},{16,8},{20,12},{24,0},{28,4},{1,25},{... | collective-permute-start | bytes 172040 | tf_op jit(solution)/shard_map/ppermute | solution.py:372
  23.3 0.5 %collective-permute-start.9 = (f32[2,7,8,128]{3,2,1,0:T(8,128)S(1)}, f32[2,7,8,128]{3,2,1,0:T(8,128)S(1)}, u32[]{:S(2)}, u32[]{:S(2)}) collective-permute-start(f32[2,7,8,128]{3,2,1,0:T(8,128)S(1)} %pad_maximum_fusion.1), channel_id=1, source_target_pairs={{0,16},{4,20},{8,24},{12,28},{16,0},{20,4},{24,8},{28,12},{1,17},{... | collective-permute-start | bytes 172040 | tf_op jit(solution)/shard_map/ppermute | solution.py:372
  23.8 0.5 %collective-permute-start.8 = (f32[2,7,8,128]{3,2,1,0:T(8,128)S(1)}, f32[2,7,8,128]{3,2,1,0:T(8,128)S(1)}, u32[]{:S(2)}, u32[]{:S(2)}) collective-permute-start(f32[2,7,8,128]{3,2,1,0:T(8,128)S(1)} %pad_maximum_fusion), channel_id=1, source_target_pairs={{0,8},{4,12},{8,0},{12,4},{16,24},{20,28},{24,16},{28,20},{1,9},{5... | collective-permute-start | bytes 172040 | tf_op jit(solution)/shard_map/ppermute | solution.py:372
  24.4 1.6 %collective-permute-done.10.refs_2_ = f32[2,7,8,128]{3,2,1,0:T(8,128)S(1)} collective-permute-done((f32[2,7,8,128]{3,2,1,0:T(8,128)S(1)}, f32[2,7,8,128]{3,2,1,0:T(8,128)S(1)}, u32[]{:S(2)}, u32[]{:S(2)}) %collective-permute-start.10) | collective-permute-done | bytes 57376 | tf_op jit(solution)/shard_map/ppermute | solution.py:372
  25.9 1.5 %collective-permute-done.9.refs_1_ = f32[2,7,8,128]{3,2,1,0:T(8,128)S(1)} collective-permute-done((f32[2,7,8,128]{3,2,1,0:T(8,128)S(1)}, f32[2,7,8,128]{3,2,1,0:T(8,128)S(1)}, u32[]{:S(2)}, u32[]{:S(2)}) %collective-permute-start.9) | collective-permute-done | bytes 57376 | tf_op jit(solution)/shard_map/ppermute | solution.py:372
  27.5 0.5 %collective-permute-done.8.refs_0_ = f32[2,7,8,128]{3,2,1,0:T(8,128)S(1)} collective-permute-done((f32[2,7,8,128]{3,2,1,0:T(8,128)S(1)}, f32[2,7,8,128]{3,2,1,0:T(8,128)S(1)}, u32[]{:S(2)}, u32[]{:S(2)}) %collective-permute-start.8) | collective-permute-done | bytes 57376 | tf_op jit(solution)/shard_map/ppermute | solution.py:372
  28.0 0.1 shard_map.63
  28.1 0.6 %copy.6 = f32[2,4,8,128]{3,2,1,0:T(8,128)} copy(f32[2,4,8,128]{3,2,1,0:T(8,128)S(1)} %shard_map.63) | data formatting | bytes 65536
  (10 shorter events, 0.1 us)
Async XLA Ops:
  1.6 6.6 %collective-permute-start.1 = (f32[40,512]{1,0:T(8,128)S(1)}, f32[40,512]{1,0:T(8,128)S(1)}, u32[]{:S(2)}, u32[]{:S(2)}) collective-permute-start(f32[40,512]{1,0:T(8,128)S(1)} %get-tuple-element.30), channel_id=1, source_target_pairs={{0,1},{1,0},{2,3},{3,2},{4,5},{5,4},{6,7},{7,6},{8,9},{9,8},{10,11... | collective-permute-start | bytes 245768 | tf_op jit(solution)/shard_map/ppermute | solution.py:283
  4.7 7.1 %collective-permute-start.3 = (f32[24,512]{1,0:T(8,128)S(1)}, f32[24,512]{1,0:T(8,128)S(1)}, u32[]{:S(2)}, u32[]{:S(2)}) collective-permute-start(f32[24,512]{1,0:T(8,128)S(1)} %get-tuple-element.31.same_ref), channel_id=1, source_target_pairs={{0,2},{1,3},{2,0},{3,1},{4,6},{5,7},{6,4},{7,5},{8,10},{9,11},{10,... | collective-permute-start | bytes 147464 | tf_op jit(solution)/shard_map/ppermute | solution.py:283
  7.2 6.6 %collective-permute-start.4 = (f32[24,512]{1,0:T(8,128)S(1)}, f32[24,512]{1,0:T(8,128)S(1)}, u32[]{:S(2)}, u32[]{:S(2)}) collective-permute-start(f32[24,512]{1,0:T(8,128)S(1)} %get-tuple-element.32), channel_id=1, source_target_pairs={{0,3},{1,2},{2,1},{3,0},{4,7},{5,6},{6,5},{7,4},{8,11},{9,10},{10,... | collective-permute-start | bytes 147464 | tf_op jit(solution)/shard_map/ppermute | solution.py:283
  7.2 7.6 %collective-permute-start = (f32[64,512]{1,0:T(8,128)S(1)}, f32[64,512]{1,0:T(8,128)S(1)}, u32[]{:S(2)}, u32[]{:S(2)}) collective-permute-start(f32[64,512]{1,0:T(8,128)S(1)} %get-tuple-element.22), channel_id=1, source_target_pairs={{0,1},{1,0},{2,3},{3,2},{4,5},{5,4},{6,7},{7,6},{8,9},{9,8},{10,11... | collective-permute-start | bytes 393224 | tf_op jit(solution)/shard_map/ppermute | solution.py:283
  8.2 6.7 %copy-start = (f32[1024]{0:T(1024)S(1)}, f32[1024]{0:T(1024)}, u32[]{:S(2)}) copy-start(f32[1024]{0:T(1024)} %param.6) | copy-start | bytes 12292
  8.2 6.7 %copy-start.1 = (f32[2,1024]{1,0:T(2,128)S(1)}, f32[2,1024]{1,0:T(2,128)}, u32[]{:S(2)}) copy-start(f32[2,1024]{1,0:T(2,128)} %view_ref.1) | copy-start | bytes 24580
  8.2 9.0 %collective-permute-start.2 = (f32[40,512]{1,0:T(8,128)S(1)}, f32[40,512]{1,0:T(8,128)S(1)}, u32[]{:S(2)}, u32[]{:S(2)}) collective-permute-start(f32[40,512]{1,0:T(8,128)S(1)} %shard_map.58), channel_id=1, source_target_pairs={{0,2},{1,3},{2,0},{3,1},{4,6},{5,7},{6,4},{7,5},{8,10},{9,11},{10,... | collective-permute-start | bytes 245768 | tf_op jit(solution)/shard_map/ppermute | solution.py:283
  11.7 7.1 %collective-permute-start.6 = (f32[40,512]{1,0:T(8,128)S(1)}, f32[40,512]{1,0:T(8,128)S(1)}, u32[]{:S(2)}, u32[]{:S(2)}) collective-permute-start(f32[40,512]{1,0:T(8,128)S(1)} %shard_map.58), channel_id=1, source_target_pairs={{0,3},{1,2},{2,1},{3,0},{4,7},{5,6},{6,5},{7,4},{8,11},{9,10},{10,... | collective-permute-start | bytes 245768 | tf_op jit(solution)/shard_map/ppermute | solution.py:283
  13.8 4.2 %collective-permute-start.5 = (f32[24,512]{1,0:T(8,128)S(1)}, f32[24,512]{1,0:T(8,128)S(1)}, u32[]{:S(2)}, u32[]{:S(2)}) collective-permute-start(f32[24,512]{1,0:T(8,128)S(1)} %get-tuple-element.34), channel_id=1, source_target_pairs={{0,1},{1,0},{2,3},{3,2},{4,5},{5,4},{6,7},{7,6},{8,9},{9,8},{10,11... | collective-permute-start | bytes 147464 | tf_op jit(solution)/shard_map/ppermute | solution.py:283
  19.4 1.4 %collective-permute-start.7 = (f32[4,7,8,128]{3,2,1,0:T(8,128)S(1)}, f32[4,7,8,128]{3,2,1,0:T(8,128)S(1)}, u32[]{:S(2)}, u32[]{:S(2)}) collective-permute-start(f32[4,7,8,128]{3,2,1,0:T(8,128)S(1)} %slice_bitcast_fusion), channel_id=1, source_target_pairs={{0,4},{4,0},{8,12},{12,8},{16,20},{20,16},{24,28},{28,24},{1,5},{5... | collective-permute-start | bytes 344072 | tf_op jit(solution)/shard_map/ppermute | solution.py:372
  20.8 5.2 %collective-permute-start.10 = (f32[2,7,8,128]{3,2,1,0:T(8,128)S(1)}, f32[2,7,8,128]{3,2,1,0:T(8,128)S(1)}, u32[]{:S(2)}, u32[]{:S(2)}) collective-permute-start(f32[2,7,8,128]{3,2,1,0:T(8,128)S(1)} %pad_maximum_fusion.2), channel_id=1, source_target_pairs={{0,24},{4,28},{8,16},{12,20},{16,8},{20,12},{24,0},{28,4},{1,25},{... | collective-permute-start | bytes 172040 | tf_op jit(solution)/shard_map/ppermute | solution.py:372
  23.3 4.2 %collective-permute-start.9 = (f32[2,7,8,128]{3,2,1,0:T(8,128)S(1)}, f32[2,7,8,128]{3,2,1,0:T(8,128)S(1)}, u32[]{:S(2)}, u32[]{:S(2)}) collective-permute-start(f32[2,7,8,128]{3,2,1,0:T(8,128)S(1)} %pad_maximum_fusion.1), channel_id=1, source_target_pairs={{0,16},{4,20},{8,24},{12,28},{16,0},{20,4},{24,8},{28,12},{1,17},{... | collective-permute-start | bytes 172040 | tf_op jit(solution)/shard_map/ppermute | solution.py:372
  23.8 4.2 %collective-permute-start.8 = (f32[2,7,8,128]{3,2,1,0:T(8,128)S(1)}, f32[2,7,8,128]{3,2,1,0:T(8,128)S(1)}, u32[]{:S(2)}, u32[]{:S(2)}) collective-permute-start(f32[2,7,8,128]{3,2,1,0:T(8,128)S(1)} %pad_maximum_fusion), channel_id=1, source_target_pairs={{0,8},{4,12},{8,0},{12,4},{16,24},{20,28},{24,16},{28,20},{1,9},{5... | collective-permute-start | bytes 172040 | tf_op jit(solution)/shard_map/ppermute | solution.py:372

commit v8 on v7

--- a/solution.py
+++ b/solution.py
@@ -186,6 +186,45 @@
             out_ref[tile ^ core, slot, 6] = rest_ref[tile ^ core, slot, 6] if second else rest_ref[:, at][:, lanes]
 
 
+def post_tiles_kernel(
+    rows, which, runs, assemble, light_ref, table_ref, near_ref, far_ref, red_ref, green_ref, blue_ref, rest_ref, *refs
+):
+    *refs, out_ref, lit_ref = refs
+    assemble(refs, lit_ref)
+    columns = near_ref.shape[1]
+    place = lax.axis_index("depth")
+    chip, core = place // 2, place % 2
+    odd = lax.axis_index("light") % 2
+    shape = (rows, LANES)
+    scales = [jnp.broadcast_to(table_ref[3 + k : 4 + k, :], shape) for k in range(3)]
+    blocks = columns // (2 * LANES)
+    for side, pieces in enumerate(runs):
+        start = side * columns // 2
+        light = light_ref[:, start : start + columns // 2] * -LOG2E
+        for _, _, count, row in pieces:
+            lit_ref[row : row + count, :] = jnp.exp2(lit_ref[row : row + count, :] * light)
+        tiles = range(side * blocks // 2, (side + 1) * blocks // 2)
+        lanes = [pl.ds(pl.multiple_of((2 * tile + (which ^ core)) * LANES, LANES), LANES) for tile in tiles]
+        near_lanes = [pl.ds(pl.multiple_of((2 * tile + (which ^ core)) * LANES - start, LANES), LANES) for tile in tiles]
+        sums = [[jnp.zeros(shape, F32)] * 6 for _ in tiles]
+        for even_first, odd_first, count, row in pieces:
+            first = even_first + odd * (odd_first - even_first)
+            for group in range(0, count, 8):
+                lits = [lit_ref[row + group : row + group + 8, at] for at in near_lanes]
+                for part in range(8):
+                    here = pl.ds(pl.multiple_of((first + group + part) * rows, rows), rows)
+                    for n, at in enumerate(lanes):
+                        shade = jnp.broadcast_to(lits[n][part : part + 1], shape)
+                        weights = near_ref[here, at] * shade, far_ref[here, at] * shade
+                        colors = [ref[here, at] for ref in (red_ref, green_ref, blue_ref)]
+                        sums[n] = [sums[n][3 * v + k] + weights[v] * colors[k] for v in range(2) for k in range(3)]
+        for n, tile in enumerate(tiles):
+            slot = tile ^ chip
+            for channel in range(6):
+                out_ref[slot, channel] = sums[n][channel] * scales[channel % 3] + rest_ref[which, slot, channel]
+            out_ref[slot, 6] = rest_ref[which, slot, 6]
+
+
 def call(kernel, outs, spaces, scratch, flops, moved, *args, limit=8):
     specs = {"v": pl.BlockSpec(memory_space=pltpu.VMEM), "s": pl.BlockSpec(memory_space=pltpu.SMEM), "a": pl.BlockSpec(memory_space=pl.ANY)}
     forced = {"V": pltpu.VMEM, "A": pltpu.HBM, "S": pltpu.SMEM}
@@ -247,10 +286,11 @@
     return jnp.where(depth < 0.35, depth * small, 1.0 - jnp.exp2(depth * -LOG2E))
 
 
-def slots_kernel(table_ref, rate_ref, own_ref, sibling_ref, *refs):
+def slots_kernel(order, table_ref, rate_ref, own_ref, sibling_ref, *refs):
     *chip_refs, out_ref = refs
     shape = out_ref.shape[2:]
-    blocks = [own_ref.at[0, 0], sibling_ref.at[0]] + [ref.at[t] for ref in chip_refs for t in range(2)]
+    chips = dict(zip(order, chip_refs, strict=True))
+    blocks = [own_ref.at[0], sibling_ref.at[0]] + [chips[chip].at[t] for chip in sorted(order) for t in range(2)]
     depths = [block[6] for block in blocks]
     for view in range(2):
         rate = jnp.broadcast_to(rate_ref[view : view + 1, :], shape)
@@ -269,11 +309,11 @@
         out_ref[view, 3] = opacity(sum(depths) * rate)
 
 
-def composite_slots(table, rate, own, sibling, chips):
+def composite_slots(table, rate, own, sibling, order, chips):
     blocks = [own, sibling, *chips]
-    _, rows, columns = own.shape[2:]
+    _, rows, columns = own.shape[1:]
     (image,) = call(
-        slots_kernel, [((2, 4, rows, columns), F32)], "VV" + "V" * len(blocks), [], 1 << 10, 1 << 10,
+        functools.partial(slots_kernel, order), [((2, 4, rows, columns), F32)], "VV" + "V" * len(blocks), [], 1 << 10, 1 << 10,
         table, rate, *blocks,
     )
     return image
@@ -360,20 +400,29 @@
         half = samples // 2
         runs = [[[(start, start, half, half * side)] for side in range(2)] for start in (0, half)]
         rows_of = samples, samples
-    for second in range(len(runs)):
-        (packed,) = call(
-            functools.partial(post_kernel, rows, second > 0, runs[second], sliced, assemble[second]),
-            [((2, columns // (2 * LANES), 7, rows, LANES), F32)], "V" * (8 + len(pieces[second])),
-            [pltpu.VMEM((rows_of[second], columns // 2), F32)], 1 << 10, 1 << 10,
-            light, table, near, far, red, green, blue, packed, *pieces[second],
-        )
+    def post(kernel, second, out, packed):
+        return call(
+            kernel, [(out, F32)], "V" * (8 + len(pieces[second])), [pltpu.VMEM((rows_of[second], columns // 2), F32)],
+            1 << 10, 1 << 10, light, table, near, far, red, green, blue, packed, *pieces[second],
+        )[0]
+
+    packs = columns // (2 * LANES), 7, rows, LANES
+    whole_runs = len(runs) - 1 if sliced else len(runs)
+    for second in range(whole_runs):
+        kernel = functools.partial(post_kernel, rows, second > 0, runs[second], sliced, assemble[second])
+        packed = post(kernel, second, (2, *packs), packed)
     if sliced:
         def send_to(x, stride):
             return lax.ppermute(x, "depth", [(i, i ^ stride) for i in range(depth_n)])
 
-        got = send_to(packed[1], 1)
-        chips = [send_to(jnp.stack([packed[0, chip], got[chip]]), 2 * chip) for chip in range(1, depth_n // 2)]
-        return composite_slots(table, rate, packed, got, chips)
+        theirs, mine = (
+            post(functools.partial(post_tiles_kernel, rows, which, runs[-1], assemble[-1]), len(runs) - 1, packs, packed)
+            for which in (1, 0)
+        )
+        got = send_to(theirs, 1)
+        order = sorted(range(1, depth_n // 2), key=lambda chip: (chip % 2, chip))
+        sent = {chip: send_to(jnp.stack([mine[chip], got[chip]]), 2 * chip) for chip in order}
+        return composite_slots(table, rate, mine, got, order, [sent[chip] for chip in order])
     parts = packed.transpose(1, 0, 2, 3, 4).reshape(columns // LANES, 7, rows, LANES)
     if own % LANES == 0:
         parts = parts.reshape(depth_n, own // LANES, 7, rows, LANES).transpose(0, 2, 3, 1, 4)

time: 28.8 us -> 28.6 us (level)
    pallas_call x9 -> x10, Pallas kernels: 5.32 us -> 5.39 us  [call(): pl.pallas_call(kernel, out_shape=tuple((pltpu.VMEM(o, t) for o, t in outs...]
  transfers between devices with their start and end apart: 11 -> 11, of which waited for: 8 -> 8; matrix products, arithmetic and copies ran while one was open for 0% -> 0% of each run, Pallas kernels for 11% -> 12%
where the time goes in v8:
time: 28.6 us; the launch traced here: 28.5 us
  starting transfers between devices  13.8 us (48%)
  waiting for transfers between devices  8.46 us (30%)
  Pallas kernels  5.39 us (19%)
  local copies, waits for them, and re-layouts  0.65 us (2%)
    ppermute x7, starting transfers between devices, swap(): return lax.ppermute(x, 'light', [(i, i ^ stride) for i in range(n)])  10.2 us
    pallas_call x10, Pallas kernels, call(): pl.pallas_call(kernel, out_shape=tuple((pltpu.VMEM(o, t) for o, t in outs...  5.39 us
    ppermute x4, waiting for transfers between devices, send_to(): return lax.ppermute(x, 'depth', [(i, i ^ stride) for i in range(depth_n)])  4.68 us
    ppermute x7, waiting for transfers between devices, swap(): return lax.ppermute(x, 'light', [(i, i ^ stride) for i in range(n)])  3.78 us
    ppermute x4, starting transfers between devices, send_to(): return lax.ppermute(x, 'depth', [(i, i ^ stride) for i in range(depth_n)])  3.62 us
    unnamed x5, local copies, waits for them, and re-layouts  0.63 us
  transfers between devices with their start and end apart: 11, of which 8 were waited for; matrix products, arithmetic and copies ran while one was open for 0% of the time, Pallas kernels for 12%

profile of v8, /device:TPU:0, one launch (start us, length us, event | category | flops | bytes accessed | tf_op | source)
XLA Modules:
  0.0 28.5 jit_solution(8192139140755633865)
XLA Ops:
  0.0 1.6 %shard_map.55 = (f32[40,512]{1,0:T(8,128)S(1)}, f32[40,512]{1,0:T(8,128)S(1)}, f32[24,512]{1,0:T(8,128)S(1)}, f32[24,512]{1,0:T(8,128)S(1)}, f32[64,512]{1,0:T(8...) custom-call(bf16[512,1024]{1,0:T(8,128)(2,1)} %bitcast.7, s32[2,8]{1,0:T(2,128)} %rank_hbm.1, f32[3]{0:T(128)} %center_hbm.1), custom_call_target="tpu_custom_call" | custom-call | flops 1048576 | bytes 1048576 | tf_op jit(solution)/shard_map/pallas_call | solution.py:232
  1.6 3.1 %collective-permute-start.1 = (f32[40,512]{1,0:T(8,128)S(1)}, f32[40,512]{1,0:T(8,128)S(1)}, u32[]{:S(2)}, u32[]{:S(2)}) collective-permute-start(f32[40,512]{1,0:T(8,128)S(1)} %get-tuple-element.30), channel_id=1, source_target_pairs={{0,1},{1,0},{2,3},{3,2},{4,5},{5,4},{6,7},{7,6},{8,9},{9,8},{10,11... | collective-permute-start | bytes 245768 | tf_op jit(solution)/shard_map/ppermute | solution.py:323
  4.7 2.6 %collective-permute-start.3 = (f32[24,512]{1,0:T(8,128)S(1)}, f32[24,512]{1,0:T(8,128)S(1)}, u32[]{:S(2)}, u32[]{:S(2)}) collective-permute-start(f32[24,512]{1,0:T(8,128)S(1)} %get-tuple-element.31.same_ref), channel_id=1, source_target_pairs={{0,2},{1,3},{2,0},{3,1},{4,6},{5,7},{6,4},{7,5},{8,10},{9,11},{10,... | collective-permute-start | bytes 147464 | tf_op jit(solution)/shard_map/ppermute | solution.py:323
  7.2 0.0 collective-permute-start.4
  7.2 0.9 %collective-permute-start = (f32[64,512]{1,0:T(8,128)S(1)}, f32[64,512]{1,0:T(8,128)S(1)}, u32[]{:S(2)}, u32[]{:S(2)}) collective-permute-start(f32[64,512]{1,0:T(8,128)S(1)} %get-tuple-element.22), channel_id=1, source_target_pairs={{0,1},{1,0},{2,3},{3,2},{4,5},{5,4},{6,7},{7,6},{8,9},{9,8},{10,11... | collective-permute-start | bytes 393224 | tf_op jit(solution)/shard_map/ppermute | solution.py:323
  8.1 0.0 collective-permute-done.1.given_ref.refs_1_
  8.2 0.0 copy-start
  8.2 0.0 copy-start.1
  8.2 3.6 %collective-permute-start.2 = (f32[40,512]{1,0:T(8,128)S(1)}, f32[40,512]{1,0:T(8,128)S(1)}, u32[]{:S(2)}, u32[]{:S(2)}) collective-permute-start(f32[40,512]{1,0:T(8,128)S(1)} %shard_map.58), channel_id=1, source_target_pairs={{0,2},{1,3},{2,0},{3,1},{4,6},{5,7},{6,4},{7,5},{8,10},{9,11},{10,... | collective-permute-start | bytes 245768 | tf_op jit(solution)/shard_map/ppermute | solution.py:323
  11.7 0.0 collective-permute-start.6
  11.8 0.0 collective-permute-done.3.straight_ref
  11.8 2.1 %collective-permute-done.4.across_ref = f32[24,512]{1,0:T(8,128)S(1)} collective-permute-done((f32[24,512]{1,0:T(8,128)S(1)}, f32[24,512]{1,0:T(8,128)S(1)}, u32[]{:S(2)}, u32[]{:S(2)}) %collective-permute-start.4) | collective-permute-done | bytes 49184 | tf_op jit(solution)/shard_map/ppermute | solution.py:323
  13.8 0.1 collective-permute-start.5
  13.9 0.9 %collective-permute-done.late_ref = f32[64,512]{1,0:T(8,128)S(1)} collective-permute-done((f32[64,512]{1,0:T(8,128)S(1)}, f32[64,512]{1,0:T(8,128)S(1)}, u32[]{:S(2)}, u32[]{:S(2)}) %collective-permute-start) | collective-permute-done | bytes 131104 | tf_op jit(solution)/shard_map/ppermute | solution.py:323
  14.9 0.0 copy-done
  14.9 0.0 copy-done.1
  14.9 2.2 %shard_map.57 = (f32[512,1024]{1,0:T(8,128)S(1)}, f32[512,1024]{1,0:T(8,128)S(1)}, f32[512,1024]{1,0:T(8,128)S(1)}, f32[512,1024]{1,0:T(8,128)S(1)}, f32[512,1024]{1,0:T(8,128)S(1)}, /*index=5*/f32[8,1024]{1,0:T(8,128)S(1)}) custom-call(bf16[512,1024]{1,0:T(8,128)(2,1)S(1)} %get-tuple-element.21.rho_ref, f32[1,1024]{1,0:T(1,128)S(1)} %bitcast.2, ...), custom_call_target="tpu_custom_call" | custom-call | flops 1048576 | bytes 12582912 | tf_op jit(solution)/shard_map/pallas_call | solution.py:232
  17.2 0.0 collective-permute-done.2.refs_0_
  17.2 0.5 %shard_map.59.rest_ref = f32[2,4,7,8,128]{4,3,2,1,0:T(8,128)S(1)} custom-call(f32[1,1024]{1,0:T(1,128)S(1)} %bitcast.3, f32[24,128]{1,0:T(8,128)S(1)} %get-tuple-element.20.table_ref, f32[512,1024]{1,0:T(8,128)S(1)} %get-tuple-element.23.near_ref, f32[512,1024]{1,0:T(8,128)S(1)} %get-tuple-element.24.far_ref, f32[512,1024]{1,0:T(8,128)S(1)} %get-tuple-element.25.red_ref, ...), custom_call_target="tpu_custom_call" | custom-call | flops 1024 | bytes 1024 | tf_op jit(solution)/shard_map/pallas_call | solution.py:232
  17.6 0.4 %collective-permute-done.5.refs_1_ = f32[24,512]{1,0:T(8,128)S(1)} collective-permute-done((f32[24,512]{1,0:T(8,128)S(1)}, f32[24,512]{1,0:T(8,128)S(1)}, u32[]{:S(2)}, u32[]{:S(2)}) %collective-permute-start.5) | collective-permute-done | bytes 49184 | tf_op jit(solution)/shard_map/ppermute | solution.py:323
  18.0 0.5 %shard_map.61.rest_ref = f32[2,4,7,8,128]{4,3,2,1,0:T(8,128)S(1)} custom-call(f32[1,1024]{1,0:T(1,128)S(1)} %bitcast.4, f32[24,128]{1,0:T(8,128)S(1)} %get-tuple-element.20.table_ref, f32[512,1024]{1,0:T(8,128)S(1)} %get-tuple-element.23.near_ref, f32[512,1024]{1,0:T(8,128)S(1)} %get-tuple-element.24.far_ref, f32[512,1024]{1,0:T(8,128)S(1)} %get-tuple-element.25.red_ref, ...), custom_call_target="tpu_custom_call" | custom-call | flops 1024 | bytes 1024 | tf_op jit(solution)/shard_map/pallas_call | solution.py:232
  18.5 0.4 %collective-permute-done.6.refs_0_ = f32[40,512]{1,0:T(8,128)S(1)} collective-permute-done((f32[40,512]{1,0:T(8,128)S(1)}, f32[40,512]{1,0:T(8,128)S(1)}, u32[]{:S(2)}, u32[]{:S(2)}) %collective-permute-start.6) | collective-permute-done | bytes 81952 | tf_op jit(solution)/shard_map/ppermute | solution.py:323
  18.9 0.3 shard_map.63
  19.2 0.1 collective-permute-start.7
  19.2 0.3 shard_map.62.own_ref
  19.5 1.0 %collective-permute-done.7.sibling_ref = f32[4,7,8,128]{3,2,1,0:T(8,128)S(1)} collective-permute-done((f32[4,7,8,128]{3,2,1,0:T(8,128)S(1)}, f32[4,7,8,128]{3,2,1,0:T(8,128)S(1)}, u32[]{:S(2)}, u32[]{:S(2)}) %collective-permute-start.7) | collective-permute-done | bytes 114720 | tf_op jit(solution)/shard_map/ppermute | solution.py:416
  20.6 2.5 %collective-permute-start.10 = (f32[2,7,8,128]{3,2,1,0:T(8,128)S(1)}, f32[2,7,8,128]{3,2,1,0:T(8,128)S(1)}, u32[]{:S(2)}, u32[]{:S(2)}) collective-permute-start(f32[2,7,8,128]{3,2,1,0:T(8,128)S(1)} %pad_maximum_fusion.2), channel_id=1, source_target_pairs={{0,24},{4,28},{8,16},{12,20},{16,8},{20,12},{24,0},{28,4},{1,25},{... | collective-permute-start | bytes 172040 | tf_op jit(solution)/shard_map/ppermute | solution.py:416
  23.1 0.5 %collective-permute-start.9 = (f32[2,7,8,128]{3,2,1,0:T(8,128)S(1)}, f32[2,7,8,128]{3,2,1,0:T(8,128)S(1)}, u32[]{:S(2)}, u32[]{:S(2)}) collective-permute-start(f32[2,7,8,128]{3,2,1,0:T(8,128)S(1)} %pad_maximum_fusion.1), channel_id=1, source_target_pairs={{0,8},{4,12},{8,0},{12,4},{16,24},{20,28},{24,16},{28,20},{1,9},{5... | collective-permute-start | bytes 172040 | tf_op jit(solution)/shard_map/ppermute | solution.py:416
  23.6 0.5 %collective-permute-start.8 = (f32[2,7,8,128]{3,2,1,0:T(8,128)S(1)}, f32[2,7,8,128]{3,2,1,0:T(8,128)S(1)}, u32[]{:S(2)}, u32[]{:S(2)}) collective-permute-start(f32[2,7,8,128]{3,2,1,0:T(8,128)S(1)} %pad_maximum_fusion), channel_id=1, source_target_pairs={{0,16},{4,20},{8,24},{12,28},{16,0},{20,4},{24,8},{28,12},{1,17},{... | collective-permute-start | bytes 172040 | tf_op jit(solution)/shard_map/ppermute | solution.py:416
  24.1 1.9 %collective-permute-done.10.refs_2_ = f32[2,7,8,128]{3,2,1,0:T(8,128)S(1)} collective-permute-done((f32[2,7,8,128]{3,2,1,0:T(8,128)S(1)}, f32[2,7,8,128]{3,2,1,0:T(8,128)S(1)}, u32[]{:S(2)}, u32[]{:S(2)}) %collective-permute-start.10) | collective-permute-done | bytes 57376 | tf_op jit(solution)/shard_map/ppermute | solution.py:416
  26.0 1.2 %collective-permute-done.9.refs_1_ = f32[2,7,8,128]{3,2,1,0:T(8,128)S(1)} collective-permute-done((f32[2,7,8,128]{3,2,1,0:T(8,128)S(1)}, f32[2,7,8,128]{3,2,1,0:T(8,128)S(1)}, u32[]{:S(2)}, u32[]{:S(2)}) %collective-permute-start.9) | collective-permute-done | bytes 57376 | tf_op jit(solution)/shard_map/ppermute | solution.py:416
  27.3 0.5 %collective-permute-done.8.refs_0_ = f32[2,7,8,128]{3,2,1,0:T(8,128)S(1)} collective-permute-done((f32[2,7,8,128]{3,2,1,0:T(8,128)S(1)}, f32[2,7,8,128]{3,2,1,0:T(8,128)S(1)}, u32[]{:S(2)}, u32[]{:S(2)}) %collective-permute-start.8) | collective-permute-done | bytes 57376 | tf_op jit(solution)/shard_map/ppermute | solution.py:416
  27.8 0.1 shard_map.64
  27.9 0.6 %copy.6 = f32[2,4,8,128]{3,2,1,0:T(8,128)} copy(f32[2,4,8,128]{3,2,1,0:T(8,128)S(1)} %shard_map.64) | data formatting | bytes 65536
  (9 shorter events, 0.1 us)
Async XLA Ops:
  1.6 6.6 %collective-permute-start.1 = (f32[40,512]{1,0:T(8,128)S(1)}, f32[40,512]{1,0:T(8,128)S(1)}, u32[]{:S(2)}, u32[]{:S(2)}) collective-permute-start(f32[40,512]{1,0:T(8,128)S(1)} %get-tuple-element.30), channel_id=1, source_target_pairs={{0,1},{1,0},{2,3},{3,2},{4,5},{5,4},{6,7},{7,6},{8,9},{9,8},{10,11... | collective-permute-start | bytes 245768 | tf_op jit(solution)/shard_map/ppermute | solution.py:323
  4.7 7.1 %collective-permute-start.3 = (f32[24,512]{1,0:T(8,128)S(1)}, f32[24,512]{1,0:T(8,128)S(1)}, u32[]{:S(2)}, u32[]{:S(2)}) collective-permute-start(f32[24,512]{1,0:T(8,128)S(1)} %get-tuple-element.31.same_ref), channel_id=1, source_target_pairs={{0,2},{1,3},{2,0},{3,1},{4,6},{5,7},{6,4},{7,5},{8,10},{9,11},{10,... | collective-permute-start | bytes 147464 | tf_op jit(solution)/shard_map/ppermute | solution.py:323
  7.2 6.6 %collective-permute-start.4 = (f32[24,512]{1,0:T(8,128)S(1)}, f32[24,512]{1,0:T(8,128)S(1)}, u32[]{:S(2)}, u32[]{:S(2)}) collective-permute-start(f32[24,512]{1,0:T(8,128)S(1)} %get-tuple-element.32), channel_id=1, source_target_pairs={{0,3},{1,2},{2,1},{3,0},{4,7},{5,6},{6,5},{7,4},{8,11},{9,10},{10,... | collective-permute-start | bytes 147464 | tf_op jit(solution)/shard_map/ppermute | solution.py:323
  7.2 7.6 %collective-permute-start = (f32[64,512]{1,0:T(8,128)S(1)}, f32[64,512]{1,0:T(8,128)S(1)}, u32[]{:S(2)}, u32[]{:S(2)}) collective-permute-start(f32[64,512]{1,0:T(8,128)S(1)} %get-tuple-element.22), channel_id=1, source_target_pairs={{0,1},{1,0},{2,3},{3,2},{4,5},{5,4},{6,7},{7,6},{8,9},{9,8},{10,11... | collective-permute-start | bytes 393224 | tf_op jit(solution)/shard_map/ppermute | solution.py:323
  8.2 6.7 %copy-start = (f32[1024]{0:T(1024)S(1)}, f32[1024]{0:T(1024)}, u32[]{:S(2)}) copy-start(f32[1024]{0:T(1024)} %param.6) | copy-start | bytes 12292
  8.2 6.7 %copy-start.1 = (f32[2,1024]{1,0:T(2,128)S(1)}, f32[2,1024]{1,0:T(2,128)}, u32[]{:S(2)}) copy-start(f32[2,1024]{1,0:T(2,128)} %view_ref.1) | copy-start | bytes 24580
  8.2 9.0 %collective-permute-start.2 = (f32[40,512]{1,0:T(8,128)S(1)}, f32[40,512]{1,0:T(8,128)S(1)}, u32[]{:S(2)}, u32[]{:S(2)}) collective-permute-start(f32[40,512]{1,0:T(8,128)S(1)} %shard_map.58), channel_id=1, source_target_pairs={{0,2},{1,3},{2,0},{3,1},{4,6},{5,7},{6,4},{7,5},{8,10},{9,11},{10,... | collective-permute-start | bytes 245768 | tf_op jit(solution)/shard_map/ppermute | solution.py:323
  11.7 7.1 %collective-permute-start.6 = (f32[40,512]{1,0:T(8,128)S(1)}, f32[40,512]{1,0:T(8,128)S(1)}, u32[]{:S(2)}, u32[]{:S(2)}) collective-permute-start(f32[40,512]{1,0:T(8,128)S(1)} %shard_map.58), channel_id=1, source_target_pairs={{0,3},{1,2},{2,1},{3,0},{4,7},{5,6},{6,5},{7,4},{8,11},{9,10},{10,... | collective-permute-start | bytes 245768 | tf_op jit(solution)/shard_map/ppermute | solution.py:323
  13.8 4.2 %collective-permute-start.5 = (f32[24,512]{1,0:T(8,128)S(1)}, f32[24,512]{1,0:T(8,128)S(1)}, u32[]{:S(2)}, u32[]{:S(2)}) collective-permute-start(f32[24,512]{1,0:T(8,128)S(1)} %get-tuple-element.34), channel_id=1, source_target_pairs={{0,1},{1,0},{2,3},{3,2},{4,5},{5,4},{6,7},{7,6},{8,9},{9,8},{10,11... | collective-permute-start | bytes 147464 | tf_op jit(solution)/shard_map/ppermute | solution.py:323
  19.2 1.4 %collective-permute-start.7 = (f32[4,7,8,128]{3,2,1,0:T(8,128)S(1)}, f32[4,7,8,128]{3,2,1,0:T(8,128)S(1)}, u32[]{:S(2)}, u32[]{:S(2)}) collective-permute-start(f32[4,7,8,128]{3,2,1,0:T(8,128)S(1)} %shard_map.63), channel_id=1, source_target_pairs={{0,4},{4,0},{8,12},{12,8},{16,20},{20,16},{24,28},{28,24},{1,5},{5... | collective-permute-start | bytes 344072 | tf_op jit(solution)/shard_map/ppermute | solution.py:416
  20.6 5.5 %collective-permute-start.10 = (f32[2,7,8,128]{3,2,1,0:T(8,128)S(1)}, f32[2,7,8,128]{3,2,1,0:T(8,128)S(1)}, u32[]{:S(2)}, u32[]{:S(2)}) collective-permute-start(f32[2,7,8,128]{3,2,1,0:T(8,128)S(1)} %pad_maximum_fusion.2), channel_id=1, source_target_pairs={{0,24},{4,28},{8,16},{12,20},{16,8},{20,12},{24,0},{28,4},{1,25},{... | collective-permute-start | bytes 172040 | tf_op jit(solution)/shard_map/ppermute | solution.py:416
  23.1 4.2 %collective-permute-start.9 = (f32[2,7,8,128]{3,2,1,0:T(8,128)S(1)}, f32[2,7,8,128]{3,2,1,0:T(8,128)S(1)}, u32[]{:S(2)}, u32[]{:S(2)}) collective-permute-start(f32[2,7,8,128]{3,2,1,0:T(8,128)S(1)} %pad_maximum_fusion.1), channel_id=1, source_target_pairs={{0,8},{4,12},{8,0},{12,4},{16,24},{20,28},{24,16},{28,20},{1,9},{5... | collective-permute-start | bytes 172040 | tf_op jit(solution)/shard_map/ppermute | solution.py:416
  23.6 4.2 %collective-permute-start.8 = (f32[2,7,8,128]{3,2,1,0:T(8,128)S(1)}, f32[2,7,8,128]{3,2,1,0:T(8,128)S(1)}, u32[]{:S(2)}, u32[]{:S(2)}) collective-permute-start(f32[2,7,8,128]{3,2,1,0:T(8,128)S(1)} %pad_maximum_fusion), channel_id=1, source_target_pairs={{0,16},{4,20},{8,24},{12,28},{16,0},{20,4},{24,8},{28,12},{1,17},{... | collective-permute-start | bytes 172040 | tf_op jit(solution)/shard_map/ppermute | solution.py:416

commit v9 on v8

--- a/solution.py
+++ b/solution.py
@@ -72,7 +72,7 @@
 
 
 def pre_kernel(
-    samples, rows, width, rho_ref, light_ref, view_ref, table_ref, _,
+    samples, rows, width, rho_ref, light_ref, view_ref, table_ref,
     near_ref, far_ref, red_ref, green_ref, blue_ref, total_ref, above_ref,
 ):
     columns = rho_ref.shape[1]
@@ -381,8 +381,8 @@
         pieces = [below[: samples // 2]], [below[samples // 2 :]]
         assemble = whole_below, whole_below
     near, far, red, green, blue, total = call(
-        functools.partial(pre_kernel, samples, rows, 256), [(whole, F32)] * 5 + [((rows, columns), F32)], "VVVVV",
-        [pltpu.VMEM(whole, F32)], 1 << 20, 12 << 20, rho, light, view_rate, table, pieces[1][-1],
+        functools.partial(pre_kernel, samples, rows, 256), [(whole, F32)] * 5 + [((rows, columns), F32)], "VVVV",
+        [pltpu.VMEM(whole, F32)], 1 << 20, 12 << 20, rho, light, view_rate, table,
     )
     place = lax.axis_index("depth")
     rate = lax.dynamic_slice_in_dim(view_rate, place * own, own, axis=1)

time: 28.6 us -> 28.6 us (level)
  no operation moved by 1% of the time
where the time goes in v9:
time: 28.6 us; the launch traced here: 28.5 us
  starting transfers between devices  13.9 us (49%)
  waiting for transfers between devices  8.45 us (30%)
  Pallas kernels  5.4 us (19%)
  local copies, waits for them, and re-layouts  0.65 us (2%)
    ppermute x7, starting transfers between devices, swap(): return lax.ppermute(x, 'light', [(i, i ^ stride) for i in range(n)])  10.2 us
    pallas_call x10, Pallas kernels, call(): pl.pallas_call(kernel, out_shape=tuple((pltpu.VMEM(o, t) for o, t in outs...  5.4 us
    ppermute x4, waiting for transfers between devices, send_to(): return lax.ppermute(x, 'depth', [(i, i ^ stride) for i in range(depth_n)])  4.68 us
    ppermute x7, waiting for transfers between devices, swap(): return lax.ppermute(x, 'light', [(i, i ^ stride) for i in range(n)])  3.78 us
    ppermute x4, starting transfers between devices, send_to(): return lax.ppermute(x, 'depth', [(i, i ^ stride) for i in range(depth_n)])  3.62 us
    unnamed x5, local copies, waits for them, and re-layouts  0.63 us
  transfers between devices with their start and end apart: 11, of which 8 were waited for; matrix products, arithmetic and copies ran while one was open for 0% of the time, Pallas kernels for 12%

profile of v9, /device:TPU:0, one launch (start us, length us, event | category | flops | bytes accessed | tf_op | source)
XLA Modules:
  0.0 28.5 jit_solution(8356900567285705967)
XLA Ops:
  0.0 1.6 %shard_map.55 = (f32[40,512]{1,0:T(8,128)S(1)}, f32[40,512]{1,0:T(8,128)S(1)}, f32[24,512]{1,0:T(8,128)S(1)}, f32[24,512]{1,0:T(8,128)S(1)}, f32[64,512]{1,0:T(8...) custom-call(bf16[512,1024]{1,0:T(8,128)(2,1)} %bitcast.7, s32[2,8]{1,0:T(2,128)} %rank_hbm.1, f32[3]{0:T(128)} %center_hbm.1), custom_call_target="tpu_custom_call" | custom-call | flops 1048576 | bytes 1048576 | tf_op jit(solution)/shard_map/pallas_call | solution.py:232
  1.6 3.1 %collective-permute-start = (f32[40,512]{1,0:T(8,128)S(1)}, f32[40,512]{1,0:T(8,128)S(1)}, u32[]{:S(2)}, u32[]{:S(2)}) collective-permute-start(f32[40,512]{1,0:T(8,128)S(1)} %get-tuple-element.29), channel_id=1, source_target_pairs={{0,1},{1,0},{2,3},{3,2},{4,5},{5,4},{6,7},{7,6},{8,9},{9,8},{10,11... | collective-permute-start | bytes 245768 | tf_op jit(solution)/shard_map/ppermute | solution.py:323
  4.7 2.6 %collective-permute-start.2 = (f32[24,512]{1,0:T(8,128)S(1)}, f32[24,512]{1,0:T(8,128)S(1)}, u32[]{:S(2)}, u32[]{:S(2)}) collective-permute-start(f32[24,512]{1,0:T(8,128)S(1)} %get-tuple-element.30.same_ref), channel_id=1, source_target_pairs={{0,2},{1,3},{2,0},{3,1},{4,6},{5,7},{6,4},{7,5},{8,10},{9,11},{10,... | collective-permute-start | bytes 147464 | tf_op jit(solution)/shard_map/ppermute | solution.py:323
  7.2 0.0 collective-permute-start.3
  7.2 0.9 %collective-permute-start.5 = (f32[64,512]{1,0:T(8,128)S(1)}, f32[64,512]{1,0:T(8,128)S(1)}, u32[]{:S(2)}, u32[]{:S(2)}) collective-permute-start(f32[64,512]{1,0:T(8,128)S(1)} %get-tuple-element.34), channel_id=1, source_target_pairs={{0,1},{1,0},{2,3},{3,2},{4,5},{5,4},{6,7},{7,6},{8,9},{9,8},{10,11... | collective-permute-start | bytes 393224 | tf_op jit(solution)/shard_map/ppermute | solution.py:323
  8.1 0.0 collective-permute-done.given_ref.refs_1_
  8.2 0.0 copy-start
  8.2 0.0 copy-start.1
  8.2 3.6 %collective-permute-start.1 = (f32[40,512]{1,0:T(8,128)S(1)}, f32[40,512]{1,0:T(8,128)S(1)}, u32[]{:S(2)}, u32[]{:S(2)}) collective-permute-start(f32[40,512]{1,0:T(8,128)S(1)} %shard_map.57), channel_id=1, source_target_pairs={{0,2},{1,3},{2,0},{3,1},{4,6},{5,7},{6,4},{7,5},{8,10},{9,11},{10,... | collective-permute-start | bytes 245768 | tf_op jit(solution)/shard_map/ppermute | solution.py:323
  11.7 0.0 collective-permute-start.6
  11.8 0.0 collective-permute-done.2.straight_ref
  11.8 2.1 %collective-permute-done.3.across_ref = f32[24,512]{1,0:T(8,128)S(1)} collective-permute-done((f32[24,512]{1,0:T(8,128)S(1)}, f32[24,512]{1,0:T(8,128)S(1)}, u32[]{:S(2)}, u32[]{:S(2)}) %collective-permute-start.3) | collective-permute-done | bytes 49184 | tf_op jit(solution)/shard_map/ppermute | solution.py:323
  13.8 0.1 collective-permute-start.4
  13.9 0.0 copy-done
  13.9 0.0 copy-done.1
  14.0 2.2 %shard_map.56 = (f32[512,1024]{1,0:T(8,128)S(1)}, f32[512,1024]{1,0:T(8,128)S(1)}, f32[512,1024]{1,0:T(8,128)S(1)}, f32[512,1024]{1,0:T(8,128)S(1)}, f32[512,1024]{1,0:T(8,128)S(1)}, /*index=5*/f32[8,1024]{1,0:T(8,128)S(1)}) custom-call(bf16[512,1024]{1,0:T(8,128)(2,1)S(1)} %get-tuple-element.21.rho_ref, f32[1,1024]{1,0:T(1,128)S(1)} %bitcast.2, ...), custom_call_target="tpu_custom_call" | custom-call | flops 1048576 | bytes 12582912 | tf_op jit(solution)/shard_map/pallas_call | solution.py:232
  16.2 0.0 collective-permute-done.5.late_ref
  16.2 0.5 %collective-permute-done.1.refs_0_ = f32[40,512]{1,0:T(8,128)S(1)} collective-permute-done((f32[40,512]{1,0:T(8,128)S(1)}, f32[40,512]{1,0:T(8,128)S(1)}, u32[]{:S(2)}, u32[]{:S(2)}) %collective-permute-start.1) | collective-permute-done | bytes 81952 | tf_op jit(solution)/shard_map/ppermute | solution.py:323
  16.8 0.5 %shard_map.58.rest_ref = f32[2,4,7,8,128]{4,3,2,1,0:T(8,128)S(1)} custom-call(f32[1,1024]{1,0:T(1,128)S(1)} %bitcast.3, f32[24,128]{1,0:T(8,128)S(1)} %get-tuple-element.20.table_ref, f32[512,1024]{1,0:T(8,128)S(1)} %get-tuple-element.22.near_ref, f32[512,1024]{1,0:T(8,128)S(1)} %get-tuple-element.23.far_ref, f32[512,1024]{1,0:T(8,128)S(1)} %get-tuple-element.24.red_ref, ...), custom_call_target="tpu_custom_call" | custom-call | flops 1024 | bytes 1024 | tf_op jit(solution)/shard_map/pallas_call | solution.py:232
  17.3 0.8 %collective-permute-done.4.refs_1_ = f32[24,512]{1,0:T(8,128)S(1)} collective-permute-done((f32[24,512]{1,0:T(8,128)S(1)}, f32[24,512]{1,0:T(8,128)S(1)}, u32[]{:S(2)}, u32[]{:S(2)}) %collective-permute-start.4) | collective-permute-done | bytes 49184 | tf_op jit(solution)/shard_map/ppermute | solution.py:323
  18.0 0.5 %shard_map.61.rest_ref = f32[2,4,7,8,128]{4,3,2,1,0:T(8,128)S(1)} custom-call(f32[1,1024]{1,0:T(1,128)S(1)} %bitcast.4, f32[24,128]{1,0:T(8,128)S(1)} %get-tuple-element.20.table_ref, f32[512,1024]{1,0:T(8,128)S(1)} %get-tuple-element.22.near_ref, f32[512,1024]{1,0:T(8,128)S(1)} %get-tuple-element.23.far_ref, f32[512,1024]{1,0:T(8,128)S(1)} %get-tuple-element.24.red_ref, ...), custom_call_target="tpu_custom_call" | custom-call | flops 1024 | bytes 1024 | tf_op jit(solution)/shard_map/pallas_call | solution.py:232
  18.5 0.4 %collective-permute-done.6.refs_0_ = f32[40,512]{1,0:T(8,128)S(1)} collective-permute-done((f32[40,512]{1,0:T(8,128)S(1)}, f32[40,512]{1,0:T(8,128)S(1)}, u32[]{:S(2)}, u32[]{:S(2)}) %collective-permute-start.6) | collective-permute-done | bytes 81952 | tf_op jit(solution)/shard_map/ppermute | solution.py:323
  18.9 0.3 shard_map.63
  19.2 0.1 collective-permute-start.7
  19.2 0.3 shard_map.62.own_ref
  19.5 1.0 %collective-permute-done.7.sibling_ref = f32[4,7,8,128]{3,2,1,0:T(8,128)S(1)} collective-permute-done((f32[4,7,8,128]{3,2,1,0:T(8,128)S(1)}, f32[4,7,8,128]{3,2,1,0:T(8,128)S(1)}, u32[]{:S(2)}, u32[]{:S(2)}) %collective-permute-start.7) | collective-permute-done | bytes 114720 | tf_op jit(solution)/shard_map/ppermute | solution.py:416
  20.6 2.5 %collective-permute-start.10 = (f32[2,7,8,128]{3,2,1,0:T(8,128)S(1)}, f32[2,7,8,128]{3,2,1,0:T(8,128)S(1)}, u32[]{:S(2)}, u32[]{:S(2)}) collective-permute-start(f32[2,7,8,128]{3,2,1,0:T(8,128)S(1)} %pad_maximum_fusion.2), channel_id=1, source_target_pairs={{0,24},{4,28},{8,16},{12,20},{16,8},{20,12},{24,0},{28,4},{1,25},{... | collective-permute-start | bytes 172040 | tf_op jit(solution)/shard_map/ppermute | solution.py:416
  23.1 0.5 %collective-permute-start.9 = (f32[2,7,8,128]{3,2,1,0:T(8,128)S(1)}, f32[2,7,8,128]{3,2,1,0:T(8,128)S(1)}, u32[]{:S(2)}, u32[]{:S(2)}) collective-permute-start(f32[2,7,8,128]{3,2,1,0:T(8,128)S(1)} %pad_maximum_fusion.1), channel_id=1, source_target_pairs={{0,8},{4,12},{8,0},{12,4},{16,24},{20,28},{24,16},{28,20},{1,9},{5... | collective-permute-start | bytes 172040 | tf_op jit(solution)/shard_map/ppermute | solution.py:416
  23.6 0.5 %collective-permute-start.8 = (f32[2,7,8,128]{3,2,1,0:T(8,128)S(1)}, f32[2,7,8,128]{3,2,1,0:T(8,128)S(1)}, u32[]{:S(2)}, u32[]{:S(2)}) collective-permute-start(f32[2,7,8,128]{3,2,1,0:T(8,128)S(1)} %pad_maximum_fusion), channel_id=1, source_target_pairs={{0,16},{4,20},{8,24},{12,28},{16,0},{20,4},{24,8},{28,12},{1,17},{... | collective-permute-start | bytes 172040 | tf_op jit(solution)/shard_map/ppermute | solution.py:416
  24.1 1.9 %collective-permute-done.10.refs_2_ = f32[2,7,8,128]{3,2,1,0:T(8,128)S(1)} collective-permute-done((f32[2,7,8,128]{3,2,1,0:T(8,128)S(1)}, f32[2,7,8,128]{3,2,1,0:T(8,128)S(1)}, u32[]{:S(2)}, u32[]{:S(2)}) %collective-permute-start.10) | collective-permute-done | bytes 57376 | tf_op jit(solution)/shard_map/ppermute | solution.py:416
  26.0 1.2 %collective-permute-done.9.refs_1_ = f32[2,7,8,128]{3,2,1,0:T(8,128)S(1)} collective-permute-done((f32[2,7,8,128]{3,2,1,0:T(8,128)S(1)}, f32[2,7,8,128]{3,2,1,0:T(8,128)S(1)}, u32[]{:S(2)}, u32[]{:S(2)}) %collective-permute-start.9) | collective-permute-done | bytes 57376 | tf_op jit(solution)/shard_map/ppermute | solution.py:416
  27.3 0.5 %collective-permute-done.8.refs_0_ = f32[2,7,8,128]{3,2,1,0:T(8,128)S(1)} collective-permute-done((f32[2,7,8,128]{3,2,1,0:T(8,128)S(1)}, f32[2,7,8,128]{3,2,1,0:T(8,128)S(1)}, u32[]{:S(2)}, u32[]{:S(2)}) %collective-permute-start.8) | collective-permute-done | bytes 57376 | tf_op jit(solution)/shard_map/ppermute | solution.py:416
  27.8 0.1 shard_map.64
  27.9 0.6 %copy.6 = f32[2,4,8,128]{3,2,1,0:T(8,128)} copy(f32[2,4,8,128]{3,2,1,0:T(8,128)S(1)} %shard_map.64) | data formatting | bytes 65536
  (9 shorter events, 0.1 us)
Async XLA Ops:
  1.6 6.6 %collective-permute-start = (f32[40,512]{1,0:T(8,128)S(1)}, f32[40,512]{1,0:T(8,128)S(1)}, u32[]{:S(2)}, u32[]{:S(2)}) collective-permute-start(f32[40,512]{1,0:T(8,128)S(1)} %get-tuple-element.29), channel_id=1, source_target_pairs={{0,1},{1,0},{2,3},{3,2},{4,5},{5,4},{6,7},{7,6},{8,9},{9,8},{10,11... | collective-permute-start | bytes 245768 | tf_op jit(solution)/shard_map/ppermute | solution.py:323
  4.7 7.1 %collective-permute-start.2 = (f32[24,512]{1,0:T(8,128)S(1)}, f32[24,512]{1,0:T(8,128)S(1)}, u32[]{:S(2)}, u32[]{:S(2)}) collective-permute-start(f32[24,512]{1,0:T(8,128)S(1)} %get-tuple-element.30.same_ref), channel_id=1, source_target_pairs={{0,2},{1,3},{2,0},{3,1},{4,6},{5,7},{6,4},{7,5},{8,10},{9,11},{10,... | collective-permute-start | bytes 147464 | tf_op jit(solution)/shard_map/ppermute | solution.py:323
  7.2 6.6 %collective-permute-start.3 = (f32[24,512]{1,0:T(8,128)S(1)}, f32[24,512]{1,0:T(8,128)S(1)}, u32[]{:S(2)}, u32[]{:S(2)}) collective-permute-start(f32[24,512]{1,0:T(8,128)S(1)} %get-tuple-element.31), channel_id=1, source_target_pairs={{0,3},{1,2},{2,1},{3,0},{4,7},{5,6},{6,5},{7,4},{8,11},{9,10},{10,... | collective-permute-start | bytes 147464 | tf_op jit(solution)/shard_map/ppermute | solution.py:323
  7.2 8.9 %collective-permute-start.5 = (f32[64,512]{1,0:T(8,128)S(1)}, f32[64,512]{1,0:T(8,128)S(1)}, u32[]{:S(2)}, u32[]{:S(2)}) collective-permute-start(f32[64,512]{1,0:T(8,128)S(1)} %get-tuple-element.34), channel_id=1, source_target_pairs={{0,1},{1,0},{2,3},{3,2},{4,5},{5,4},{6,7},{7,6},{8,9},{9,8},{10,11... | collective-permute-start | bytes 393224 | tf_op jit(solution)/shard_map/ppermute | solution.py:323
  8.2 5.8 %copy-start = (f32[1024]{0:T(1024)S(1)}, f32[1024]{0:T(1024)}, u32[]{:S(2)}) copy-start(f32[1024]{0:T(1024)} %param.6) | copy-start | bytes 12292
  8.2 5.8 %copy-start.1 = (f32[2,1024]{1,0:T(2,128)S(1)}, f32[2,1024]{1,0:T(2,128)}, u32[]{:S(2)}) copy-start(f32[2,1024]{1,0:T(2,128)} %view_ref.1) | copy-start | bytes 24580
  8.2 8.6 %collective-permute-start.1 = (f32[40,512]{1,0:T(8,128)S(1)}, f32[40,512]{1,0:T(8,128)S(1)}, u32[]{:S(2)}, u32[]{:S(2)}) collective-permute-start(f32[40,512]{1,0:T(8,128)S(1)} %shard_map.57), channel_id=1, source_target_pairs={{0,2},{1,3},{2,0},{3,1},{4,6},{5,7},{6,4},{7,5},{8,10},{9,11},{10,... | collective-permute-start | bytes 245768 | tf_op jit(solution)/shard_map/ppermute | solution.py:323
  11.7 7.1 %collective-permute-start.6 = (f32[40,512]{1,0:T(8,128)S(1)}, f32[40,512]{1,0:T(8,128)S(1)}, u32[]{:S(2)}, u32[]{:S(2)}) collective-permute-start(f32[40,512]{1,0:T(8,128)S(1)} %shard_map.57), channel_id=1, source_target_pairs={{0,3},{1,2},{2,1},{3,0},{4,7},{5,6},{6,5},{7,4},{8,11},{9,10},{10,... | collective-permute-start | bytes 245768 | tf_op jit(solution)/shard_map/ppermute | solution.py:323
  13.8 4.2 %collective-permute-start.4 = (f32[24,512]{1,0:T(8,128)S(1)}, f32[24,512]{1,0:T(8,128)S(1)}, u32[]{:S(2)}, u32[]{:S(2)}) collective-permute-start(f32[24,512]{1,0:T(8,128)S(1)} %get-tuple-element.33), channel_id=1, source_target_pairs={{0,1},{1,0},{2,3},{3,2},{4,5},{5,4},{6,7},{7,6},{8,9},{9,8},{10,11... | collective-permute-start | bytes 147464 | tf_op jit(solution)/shard_map/ppermute | solution.py:323
  19.2 1.4 %collective-permute-start.7 = (f32[4,7,8,128]{3,2,1,0:T(8,128)S(1)}, f32[4,7,8,128]{3,2,1,0:T(8,128)S(1)}, u32[]{:S(2)}, u32[]{:S(2)}) collective-permute-start(f32[4,7,8,128]{3,2,1,0:T(8,128)S(1)} %shard_map.63), channel_id=1, source_target_pairs={{0,4},{4,0},{8,12},{12,8},{16,20},{20,16},{24,28},{28,24},{1,5},{5... | collective-permute-start | bytes 344072 | tf_op jit(solution)/shard_map/ppermute | solution.py:416
  20.6 5.5 %collective-permute-start.10 = (f32[2,7,8,128]{3,2,1,0:T(8,128)S(1)}, f32[2,7,8,128]{3,2,1,0:T(8,128)S(1)}, u32[]{:S(2)}, u32[]{:S(2)}) collective-permute-start(f32[2,7,8,128]{3,2,1,0:T(8,128)S(1)} %pad_maximum_fusion.2), channel_id=1, source_target_pairs={{0,24},{4,28},{8,16},{12,20},{16,8},{20,12},{24,0},{28,4},{1,25},{... | collective-permute-start | bytes 172040 | tf_op jit(solution)/shard_map/ppermute | solution.py:416
  23.1 4.2 %collective-permute-start.9 = (f32[2,7,8,128]{3,2,1,0:T(8,128)S(1)}, f32[2,7,8,128]{3,2,1,0:T(8,128)S(1)}, u32[]{:S(2)}, u32[]{:S(2)}) collective-permute-start(f32[2,7,8,128]{3,2,1,0:T(8,128)S(1)} %pad_maximum_fusion.1), channel_id=1, source_target_pairs={{0,8},{4,12},{8,0},{12,4},{16,24},{20,28},{24,16},{28,20},{1,9},{5... | collective-permute-start | bytes 172040 | tf_op jit(solution)/shard_map/ppermute | solution.py:416
  23.6 4.2 %collective-permute-start.8 = (f32[2,7,8,128]{3,2,1,0:T(8,128)S(1)}, f32[2,7,8,128]{3,2,1,0:T(8,128)S(1)}, u32[]{:S(2)}, u32[]{:S(2)}) collective-permute-start(f32[2,7,8,128]{3,2,1,0:T(8,128)S(1)} %pad_maximum_fusion), channel_id=1, source_target_pairs={{0,16},{4,20},{8,24},{12,28},{16,0},{20,4},{24,8},{28,12},{1,17},{... | collective-permute-start | bytes 172040 | tf_op jit(solution)/shard_map/ppermute | solution.py:416

commit v10 on v9

--- a/solution.py
+++ b/solution.py
@@ -73,38 +73,42 @@
 
 def pre_kernel(
     samples, rows, width, rho_ref, light_ref, view_ref, table_ref,
-    near_ref, far_ref, red_ref, green_ref, blue_ref, total_ref, above_ref,
+    near_ref, far_ref, red_ref, green_ref, blue_ref, total_ref,
 ):
     columns = rho_ref.shape[1]
     narrow = (rows, samples * rows)
     of_row = lax.broadcasted_iota(jnp.int32, narrow, 1) % rows == lax.broadcasted_iota(jnp.int32, narrow, 0)
-    total_ref[...] = jnp.dot(of_row.astype(jnp.bfloat16), rho_ref[...], preferred_element_type=F32)
+    of_row = of_row.astype(jnp.bfloat16)
     block = 256
     square = (block, block)
     i = lax.broadcasted_iota(jnp.int32, square, 0)
     j = lax.broadcasted_iota(jnp.int32, square, 1)
     above = ((i // rows == j // rows) & (j < i)).astype(jnp.bfloat16)
-    for start in range(0, samples * rows, block):
-        above_ref[start : start + block, :] = jnp.dot(
-            above, rho_ref[start : start + block, :], preferred_element_type=F32
-        )
 
     shape = (rows, width)
     tone = [jnp.broadcast_to(jnp.concatenate([table_ref[k : k + 1, :]] * (width // LANES), 1), shape) for k in range(3)]
     for first in range(0, columns, width):
         at = pl.ds(first, width)
+        total_ref[:, at] = jnp.dot(of_row, rho_ref[:, at], preferred_element_type=F32)
+        inner = [
+            jnp.dot(above, rho_ref[start : start + block, at], preferred_element_type=F32)
+            for start in range(0, samples * rows, block)
+        ]
         light = jnp.broadcast_to(light_ref[:, at] * LOG2E, shape)
         r0, r1 = view_ref[0:1, at], view_ref[1:2, at]
         fade = [jnp.broadcast_to(c, shape) for c in (r0, r0 * r0 * 0.5, r0 * r0 * r0 * (1 / 6))]
         grow = [jnp.broadcast_to(c, shape) for c in (r1, r1 * r1 * 0.5, r1 * r1 * r1 * (1 / 6))]
 
-        def pair(step, carry):
-            clear, behind = carry
-            two = rho_ref[pl.ds(pl.multiple_of(step * 2 * rows, 2 * rows), 2 * rows), at].astype(F32)
+        clear = jnp.ones(shape, F32)
+        behind = jnp.exp2(total_ref[:, at] * view_ref[1:2, at] * -LOG2E)
+        for start in range(0, samples * rows, 2 * rows):
+            two = rho_ref[start : start + 2 * rows, at].astype(F32)
             for part in range(2):
                 rho = two[part * rows : (part + 1) * rows]
-                here = pl.ds(pl.multiple_of((step * 2 + part) * rows, rows), rows)
-                tint = jnp.exp2(rho * rho * (-8.0 * LOG2E) - light * above_ref[here, at])
+                first_row = start + part * rows
+                here = slice(first_row, first_row + rows)
+                shade = inner[first_row // block][first_row % block : first_row % block + rows]
+                tint = jnp.exp2(rho * rho * (-8.0 * LOG2E) - light * shade)
                 w0 = clear * (rho * (fade[0] - rho * (fade[1] - rho * fade[2])))
                 clear = clear - w0
                 w1 = behind * (rho * (grow[0] + rho * (grow[1] + rho * grow[2])))
@@ -113,10 +117,6 @@
                 far_ref[here, at] = w1 * tint
                 for k, color_ref in enumerate((red_ref, green_ref, blue_ref)):
                     color_ref[here, at] = jnp.exp2(rho * tone[k])
-            return clear, behind
-
-        start = (jnp.ones(shape, F32), jnp.exp2(total_ref[:, at] * view_ref[1:2, at] * -LOG2E))
-        lax.fori_loop(0, samples // 2, pair, start, unroll=True)
 
 
 def straight_below(refs, below_ref):
@@ -382,7 +382,7 @@
         assemble = whole_below, whole_below
     near, far, red, green, blue, total = call(
         functools.partial(pre_kernel, samples, rows, 256), [(whole, F32)] * 5 + [((rows, columns), F32)], "VVVV",
-        [pltpu.VMEM(whole, F32)], 1 << 20, 12 << 20, rho, light, view_rate, table,
+        [], 1 << 20, 12 << 20, rho, light, view_rate, table,
     )
     place = lax.axis_index("depth")
     rate = lax.dynamic_slice_in_dim(view_rate, place * own, own, axis=1)

time: 28.6 us -> 28.6 us (level)
  no operation moved by 1% of the time
where the time goes in v10:
time: 28.6 us; the launch traced here: 28.5 us
  starting transfers between devices  13.9 us (49%)
  waiting for transfers between devices  8.54 us (30%)
  Pallas kernels  5.31 us (19%)
  local copies, waits for them, and re-layouts  0.65 us (2%)
    ppermute x7, starting transfers between devices, swap(): return lax.ppermute(x, 'light', [(i, i ^ stride) for i in range(n)])  10.2 us
    pallas_call x10, Pallas kernels, call(): pl.pallas_call(kernel, out_shape=tuple((pltpu.VMEM(o, t) for o, t in outs...  5.31 us
    ppermute x4, waiting for transfers between devices, send_to(): return lax.ppermute(x, 'depth', [(i, i ^ stride) for i in range(depth_n)])  4.68 us
    ppermute x7, waiting for transfers between devices, swap(): return lax.ppermute(x, 'light', [(i, i ^ stride) for i in range(n)])  3.86 us
    ppermute x4, starting transfers between devices, send_to(): return lax.ppermute(x, 'depth', [(i, i ^ stride) for i in range(depth_n)])  3.62 us
    unnamed x5, local copies, waits for them, and re-layouts  0.63 us
  transfers between devices with their start and end apart: 11, of which 8 were waited for; matrix products, arithmetic and copies ran while one was open for 0% of the time, Pallas kernels for 12%

profile of v10, /device:TPU:0, one launch (start us, length us, event | category | flops | bytes accessed | tf_op | source)
XLA Modules:
  0.0 28.5 jit_solution(16641038528530573645)
XLA Ops:
  0.0 1.6 %shard_map.55 = (f32[40,512]{1,0:T(8,128)S(1)}, f32[40,512]{1,0:T(8,128)S(1)}, f32[24,512]{1,0:T(8,128)S(1)}, f32[24,512]{1,0:T(8,128)S(1)}, f32[64,512]{1,0:T(8...) custom-call(bf16[512,1024]{1,0:T(8,128)(2,1)} %bitcast.7, s32[2,8]{1,0:T(2,128)} %rank_hbm.1, f32[3]{0:T(128)} %center_hbm.1), custom_call_target="tpu_custom_call" | custom-call | flops 1048576 | bytes 1048576 | tf_op jit(solution)/shard_map/pallas_call | solution.py:232
  1.6 3.1 %collective-permute-start = (f32[40,512]{1,0:T(8,128)S(1)}, f32[40,512]{1,0:T(8,128)S(1)}, u32[]{:S(2)}, u32[]{:S(2)}) collective-permute-start(f32[40,512]{1,0:T(8,128)S(1)} %get-tuple-element.29), channel_id=1, source_target_pairs={{0,1},{1,0},{2,3},{3,2},{4,5},{5,4},{6,7},{7,6},{8,9},{9,8},{10,11... | collective-permute-start | bytes 245768 | tf_op jit(solution)/shard_map/ppermute | solution.py:323
  4.7 2.6 %collective-permute-start.2 = (f32[24,512]{1,0:T(8,128)S(1)}, f32[24,512]{1,0:T(8,128)S(1)}, u32[]{:S(2)}, u32[]{:S(2)}) collective-permute-start(f32[24,512]{1,0:T(8,128)S(1)} %get-tuple-element.30.same_ref), channel_id=1, source_target_pairs={{0,2},{1,3},{2,0},{3,1},{4,6},{5,7},{6,4},{7,5},{8,10},{9,11},{10,... | collective-permute-start | bytes 147464 | tf_op jit(solution)/shard_map/ppermute | solution.py:323
  7.2 0.0 collective-permute-start.3
  7.2 0.9 %collective-permute-start.5 = (f32[64,512]{1,0:T(8,128)S(1)}, f32[64,512]{1,0:T(8,128)S(1)}, u32[]{:S(2)}, u32[]{:S(2)}) collective-permute-start(f32[64,512]{1,0:T(8,128)S(1)} %get-tuple-element.34), channel_id=1, source_target_pairs={{0,1},{1,0},{2,3},{3,2},{4,5},{5,4},{6,7},{7,6},{8,9},{9,8},{10,11... | collective-permute-start | bytes 393224 | tf_op jit(solution)/shard_map/ppermute | solution.py:323
  8.1 0.0 collective-permute-done.given_ref.refs_1_
  8.2 0.0 copy-start
  8.2 0.0 copy-start.1
  8.2 3.6 %collective-permute-start.1 = (f32[40,512]{1,0:T(8,128)S(1)}, f32[40,512]{1,0:T(8,128)S(1)}, u32[]{:S(2)}, u32[]{:S(2)}) collective-permute-start(f32[40,512]{1,0:T(8,128)S(1)} %shard_map.57), channel_id=1, source_target_pairs={{0,2},{1,3},{2,0},{3,1},{4,6},{5,7},{6,4},{7,5},{8,10},{9,11},{10,... | collective-permute-start | bytes 245768 | tf_op jit(solution)/shard_map/ppermute | solution.py:323
  11.7 0.0 collective-permute-start.6
  11.8 0.0 collective-permute-done.2.straight_ref
  11.8 2.1 %collective-permute-done.3.across_ref = f32[24,512]{1,0:T(8,128)S(1)} collective-permute-done((f32[24,512]{1,0:T(8,128)S(1)}, f32[24,512]{1,0:T(8,128)S(1)}, u32[]{:S(2)}, u32[]{:S(2)}) %collective-permute-start.3) | collective-permute-done | bytes 49184 | tf_op jit(solution)/shard_map/ppermute | solution.py:323
  13.8 0.1 collective-permute-start.4
  13.9 0.0 copy-done
  13.9 0.0 copy-done.1
  14.0 2.2 %shard_map.56 = (f32[512,1024]{1,0:T(8,128)S(1)}, f32[512,1024]{1,0:T(8,128)S(1)}, f32[512,1024]{1,0:T(8,128)S(1)}, f32[512,1024]{1,0:T(8,128)S(1)}, f32[512,1024]{1,0:T(8,128)S(1)}, /*index=5*/f32[8,1024]{1,0:T(8,128)S(1)}) custom-call(bf16[512,1024]{1,0:T(8,128)(2,1)S(1)} %get-tuple-element.21.rho_ref, f32[1,1024]{1,0:T(1,128)S(1)} %bitcast.2, ...), custom_call_target="tpu_custom_call" | custom-call | flops 1048576 | bytes 12582912 | tf_op jit(solution)/shard_map/pallas_call | solution.py:232
  16.1 0.0 collective-permute-done.5.late_ref
  16.2 0.6 %collective-permute-done.1.refs_0_ = f32[40,512]{1,0:T(8,128)S(1)} collective-permute-done((f32[40,512]{1,0:T(8,128)S(1)}, f32[40,512]{1,0:T(8,128)S(1)}, u32[]{:S(2)}, u32[]{:S(2)}) %collective-permute-start.1) | collective-permute-done | bytes 81952 | tf_op jit(solution)/shard_map/ppermute | solution.py:323
  16.8 0.5 %shard_map.58.rest_ref = f32[2,4,7,8,128]{4,3,2,1,0:T(8,128)S(1)} custom-call(f32[1,1024]{1,0:T(1,128)S(1)} %bitcast.3, f32[24,128]{1,0:T(8,128)S(1)} %get-tuple-element.20.table_ref, f32[512,1024]{1,0:T(8,128)S(1)} %get-tuple-element.22.near_ref, f32[512,1024]{1,0:T(8,128)S(1)} %get-tuple-element.23.far_ref, f32[512,1024]{1,0:T(8,128)S(1)} %get-tuple-element.24.red_ref, ...), custom_call_target="tpu_custom_call" | custom-call | flops 1024 | bytes 1024 | tf_op jit(solution)/shard_map/pallas_call | solution.py:232
  17.3 0.8 %collective-permute-done.4.refs_1_ = f32[24,512]{1,0:T(8,128)S(1)} collective-permute-done((f32[24,512]{1,0:T(8,128)S(1)}, f32[24,512]{1,0:T(8,128)S(1)}, u32[]{:S(2)}, u32[]{:S(2)}) %collective-permute-start.4) | collective-permute-done | bytes 49184 | tf_op jit(solution)/shard_map/ppermute | solution.py:323
  18.0 0.5 %shard_map.61.rest_ref = f32[2,4,7,8,128]{4,3,2,1,0:T(8,128)S(1)} custom-call(f32[1,1024]{1,0:T(1,128)S(1)} %bitcast.4, f32[24,128]{1,0:T(8,128)S(1)} %get-tuple-element.20.table_ref, f32[512,1024]{1,0:T(8,128)S(1)} %get-tuple-element.22.near_ref, f32[512,1024]{1,0:T(8,128)S(1)} %get-tuple-element.23.far_ref, f32[512,1024]{1,0:T(8,128)S(1)} %get-tuple-element.24.red_ref, ...), custom_call_target="tpu_custom_call" | custom-call | flops 1024 | bytes 1024 | tf_op jit(solution)/shard_map/pallas_call | solution.py:232
  18.5 0.4 %collective-permute-done.6.refs_0_ = f32[40,512]{1,0:T(8,128)S(1)} collective-permute-done((f32[40,512]{1,0:T(8,128)S(1)}, f32[40,512]{1,0:T(8,128)S(1)}, u32[]{:S(2)}, u32[]{:S(2)}) %collective-permute-start.6) | collective-permute-done | bytes 81952 | tf_op jit(solution)/shard_map/ppermute | solution.py:323
  18.9 0.3 shard_map.63
  19.2 0.1 collective-permute-start.7
  19.2 0.3 shard_map.62.own_ref
  19.5 1.0 %collective-permute-done.7.sibling_ref = f32[4,7,8,128]{3,2,1,0:T(8,128)S(1)} collective-permute-done((f32[4,7,8,128]{3,2,1,0:T(8,128)S(1)}, f32[4,7,8,128]{3,2,1,0:T(8,128)S(1)}, u32[]{:S(2)}, u32[]{:S(2)}) %collective-permute-start.7) | collective-permute-done | bytes 114720 | tf_op jit(solution)/shard_map/ppermute | solution.py:416
  20.6 2.5 %collective-permute-start.10 = (f32[2,7,8,128]{3,2,1,0:T(8,128)S(1)}, f32[2,7,8,128]{3,2,1,0:T(8,128)S(1)}, u32[]{:S(2)}, u32[]{:S(2)}) collective-permute-start(f32[2,7,8,128]{3,2,1,0:T(8,128)S(1)} %pad_maximum_fusion.2), channel_id=1, source_target_pairs={{0,24},{4,28},{8,16},{12,20},{16,8},{20,12},{24,0},{28,4},{1,25},{... | collective-permute-start | bytes 172040 | tf_op jit(solution)/shard_map/ppermute | solution.py:416
  23.1 0.5 %collective-permute-start.9 = (f32[2,7,8,128]{3,2,1,0:T(8,128)S(1)}, f32[2,7,8,128]{3,2,1,0:T(8,128)S(1)}, u32[]{:S(2)}, u32[]{:S(2)}) collective-permute-start(f32[2,7,8,128]{3,2,1,0:T(8,128)S(1)} %pad_maximum_fusion.1), channel_id=1, source_target_pairs={{0,8},{4,12},{8,0},{12,4},{16,24},{20,28},{24,16},{28,20},{1,9},{5... | collective-permute-start | bytes 172040 | tf_op jit(solution)/shard_map/ppermute | solution.py:416
  23.6 0.5 %collective-permute-start.8 = (f32[2,7,8,128]{3,2,1,0:T(8,128)S(1)}, f32[2,7,8,128]{3,2,1,0:T(8,128)S(1)}, u32[]{:S(2)}, u32[]{:S(2)}) collective-permute-start(f32[2,7,8,128]{3,2,1,0:T(8,128)S(1)} %pad_maximum_fusion), channel_id=1, source_target_pairs={{0,16},{4,20},{8,24},{12,28},{16,0},{20,4},{24,8},{28,12},{1,17},{... | collective-permute-start | bytes 172040 | tf_op jit(solution)/shard_map/ppermute | solution.py:416
  24.1 1.9 %collective-permute-done.10.refs_2_ = f32[2,7,8,128]{3,2,1,0:T(8,128)S(1)} collective-permute-done((f32[2,7,8,128]{3,2,1,0:T(8,128)S(1)}, f32[2,7,8,128]{3,2,1,0:T(8,128)S(1)}, u32[]{:S(2)}, u32[]{:S(2)}) %collective-permute-start.10) | collective-permute-done | bytes 57376 | tf_op jit(solution)/shard_map/ppermute | solution.py:416
  26.0 1.2 %collective-permute-done.9.refs_1_ = f32[2,7,8,128]{3,2,1,0:T(8,128)S(1)} collective-permute-done((f32[2,7,8,128]{3,2,1,0:T(8,128)S(1)}, f32[2,7,8,128]{3,2,1,0:T(8,128)S(1)}, u32[]{:S(2)}, u32[]{:S(2)}) %collective-permute-start.9) | collective-permute-done | bytes 57376 | tf_op jit(solution)/shard_map/ppermute | solution.py:416
  27.3 0.5 %collective-permute-done.8.refs_0_ = f32[2,7,8,128]{3,2,1,0:T(8,128)S(1)} collective-permute-done((f32[2,7,8,128]{3,2,1,0:T(8,128)S(1)}, f32[2,7,8,128]{3,2,1,0:T(8,128)S(1)}, u32[]{:S(2)}, u32[]{:S(2)}) %collective-permute-start.8) | collective-permute-done | bytes 57376 | tf_op jit(solution)/shard_map/ppermute | solution.py:416
  27.8 0.1 shard_map.64
  27.9 0.6 %copy.6 = f32[2,4,8,128]{3,2,1,0:T(8,128)} copy(f32[2,4,8,128]{3,2,1,0:T(8,128)S(1)} %shard_map.64) | data formatting | bytes 65536
  (9 shorter events, 0.1 us)
Async XLA Ops:
  1.6 6.6 %collective-permute-start = (f32[40,512]{1,0:T(8,128)S(1)}, f32[40,512]{1,0:T(8,128)S(1)}, u32[]{:S(2)}, u32[]{:S(2)}) collective-permute-start(f32[40,512]{1,0:T(8,128)S(1)} %get-tuple-element.29), channel_id=1, source_target_pairs={{0,1},{1,0},{2,3},{3,2},{4,5},{5,4},{6,7},{7,6},{8,9},{9,8},{10,11... | collective-permute-start | bytes 245768 | tf_op jit(solution)/shard_map/ppermute | solution.py:323
  4.7 7.1 %collective-permute-start.2 = (f32[24,512]{1,0:T(8,128)S(1)}, f32[24,512]{1,0:T(8,128)S(1)}, u32[]{:S(2)}, u32[]{:S(2)}) collective-permute-start(f32[24,512]{1,0:T(8,128)S(1)} %get-tuple-element.30.same_ref), channel_id=1, source_target_pairs={{0,2},{1,3},{2,0},{3,1},{4,6},{5,7},{6,4},{7,5},{8,10},{9,11},{10,... | collective-permute-start | bytes 147464 | tf_op jit(solution)/shard_map/ppermute | solution.py:323
  7.2 6.6 %collective-permute-start.3 = (f32[24,512]{1,0:T(8,128)S(1)}, f32[24,512]{1,0:T(8,128)S(1)}, u32[]{:S(2)}, u32[]{:S(2)}) collective-permute-start(f32[24,512]{1,0:T(8,128)S(1)} %get-tuple-element.31), channel_id=1, source_target_pairs={{0,3},{1,2},{2,1},{3,0},{4,7},{5,6},{6,5},{7,4},{8,11},{9,10},{10,... | collective-permute-start | bytes 147464 | tf_op jit(solution)/shard_map/ppermute | solution.py:323
  7.2 8.9 %collective-permute-start.5 = (f32[64,512]{1,0:T(8,128)S(1)}, f32[64,512]{1,0:T(8,128)S(1)}, u32[]{:S(2)}, u32[]{:S(2)}) collective-permute-start(f32[64,512]{1,0:T(8,128)S(1)} %get-tuple-element.34), channel_id=1, source_target_pairs={{0,1},{1,0},{2,3},{3,2},{4,5},{5,4},{6,7},{7,6},{8,9},{9,8},{10,11... | collective-permute-start | bytes 393224 | tf_op jit(solution)/shard_map/ppermute | solution.py:323
  8.2 5.8 %copy-start = (f32[1024]{0:T(1024)S(1)}, f32[1024]{0:T(1024)}, u32[]{:S(2)}) copy-start(f32[1024]{0:T(1024)} %param.6) | copy-start | bytes 12292
  8.2 5.8 %copy-start.1 = (f32[2,1024]{1,0:T(2,128)S(1)}, f32[2,1024]{1,0:T(2,128)}, u32[]{:S(2)}) copy-start(f32[2,1024]{1,0:T(2,128)} %view_ref.1) | copy-start | bytes 24580
  8.2 8.6 %collective-permute-start.1 = (f32[40,512]{1,0:T(8,128)S(1)}, f32[40,512]{1,0:T(8,128)S(1)}, u32[]{:S(2)}, u32[]{:S(2)}) collective-permute-start(f32[40,512]{1,0:T(8,128)S(1)} %shard_map.57), channel_id=1, source_target_pairs={{0,2},{1,3},{2,0},{3,1},{4,6},{5,7},{6,4},{7,5},{8,10},{9,11},{10,... | collective-permute-start | bytes 245768 | tf_op jit(solution)/shard_map/ppermute | solution.py:323
  11.7 7.1 %collective-permute-start.6 = (f32[40,512]{1,0:T(8,128)S(1)}, f32[40,512]{1,0:T(8,128)S(1)}, u32[]{:S(2)}, u32[]{:S(2)}) collective-permute-start(f32[40,512]{1,0:T(8,128)S(1)} %shard_map.57), channel_id=1, source_target_pairs={{0,3},{1,2},{2,1},{3,0},{4,7},{5,6},{6,5},{7,4},{8,11},{9,10},{10,... | collective-permute-start | bytes 245768 | tf_op jit(solution)/shard_map/ppermute | solution.py:323
  13.8 4.2 %collective-permute-start.4 = (f32[24,512]{1,0:T(8,128)S(1)}, f32[24,512]{1,0:T(8,128)S(1)}, u32[]{:S(2)}, u32[]{:S(2)}) collective-permute-start(f32[24,512]{1,0:T(8,128)S(1)} %get-tuple-element.33), channel_id=1, source_target_pairs={{0,1},{1,0},{2,3},{3,2},{4,5},{5,4},{6,7},{7,6},{8,9},{9,8},{10,11... | collective-permute-start | bytes 147464 | tf_op jit(solution)/shard_map/ppermute | solution.py:323
  19.2 1.4 %collective-permute-start.7 = (f32[4,7,8,128]{3,2,1,0:T(8,128)S(1)}, f32[4,7,8,128]{3,2,1,0:T(8,128)S(1)}, u32[]{:S(2)}, u32[]{:S(2)}) collective-permute-start(f32[4,7,8,128]{3,2,1,0:T(8,128)S(1)} %shard_map.63), channel_id=1, source_target_pairs={{0,4},{4,0},{8,12},{12,8},{16,20},{20,16},{24,28},{28,24},{1,5},{5... | collective-permute-start | bytes 344072 | tf_op jit(solution)/shard_map/ppermute | solution.py:416
  20.6 5.5 %collective-permute-start.10 = (f32[2,7,8,128]{3,2,1,0:T(8,128)S(1)}, f32[2,7,8,128]{3,2,1,0:T(8,128)S(1)}, u32[]{:S(2)}, u32[]{:S(2)}) collective-permute-start(f32[2,7,8,128]{3,2,1,0:T(8,128)S(1)} %pad_maximum_fusion.2), channel_id=1, source_target_pairs={{0,24},{4,28},{8,16},{12,20},{16,8},{20,12},{24,0},{28,4},{1,25},{... | collective-permute-start | bytes 172040 | tf_op jit(solution)/shard_map/ppermute | solution.py:416
  23.1 4.2 %collective-permute-start.9 = (f32[2,7,8,128]{3,2,1,0:T(8,128)S(1)}, f32[2,7,8,128]{3,2,1,0:T(8,128)S(1)}, u32[]{:S(2)}, u32[]{:S(2)}) collective-permute-start(f32[2,7,8,128]{3,2,1,0:T(8,128)S(1)} %pad_maximum_fusion.1), channel_id=1, source_target_pairs={{0,8},{4,12},{8,0},{12,4},{16,24},{20,28},{24,16},{28,20},{1,9},{5... | collective-permute-start | bytes 172040 | tf_op jit(solution)/shard_map/ppermute | solution.py:416
  23.6 4.2 %collective-permute-start.8 = (f32[2,7,8,128]{3,2,1,0:T(8,128)S(1)}, f32[2,7,8,128]{3,2,1,0:T(8,128)S(1)}, u32[]{:S(2)}, u32[]{:S(2)}) collective-permute-start(f32[2,7,8,128]{3,2,1,0:T(8,128)S(1)} %pad_maximum_fusion), channel_id=1, source_target_pairs={{0,16},{4,20},{8,24},{12,28},{16,0},{20,4},{24,8},{28,12},{1,17},{... | collective-permute-start | bytes 172040 | tf_op jit(solution)/shard_map/ppermute | solution.py:416

commit v11 on v10

--- a/solution.py
+++ b/solution.py
@@ -43,9 +43,7 @@
                 table_ref[row : row + 1, :] = jnp.full((1, LANES), rank_ref[view, place ^ slot].astype(F32))
     copy.wait()
     samples = sums_ref.shape[0]
-    half = samples // 2
-    for first in (0, half):
-        sums_ref[first : first + half, :] = sample_sums(rho_ref[first * rows : (first + half) * rows, :], half, rows)
+    sums_ref[...] = sample_sums(rho_ref[...], samples, rows)
     odd = lax.axis_index("light") % 2
     for out_ref, pieces in zip(out_refs, places, strict=True):
         row, width = 0, out_ref.shape[1]

time: 28.6 us -> 28.7 us (level)
  no operation moved by 1% of the time
where the time goes in v11:
time: 28.7 us; the launch traced here: 28.5 us
  starting transfers between devices  13.8 us (48%)
  waiting for transfers between devices  8.54 us (30%)
  Pallas kernels  5.32 us (19%)
  local copies, waits for them, and re-layouts  0.65 us (2%)
    ppermute x7, starting transfers between devices, swap(): return lax.ppermute(x, 'light', [(i, i ^ stride) for i in range(n)])  10.2 us
    pallas_call x10, Pallas kernels, call(): pl.pallas_call(kernel, out_shape=tuple((pltpu.VMEM(o, t) for o, t in outs...  5.32 us
    ppermute x4, waiting for transfers between devices, send_to(): return lax.ppermute(x, 'depth', [(i, i ^ stride) for i in range(depth_n)])  4.68 us
    ppermute x7, waiting for transfers between devices, swap(): return lax.ppermute(x, 'light', [(i, i ^ stride) for i in range(n)])  3.86 us
    ppermute x4, starting transfers between devices, send_to(): return lax.ppermute(x, 'depth', [(i, i ^ stride) for i in range(depth_n)])  3.62 us
    unnamed x5, local copies, waits for them, and re-layouts  0.63 us
  transfers between devices with their start and end apart: 11, of which 8 were waited for; matrix products, arithmetic and copies ran while one was open for 0% of the time, Pallas kernels for 12%

profile of v11, /device:TPU:0, one launch (start us, length us, event | category | flops | bytes accessed | tf_op | source)
XLA Modules:
  0.0 28.5 jit_solution(17347870544852192107)
XLA Ops:
  0.0 1.6 %shard_map.55 = (f32[40,512]{1,0:T(8,128)S(1)}, f32[40,512]{1,0:T(8,128)S(1)}, f32[24,512]{1,0:T(8,128)S(1)}, f32[24,512]{1,0:T(8,128)S(1)}, f32[64,512]{1,0:T(8...) custom-call(bf16[512,1024]{1,0:T(8,128)(2,1)} %bitcast.7, s32[2,8]{1,0:T(2,128)} %rank_hbm.1, f32[3]{0:T(128)} %center_hbm.1), custom_call_target="tpu_custom_call" | custom-call | flops 1048576 | bytes 1048576 | tf_op jit(solution)/shard_map/pallas_call | solution.py:230
  1.6 3.1 %collective-permute-start = (f32[40,512]{1,0:T(8,128)S(1)}, f32[40,512]{1,0:T(8,128)S(1)}, u32[]{:S(2)}, u32[]{:S(2)}) collective-permute-start(f32[40,512]{1,0:T(8,128)S(1)} %get-tuple-element.29), channel_id=1, source_target_pairs={{0,1},{1,0},{2,3},{3,2},{4,5},{5,4},{6,7},{7,6},{8,9},{9,8},{10,11... | collective-permute-start | bytes 245768 | tf_op jit(solution)/shard_map/ppermute | solution.py:321
  4.7 2.6 %collective-permute-start.2 = (f32[24,512]{1,0:T(8,128)S(1)}, f32[24,512]{1,0:T(8,128)S(1)}, u32[]{:S(2)}, u32[]{:S(2)}) collective-permute-start(f32[24,512]{1,0:T(8,128)S(1)} %get-tuple-element.30.same_ref), channel_id=1, source_target_pairs={{0,2},{1,3},{2,0},{3,1},{4,6},{5,7},{6,4},{7,5},{8,10},{9,11},{10,... | collective-permute-start | bytes 147464 | tf_op jit(solution)/shard_map/ppermute | solution.py:321
  7.3 0.0 collective-permute-start.3
  7.3 0.9 %collective-permute-start.5 = (f32[64,512]{1,0:T(8,128)S(1)}, f32[64,512]{1,0:T(8,128)S(1)}, u32[]{:S(2)}, u32[]{:S(2)}) collective-permute-start(f32[64,512]{1,0:T(8,128)S(1)} %get-tuple-element.34), channel_id=1, source_target_pairs={{0,1},{1,0},{2,3},{3,2},{4,5},{5,4},{6,7},{7,6},{8,9},{9,8},{10,11... | collective-permute-start | bytes 393224 | tf_op jit(solution)/shard_map/ppermute | solution.py:321
  8.2 0.0 collective-permute-done.given_ref.refs_1_
  8.2 0.0 copy-start
  8.2 0.0 copy-start.1
  8.2 3.6 %collective-permute-start.1 = (f32[40,512]{1,0:T(8,128)S(1)}, f32[40,512]{1,0:T(8,128)S(1)}, u32[]{:S(2)}, u32[]{:S(2)}) collective-permute-start(f32[40,512]{1,0:T(8,128)S(1)} %shard_map.57), channel_id=1, source_target_pairs={{0,2},{1,3},{2,0},{3,1},{4,6},{5,7},{6,4},{7,5},{8,10},{9,11},{10,... | collective-permute-start | bytes 245768 | tf_op jit(solution)/shard_map/ppermute | solution.py:321
  11.7 0.0 collective-permute-start.6
  11.8 0.0 collective-permute-done.2.straight_ref
  11.8 2.1 %collective-permute-done.3.across_ref = f32[24,512]{1,0:T(8,128)S(1)} collective-permute-done((f32[24,512]{1,0:T(8,128)S(1)}, f32[24,512]{1,0:T(8,128)S(1)}, u32[]{:S(2)}, u32[]{:S(2)}) %collective-permute-start.3) | collective-permute-done | bytes 49184 | tf_op jit(solution)/shard_map/ppermute | solution.py:321
  13.9 0.1 collective-permute-start.4
  13.9 0.0 copy-done
  14.0 0.0 copy-done.1
  14.0 2.2 %shard_map.56 = (f32[512,1024]{1,0:T(8,128)S(1)}, f32[512,1024]{1,0:T(8,128)S(1)}, f32[512,1024]{1,0:T(8,128)S(1)}, f32[512,1024]{1,0:T(8,128)S(1)}, f32[512,1024]{1,0:T(8,128)S(1)}, /*index=5*/f32[8,1024]{1,0:T(8,128)S(1)}) custom-call(bf16[512,1024]{1,0:T(8,128)(2,1)S(1)} %get-tuple-element.21.rho_ref, f32[1,1024]{1,0:T(1,128)S(1)} %bitcast.2, ...), custom_call_target="tpu_custom_call" | custom-call | flops 1048576 | bytes 12582912 | tf_op jit(solution)/shard_map/pallas_call | solution.py:230
  16.1 0.0 collective-permute-done.5.late_ref
  16.2 0.6 %collective-permute-done.1.refs_0_ = f32[40,512]{1,0:T(8,128)S(1)} collective-permute-done((f32[40,512]{1,0:T(8,128)S(1)}, f32[40,512]{1,0:T(8,128)S(1)}, u32[]{:S(2)}, u32[]{:S(2)}) %collective-permute-start.1) | collective-permute-done | bytes 81952 | tf_op jit(solution)/shard_map/ppermute | solution.py:321
  16.8 0.5 %shard_map.58.rest_ref = f32[2,4,7,8,128]{4,3,2,1,0:T(8,128)S(1)} custom-call(f32[1,1024]{1,0:T(1,128)S(1)} %bitcast.3, f32[24,128]{1,0:T(8,128)S(1)} %get-tuple-element.20.table_ref, f32[512,1024]{1,0:T(8,128)S(1)} %get-tuple-element.22.near_ref, f32[512,1024]{1,0:T(8,128)S(1)} %get-tuple-element.23.far_ref, f32[512,1024]{1,0:T(8,128)S(1)} %get-tuple-element.24.red_ref, ...), custom_call_target="tpu_custom_call" | custom-call | flops 1024 | bytes 1024 | tf_op jit(solution)/shard_map/pallas_call | solution.py:230
  17.3 0.8 %collective-permute-done.4.refs_1_ = f32[24,512]{1,0:T(8,128)S(1)} collective-permute-done((f32[24,512]{1,0:T(8,128)S(1)}, f32[24,512]{1,0:T(8,128)S(1)}, u32[]{:S(2)}, u32[]{:S(2)}) %collective-permute-start.4) | collective-permute-done | bytes 49184 | tf_op jit(solution)/shard_map/ppermute | solution.py:321
  18.0 0.5 %shard_map.61.rest_ref = f32[2,4,7,8,128]{4,3,2,1,0:T(8,128)S(1)} custom-call(f32[1,1024]{1,0:T(1,128)S(1)} %bitcast.4, f32[24,128]{1,0:T(8,128)S(1)} %get-tuple-element.20.table_ref, f32[512,1024]{1,0:T(8,128)S(1)} %get-tuple-element.22.near_ref, f32[512,1024]{1,0:T(8,128)S(1)} %get-tuple-element.23.far_ref, f32[512,1024]{1,0:T(8,128)S(1)} %get-tuple-element.24.red_ref, ...), custom_call_target="tpu_custom_call" | custom-call | flops 1024 | bytes 1024 | tf_op jit(solution)/shard_map/pallas_call | solution.py:230
  18.5 0.4 %collective-permute-done.6.refs_0_ = f32[40,512]{1,0:T(8,128)S(1)} collective-permute-done((f32[40,512]{1,0:T(8,128)S(1)}, f32[40,512]{1,0:T(8,128)S(1)}, u32[]{:S(2)}, u32[]{:S(2)}) %collective-permute-start.6) | collective-permute-done | bytes 81952 | tf_op jit(solution)/shard_map/ppermute | solution.py:321
  18.9 0.3 shard_map.63
  19.2 0.1 collective-permute-start.7
  19.2 0.3 shard_map.62.own_ref
  19.5 1.0 %collective-permute-done.7.sibling_ref = f32[4,7,8,128]{3,2,1,0:T(8,128)S(1)} collective-permute-done((f32[4,7,8,128]{3,2,1,0:T(8,128)S(1)}, f32[4,7,8,128]{3,2,1,0:T(8,128)S(1)}, u32[]{:S(2)}, u32[]{:S(2)}) %collective-permute-start.7) | collective-permute-done | bytes 114720 | tf_op jit(solution)/shard_map/ppermute | solution.py:414
  20.6 2.5 %collective-permute-start.10 = (f32[2,7,8,128]{3,2,1,0:T(8,128)S(1)}, f32[2,7,8,128]{3,2,1,0:T(8,128)S(1)}, u32[]{:S(2)}, u32[]{:S(2)}) collective-permute-start(f32[2,7,8,128]{3,2,1,0:T(8,128)S(1)} %pad_maximum_fusion.2), channel_id=1, source_target_pairs={{0,24},{4,28},{8,16},{12,20},{16,8},{20,12},{24,0},{28,4},{1,25},{... | collective-permute-start | bytes 172040 | tf_op jit(solution)/shard_map/ppermute | solution.py:414
  23.1 0.5 %collective-permute-start.9 = (f32[2,7,8,128]{3,2,1,0:T(8,128)S(1)}, f32[2,7,8,128]{3,2,1,0:T(8,128)S(1)}, u32[]{:S(2)}, u32[]{:S(2)}) collective-permute-start(f32[2,7,8,128]{3,2,1,0:T(8,128)S(1)} %pad_maximum_fusion.1), channel_id=1, source_target_pairs={{0,8},{4,12},{8,0},{12,4},{16,24},{20,28},{24,16},{28,20},{1,9},{5... | collective-permute-start | bytes 172040 | tf_op jit(solution)/shard_map/ppermute | solution.py:414
  23.6 0.5 %collective-permute-start.8 = (f32[2,7,8,128]{3,2,1,0:T(8,128)S(1)}, f32[2,7,8,128]{3,2,1,0:T(8,128)S(1)}, u32[]{:S(2)}, u32[]{:S(2)}) collective-permute-start(f32[2,7,8,128]{3,2,1,0:T(8,128)S(1)} %pad_maximum_fusion), channel_id=1, source_target_pairs={{0,16},{4,20},{8,24},{12,28},{16,0},{20,4},{24,8},{28,12},{1,17},{... | collective-permute-start | bytes 172040 | tf_op jit(solution)/shard_map/ppermute | solution.py:414
  24.1 1.9 %collective-permute-done.10.refs_2_ = f32[2,7,8,128]{3,2,1,0:T(8,128)S(1)} collective-permute-done((f32[2,7,8,128]{3,2,1,0:T(8,128)S(1)}, f32[2,7,8,128]{3,2,1,0:T(8,128)S(1)}, u32[]{:S(2)}, u32[]{:S(2)}) %collective-permute-start.10) | collective-permute-done | bytes 57376 | tf_op jit(solution)/shard_map/ppermute | solution.py:414
  26.0 1.2 %collective-permute-done.9.refs_1_ = f32[2,7,8,128]{3,2,1,0:T(8,128)S(1)} collective-permute-done((f32[2,7,8,128]{3,2,1,0:T(8,128)S(1)}, f32[2,7,8,128]{3,2,1,0:T(8,128)S(1)}, u32[]{:S(2)}, u32[]{:S(2)}) %collective-permute-start.9) | collective-permute-done | bytes 57376 | tf_op jit(solution)/shard_map/ppermute | solution.py:414
  27.3 0.5 %collective-permute-done.8.refs_0_ = f32[2,7,8,128]{3,2,1,0:T(8,128)S(1)} collective-permute-done((f32[2,7,8,128]{3,2,1,0:T(8,128)S(1)}, f32[2,7,8,128]{3,2,1,0:T(8,128)S(1)}, u32[]{:S(2)}, u32[]{:S(2)}) %collective-permute-start.8) | collective-permute-done | bytes 57376 | tf_op jit(solution)/shard_map/ppermute | solution.py:414
  27.8 0.1 shard_map.64
  27.9 0.6 %copy.6 = f32[2,4,8,128]{3,2,1,0:T(8,128)} copy(f32[2,4,8,128]{3,2,1,0:T(8,128)S(1)} %shard_map.64) | data formatting | bytes 65536
  (9 shorter events, 0.1 us)
Async XLA Ops:
  1.6 6.6 %collective-permute-start = (f32[40,512]{1,0:T(8,128)S(1)}, f32[40,512]{1,0:T(8,128)S(1)}, u32[]{:S(2)}, u32[]{:S(2)}) collective-permute-start(f32[40,512]{1,0:T(8,128)S(1)} %get-tuple-element.29), channel_id=1, source_target_pairs={{0,1},{1,0},{2,3},{3,2},{4,5},{5,4},{6,7},{7,6},{8,9},{9,8},{10,11... | collective-permute-start | bytes 245768 | tf_op jit(solution)/shard_map/ppermute | solution.py:321
  4.7 7.1 %collective-permute-start.2 = (f32[24,512]{1,0:T(8,128)S(1)}, f32[24,512]{1,0:T(8,128)S(1)}, u32[]{:S(2)}, u32[]{:S(2)}) collective-permute-start(f32[24,512]{1,0:T(8,128)S(1)} %get-tuple-element.30.same_ref), channel_id=1, source_target_pairs={{0,2},{1,3},{2,0},{3,1},{4,6},{5,7},{6,4},{7,5},{8,10},{9,11},{10,... | collective-permute-start | bytes 147464 | tf_op jit(solution)/shard_map/ppermute | solution.py:321
  7.3 6.6 %collective-permute-start.3 = (f32[24,512]{1,0:T(8,128)S(1)}, f32[24,512]{1,0:T(8,128)S(1)}, u32[]{:S(2)}, u32[]{:S(2)}) collective-permute-start(f32[24,512]{1,0:T(8,128)S(1)} %get-tuple-element.31), channel_id=1, source_target_pairs={{0,3},{1,2},{2,1},{3,0},{4,7},{5,6},{6,5},{7,4},{8,11},{9,10},{10,... | collective-permute-start | bytes 147464 | tf_op jit(solution)/shard_map/ppermute | solution.py:321
  7.3 8.9 %collective-permute-start.5 = (f32[64,512]{1,0:T(8,128)S(1)}, f32[64,512]{1,0:T(8,128)S(1)}, u32[]{:S(2)}, u32[]{:S(2)}) collective-permute-start(f32[64,512]{1,0:T(8,128)S(1)} %get-tuple-element.34), channel_id=1, source_target_pairs={{0,1},{1,0},{2,3},{3,2},{4,5},{5,4},{6,7},{7,6},{8,9},{9,8},{10,11... | collective-permute-start | bytes 393224 | tf_op jit(solution)/shard_map/ppermute | solution.py:321
  8.2 5.8 %copy-start = (f32[1024]{0:T(1024)S(1)}, f32[1024]{0:T(1024)}, u32[]{:S(2)}) copy-start(f32[1024]{0:T(1024)} %param.6) | copy-start | bytes 12292
  8.2 5.8 %copy-start.1 = (f32[2,1024]{1,0:T(2,128)S(1)}, f32[2,1024]{1,0:T(2,128)}, u32[]{:S(2)}) copy-start(f32[2,1024]{1,0:T(2,128)} %view_ref.1) | copy-start | bytes 24580
  8.2 8.6 %collective-permute-start.1 = (f32[40,512]{1,0:T(8,128)S(1)}, f32[40,512]{1,0:T(8,128)S(1)}, u32[]{:S(2)}, u32[]{:S(2)}) collective-permute-start(f32[40,512]{1,0:T(8,128)S(1)} %shard_map.57), channel_id=1, source_target_pairs={{0,2},{1,3},{2,0},{3,1},{4,6},{5,7},{6,4},{7,5},{8,10},{9,11},{10,... | collective-permute-start | bytes 245768 | tf_op jit(solution)/shard_map/ppermute | solution.py:321
  11.7 7.1 %collective-permute-start.6 = (f32[40,512]{1,0:T(8,128)S(1)}, f32[40,512]{1,0:T(8,128)S(1)}, u32[]{:S(2)}, u32[]{:S(2)}) collective-permute-start(f32[40,512]{1,0:T(8,128)S(1)} %shard_map.57), channel_id=1, source_target_pairs={{0,3},{1,2},{2,1},{3,0},{4,7},{5,6},{6,5},{7,4},{8,11},{9,10},{10,... | collective-permute-start | bytes 245768 | tf_op jit(solution)/shard_map/ppermute | solution.py:321
  13.9 4.2 %collective-permute-start.4 = (f32[24,512]{1,0:T(8,128)S(1)}, f32[24,512]{1,0:T(8,128)S(1)}, u32[]{:S(2)}, u32[]{:S(2)}) collective-permute-start(f32[24,512]{1,0:T(8,128)S(1)} %get-tuple-element.33), channel_id=1, source_target_pairs={{0,1},{1,0},{2,3},{3,2},{4,5},{5,4},{6,7},{7,6},{8,9},{9,8},{10,11... | collective-permute-start | bytes 147464 | tf_op jit(solution)/shard_map/ppermute | solution.py:321
  19.2 1.4 %collective-permute-start.7 = (f32[4,7,8,128]{3,2,1,0:T(8,128)S(1)}, f32[4,7,8,128]{3,2,1,0:T(8,128)S(1)}, u32[]{:S(2)}, u32[]{:S(2)}) collective-permute-start(f32[4,7,8,128]{3,2,1,0:T(8,128)S(1)} %shard_map.63), channel_id=1, source_target_pairs={{0,4},{4,0},{8,12},{12,8},{16,20},{20,16},{24,28},{28,24},{1,5},{5... | collective-permute-start | bytes 344072 | tf_op jit(solution)/shard_map/ppermute | solution.py:414
  20.6 5.4 %collective-permute-start.10 = (f32[2,7,8,128]{3,2,1,0:T(8,128)S(1)}, f32[2,7,8,128]{3,2,1,0:T(8,128)S(1)}, u32[]{:S(2)}, u32[]{:S(2)}) collective-permute-start(f32[2,7,8,128]{3,2,1,0:T(8,128)S(1)} %pad_maximum_fusion.2), channel_id=1, source_target_pairs={{0,24},{4,28},{8,16},{12,20},{16,8},{20,12},{24,0},{28,4},{1,25},{... | collective-permute-start | bytes 172040 | tf_op jit(solution)/shard_map/ppermute | solution.py:414
  23.1 4.2 %collective-permute-start.9 = (f32[2,7,8,128]{3,2,1,0:T(8,128)S(1)}, f32[2,7,8,128]{3,2,1,0:T(8,128)S(1)}, u32[]{:S(2)}, u32[]{:S(2)}) collective-permute-start(f32[2,7,8,128]{3,2,1,0:T(8,128)S(1)} %pad_maximum_fusion.1), channel_id=1, source_target_pairs={{0,8},{4,12},{8,0},{12,4},{16,24},{20,28},{24,16},{28,20},{1,9},{5... | collective-permute-start | bytes 172040 | tf_op jit(solution)/shard_map/ppermute | solution.py:414
  23.6 4.2 %collective-permute-start.8 = (f32[2,7,8,128]{3,2,1,0:T(8,128)S(1)}, f32[2,7,8,128]{3,2,1,0:T(8,128)S(1)}, u32[]{:S(2)}, u32[]{:S(2)}) collective-permute-start(f32[2,7,8,128]{3,2,1,0:T(8,128)S(1)} %pad_maximum_fusion), channel_id=1, source_target_pairs={{0,16},{4,20},{8,24},{12,28},{16,0},{20,4},{24,8},{28,12},{1,17},{... | collective-permute-start | bytes 172040 | tf_op jit(solution)/shard_map/ppermute | solution.py:414
